TPU v7x, 128 devices: a whole 4x4x4 slice. The times are simulated.
128 devices in a mesh: grp: 4 (over z_lo, core), fsdp: 32 (over y, x, z_hi).
Axes of the slice: x: 4, y: 4, z: 4 (z_hi: 2, z_lo: 2; z = z_hi * 2 + z_lo), core: 2. Of those that a mesh axis runs over, the one named last changes fastest.
Arguments:
- activations: bfloat16 [32768, 8192], P(('grp', 'fsdp')), may hold values from -6 to 6
- out_grads: bfloat16 [32768, 14336], P(('grp', 'fsdp')), may hold values from -0.03125 to 0.03125
- basis: bfloat16 [8192, 512], P('fsdp'), may hold values from -0.0625 to 0.0625
- first_moment: float32 [14336, 512], P('fsdp'), may hold values from -6 to 6
- second_moment: float32 [14336, 512], P('fsdp'), may hold values from 0.5 to 2
Outputs:
- update: bfloat16 [8192, 14336], P('fsdp')
- new_first: float32 [14336, 512], P('fsdp')
- new_second: float32 [14336, 512], P('fsdp')
All inputs are finite; a program needn't handle non-finite values.
Results may differ from a plain program's by a relative error of at most 0.011.
Values may be sent and summed in bfloat16 or wider, within the bound.
No kernel may reach another device: no remote copies, remote signals or barrier semaphores. Data moves between devices by JAX's collectives and lax.ppermute only.
A program may use at most 128 MiB of HBM per device.

v0:
```python
import jax
import jax.numpy as jnp
from jax import lax
from jax.sharding import PartitionSpec as P

STEP = 10


beta_one = 0.9
beta_two = 0.99
eps = 1e-08
galore_scale = 4.0


def local(activations, out_grads, basis, first_moment, second_moment):
    projected = jnp.dot(
        activations,
        lax.all_gather(basis, "fsdp", axis=0, tiled=True),
        preferred_element_type=jnp.float32,
    ).astype(jnp.bfloat16)
    own_rows = lax.psum_scatter(
        lax.dot_general(
            out_grads, projected, (((0,), (0,)), ((), ())), preferred_element_type=jnp.float32
        ).astype(jnp.bfloat16),
        "fsdp",
        scatter_dimension=0,
        tiled=True,
    )
    reduced = lax.psum(own_rows, "grp").astype(jnp.float32)
    new_first = beta_one * first_moment + (1.0 - beta_one) * reduced
    new_second = beta_two * second_moment + (1.0 - beta_two) * reduced * reduced
    corrected = new_first / (1.0 - beta_one**STEP)
    normalized = (corrected / (jnp.sqrt(new_second / (1.0 - beta_two**STEP)) + eps)).astype(
        jnp.bfloat16
    )
    expanded = lax.dot_general(
        basis,
        lax.all_gather(normalized, "fsdp", axis=0, tiled=True),
        (((1,), (1,)), ((), ())),
        preferred_element_type=jnp.float32,
    )
    update = (-galore_scale * expanded).astype(jnp.bfloat16)
    return (update, new_first, new_second)


def solution(mesh):
    in_specs = (
        P(("grp", "fsdp"), None),
        P(("grp", "fsdp"), None),
        P("fsdp", None),
        P("fsdp", None),
        P("fsdp", None),
    )
    out_specs = (P("fsdp", None), P("fsdp", None), P("fsdp", None))
    return jax.shard_map(local, mesh=mesh, in_specs=in_specs, out_specs=out_specs, check_vma=False)
```

profile of v0, /device:TPU:1, one launch (start us, length us, event | category | flops | bytes accessed | tf_op | source)
XLA Modules:
  0.0 692.6 jit_solution(13242907115630180801)
XLA Ops:
  7.2 0.0 all-gather.3.cloned.1.call-start
  7.2 0.7 all-gather.3.cloned.1.call-update
  7.9 0.0 reduce-scatter.4.cloned.1.call-start
  7.9 111.0 %all-gather.3.cloned.1.call-done = bf16[8192,512]{1,0:T(8,128)(2,1)} async-done(((bf16[256,512]{1,0:T(8,128)(2,1)}), bf16[8192,512]{1,0:T(8,128)(2,1)}) %all-gather.3.cloned.1.call-update) | async-done | bytes 8388624 | tf_op jit(solution)/shard_map/all_gather | solution.py:18
  119.0 7.0 %convolution_convert_fusion.1 = bf16[256,512]{1,0:T(8,128)(2,1)S(1)} fusion(bf16[256,8192]{1,0:T(8,128)(2,1)} %param.5, bf16[8192,512]{1,0:T(8,128)(2,1)} %all-gather.3.cloned.1.call-done), kind=kOutput, calls=%fused_computation.7 | convolution fusion | flops 2147614720 | bytes 12845056 | tf_op jit(solution)/shard_map/dot_general | solution.py:16
  126.0 10.4 %fusion = bf16[14336,512]{0,1:T(8,128)(2,1)} fusion(bf16[256,512]{1,0:T(8,128)(2,1)S(1)} %convolution_convert_fusion.1, bf16[256,14336]{1,0:T(8,128)(2,1)} %param.6), kind=kOutput, calls=%fused_computation.1 | convolution fusion | flops 3765436416 | bytes 22282240 | tf_op jit(solution)/shard_map/dot_general | solution.py:22
  136.3 19.7 %copy.19 = bf16[14336,512]{1,0:T(8,128)(2,1)} copy(bf16[14336,512]{0,1:T(8,128)(2,1)} %fusion) | data formatting | bytes 29360128
  156.0 0.0 copy-start
  156.0 0.0 copy-start.1
  156.0 0.0 reduce-scatter.4.cloned.1.call-update
  156.1 0.0 copy-start.2
  156.1 0.0 all-reduce.2.cloned.1.call-start
  156.1 315.6 %reduce-scatter.4.cloned.1.call-done = bf16[448,512]{1,0:T(8,128)(2,1)} async-done(((bf16[14336,512]{1,0:T(8,128)(2,1)}), bf16[448,512]{1,0:T(8,128)(2,1)}) %reduce-scatter.4.cloned.1.call-update) | async-done | bytes 458768
  471.7 2.0 copy.20
  473.7 0.0 all-reduce.2.cloned.1.call-update
  473.7 0.0 all-gather.5.cloned.1.call-start
  473.8 0.0 copy-done
  473.8 0.3 copy.13
  474.1 0.0 copy-done.1
  474.1 1.3 copy.14
  475.4 39.8 %all-reduce.2.cloned.1.call-done = bf16[448,512]{0,1:T(8,128)(2,1)} async-done(((bf16[448,512]{0,1:T(8,128)(2,1)}), bf16[448,512]{0,1:T(8,128)(2,1)}) %all-reduce.2.cloned.1.call-update) | async-done | bytes 458768 | tf_op jit(solution)/shard_map/psum | solution.py:29
  515.2 2.9 divide_convert_fusion
  518.1 2.0 copy.15
  520.1 0.0 all-gather.5.cloned.1.call-update
  520.2 1.2 copy.17
  521.4 1.2 copy.18
  522.7 141.2 %all-gather.5.cloned.1.call-done = bf16[14336,512]{1,0:T(8,128)(2,1)} async-done(((bf16[448,512]{1,0:T(8,128)(2,1)}), bf16[14336,512]{1,0:T(8,128)(2,1)}) %all-gather.5.cloned.1.call-update) | async-done | bytes 14680080 | tf_op jit(solution)/shard_map/all_gather | solution.py:38
  663.9 0.0 copy-done.2
  663.9 12.1 %fusion.2 = bf16[256,14336]{0,1:T(8,128)(2,1)} fusion(bf16[14336,512]{1,0:T(8,128)(2,1)} %all-gather.5.cloned.1.call-done, bf16[256,512]{1,0:T(8,128)(2,1)S(1)} %copy-done.2), kind=kOutput, calls=%fused_computation.4 | convolution fusion | flops 3765436416 | bytes 22282240 | tf_op jit(solution)/shard_map/dot_general | solution.py:36
  676.0 10.1 %copy.16 = bf16[256,14336]{1,0:T(8,128)(2,1)} copy(bf16[256,14336]{0,1:T(8,128)(2,1)} %fusion.2) | data formatting | bytes 14680064
Async XLA Ops:
  7.2 111.8 %all-gather.3.cloned.1.call-start = ((), (), s32[]{:S(2)}) async-start(), calls=%async_computation.1 | async-start | bytes 8650752 | tf_op jit(solution)/shard_map/all_gather | solution.py:18
  7.9 463.8 %reduce-scatter.4.cloned.1.call-start = ((), (), s32[]{:S(2)}) async-start(), calls=%async_computation.4 | async-start | bytes 15138816
  156.0 317.8 %copy-start = (f32[448,512]{1,0:T(8,128)S(1)}, f32[448,512]{1,0:T(8,128)}, u32[]{:S(2)}) copy-start(f32[448,512]{1,0:T(8,128)} %param.8) | copy-start | bytes 2752516
  156.0 318.1 %copy-start.1 = (f32[448,512]{1,0:T(8,128)S(1)}, f32[448,512]{1,0:T(8,128)}, u32[]{:S(2)}) copy-start(f32[448,512]{1,0:T(8,128)} %param.9) | copy-start | bytes 2752516
  156.1 507.8 %copy-start.2 = (bf16[256,512]{1,0:T(8,128)(2,1)S(1)}, bf16[256,512]{1,0:T(8,128)(2,1)}, u32[]{:S(2)}) copy-start(bf16[256,512]{1,0:T(8,128)(2,1)} %param.7) | copy-start | bytes 786436
  156.1 359.2 %all-reduce.2.cloned.1.call-start = ((), (), s32[]{:S(2)}) async-start(), calls=%async_computation.2 | async-start | bytes 1048576 | tf_op jit(solution)/shard_map/psum | solution.py:29
  473.7 190.1 %all-gather.5.cloned.1.call-start = ((), (), s32[]{:S(2)}) async-start(), calls=%async_computation.3 | async-start | bytes 15138816 | tf_op jit(solution)/shard_map/all_gather | solution.py:38
Sparse Core Ops, SparseCore 0:
  11.0 107.9 all-gather.2
  156.2 315.4 reduce-scatter.3
  474.8 40.4 all-reduce.1
  520.3 143.5 all-gather.4
where the time goes:
time: 694 us; the launch traced here: 693 us
  waiting for transfers between devices  608 us (88%)
  local copies, waits for them, and re-layouts  38 us (5%)
  matrix products  29.4 us (4%)
  between operations  13.8 us (2%)
    unnamed x5, waiting for transfers between devices  316 us
    all_gather x1, waiting for transfers between devices, local(): lax.all_gather(normalized, 'fsdp', axis=0, tiled=True)  141 us
    all_gather x1, waiting for transfers between devices, local(): lax.all_gather(basis, 'fsdp', axis=0, tiled=True)  111 us
    psum x1, waiting for transfers between devices, local(): reduced = lax.psum(own_rows, 'grp').astype(jnp.float32)  39.8 us
    unnamed x13, local copies, waits for them, and re-layouts  36 us
  transfers between devices with their start and end apart: 4, of which 4 were waited for; matrix products, arithmetic and copies ran while one was open for 1% of the time, Pallas kernels for 0%

commit v1 on v0

v1 whole, which is shorter than its diff:
```python
import functools

import jax
import jax.numpy as jnp
from jax import lax
from jax.experimental import pallas as pl
from jax.experimental.pallas import tpu as pltpu
from jax.sharding import PartitionSpec as P

STEP = 10


beta_one = 0.9
beta_two = 0.99
eps = 1e-08
galore_scale = 4.0

AXES = ("grp", "fsdp")
BF = jnp.bfloat16
F32 = jnp.float32
ORDERS = (("y", "z", "x"), ("z", "x", "y"), ("x", "y", "z"))


def flat(co):
    z, c = co["z"] % 4, co["c"] % 2
    return ((z % 2) * 2 + c) * 32 + ((co["y"] % 4) * 4 + co["x"] % 4) * 2 + z // 2


def permute(arr, move):
    pairs = []
    for c in range(2):
        for y in range(4):
            for x in range(4):
                for z in range(4):
                    co = {"c": c, "y": y, "x": x, "z": z}
                    pairs.append((flat(co), flat(move(dict(co)))))
    return lax.ppermute(arr, AXES, pairs)


def shift(arr, axis, k):
    def move(co):
        co[axis] += k * (1 - 2 * co["c"])
        return co

    return permute(arr, move)


def swap_core(arr):
    def move(co):
        co["c"] = 1 - co["c"]
        return co

    return permute(arr, move)


def swap_low(arr):
    def move(co):
        co["z"] = co["z"] ^ 1
        return co

    return permute(arr, move)


def place(blocks, where, shape, at):
    n = len(blocks)

    def kernel(where_ref, *refs):
        out, sem = refs[n], refs[n + 1]
        copies = [
            pltpu.make_async_copy(refs[i], out.at[at(i, where_ref)], sem.at[i]) for i in range(n)
        ]
        for copy in copies:
            copy.start()
        for copy in copies:
            copy.wait()

    return pl.pallas_call(
        kernel,
        out_shape=jax.ShapeDtypeStruct(shape, blocks[0].dtype),
        grid_spec=pltpu.PrefetchScalarGridSpec(
            num_scalar_prefetch=1,
            grid=(1,),
            in_specs=[pl.BlockSpec(memory_space=pl.ANY)] * n,
            out_specs=pl.BlockSpec(memory_space=pl.ANY),
            scratch_shapes=[pltpu.SemaphoreType.DMA((n,))],
        ),
        cost_estimate=pl.CostEstimate(
            flops=0, bytes_accessed=2 * sum(b.size * b.dtype.itemsize for b in blocks), transcendentals=0
        ),
    )(where, *blocks)


def axis_places(pos, sign):
    return jnp.stack([lax.rem(pos - k * sign + 8, 4) for k in range(4)]).astype(jnp.int32)


def gather_part(piece, order, pos, sign):
    first, second, last = order
    cols = piece.shape[1]
    rows = piece.shape[0]
    blocks = [piece] + [shift(piece, first, k) for k in (1, 2, 3)]
    ring = place(
        blocks, axis_places(pos[first], sign), (4, rows, cols), lambda i, w: w[i]
    )
    blocks = [ring] + [shift(ring, second, k) for k in (1, 2, 3)]
    natural = "yxz"
    firstmost = natural.index(second) < natural.index(first)
    if firstmost:
        at = lambda i, w: w[i]
    else:
        at = lambda i, w: (slice(None), w[i])
    plane = place(blocks, axis_places(pos[second], sign), (4, 4, rows, cols), at)
    groups = [plane]
    for _ in range(3):
        groups.append(shift(groups[-1], last, 1))
    return groups


def index_of(axis, q):
    return {"y": (q,), "x": (slice(None), q), "z": (slice(None), slice(None), q)}[axis]


def split_rows(rows):
    tiles = rows // 16
    a = -(-tiles // 3)
    b = -(-(tiles - a) // 2)
    return (a * 16, b * 16, rows - (a + b) * 16)


def proj_kernel(a0, a1, b, o0, o1, s0, s1):
    step = pl.program_id(0)

    @pl.when(step == 0)
    def _():
        s0[...] = jnp.zeros_like(s0)
        s1[...] = jnp.zeros_like(s1)

    s0[...] += jnp.dot(a0[...], b[...], preferred_element_type=F32)
    s1[...] += jnp.dot(a1[...], b[...], preferred_element_type=F32)

    @pl.when(step == pl.num_programs(0) - 1)
    def _():
        o0[...] = s0[...].astype(BF)
        o1[...] = s1[...].astype(BF)


def project(a0, a1, b):
    tok, depth = a0.shape
    cols = b.shape[1]
    kb = 1024
    return pl.pallas_call(
        proj_kernel,
        out_shape=[jax.ShapeDtypeStruct((tok, cols), BF)] * 2,
        grid=(depth // kb,),
        in_specs=[
            pl.BlockSpec((tok, kb), lambda i: (0, i)),
            pl.BlockSpec((tok, kb), lambda i: (0, i)),
            pl.BlockSpec((kb, cols), lambda i: (i, 0)),
        ],
        out_specs=[pl.BlockSpec((tok, cols), lambda i: (0, 0))] * 2,
        scratch_shapes=[pltpu.VMEM((tok, cols), F32)] * 2,
        cost_estimate=pl.CostEstimate(
            flops=4 * tok * depth * cols, bytes_accessed=4 * tok * depth + 2 * depth * cols, transcendentals=0
        ),
    )(a0, a1, b)


def partial_kernel(g0, g1, p0, p1, o):
    dims = (((0,), (0,)), ((), ()))
    o[...] = (
        lax.dot_general(g0[...], p0[...], dims, preferred_element_type=F32)
        + lax.dot_general(g1[...], p1[...], dims, preferred_element_type=F32)
    ).astype(BF)


def partials(g0, g1, p0, p1):
    tok, ffw = g0.shape
    cols = p0.shape[1]
    nb = 896
    return pl.pallas_call(
        partial_kernel,
        out_shape=jax.ShapeDtypeStruct((ffw, cols), BF),
        grid=(ffw // nb,),
        in_specs=[
            pl.BlockSpec((tok, nb), lambda i: (0, i)),
            pl.BlockSpec((tok, nb), lambda i: (0, i)),
            pl.BlockSpec((tok, cols), lambda i: (0, 0)),
            pl.BlockSpec((tok, cols), lambda i: (0, 0)),
        ],
        out_specs=pl.BlockSpec((nb, cols), lambda i: (i, 0)),
        cost_estimate=pl.CostEstimate(
            flops=4 * tok * ffw * cols, bytes_accessed=4 * tok * ffw + 2 * ffw * cols, transcendentals=0
        ),
    )(g0, g1, p0, p1)


def update_kernel(b, n, o):
    o[...] = (
        -galore_scale
        * lax.dot_general(b[...], n[...], (((1,), (1,)), ((), ())), preferred_element_type=F32)
    ).astype(BF)


def updates(basis, norm):
    rows, rank = basis.shape
    ffw = norm.shape[0]
    nb = 896
    return pl.pallas_call(
        update_kernel,
        out_shape=jax.ShapeDtypeStruct((rows, ffw), BF),
        grid=(ffw // nb,),
        in_specs=[
            pl.BlockSpec((rows, rank), lambda i: (0, 0)),
            pl.BlockSpec((nb, rank), lambda i: (i, 0)),
        ],
        out_specs=pl.BlockSpec((rows, nb), lambda i: (0, i)),
        cost_estimate=pl.CostEstimate(
            flops=2 * rows * ffw * rank, bytes_accessed=2 * (ffw * rank + rows * ffw), transcendentals=0
        ),
    )(basis, norm)


def local(activations, out_grads, basis, first_moment, second_moment):
    grp, fsdp = lax.axis_index("grp"), lax.axis_index("fsdp")
    core, low = grp % 2, grp // 2
    pos = {"y": fsdp // 8, "x": fsdp // 2 % 4, "z": (fsdp % 2) * 2 + low}
    sign = 1 - 2 * core
    rank = basis.shape[1]
    half = rank // 2
    ffw = out_grads.shape[1]
    shard = ffw // 64

    act_other = swap_core(activations)
    og_other = swap_core(out_grads)

    brows = basis.shape[0] // 2
    mine = lax.dynamic_slice(basis, (low * brows, core * half), (brows, half))
    blocks, codes, offset = [], [], 0
    for part, (size, order) in enumerate(zip(split_rows(brows), ORDERS)):
        groups = gather_part(mine[offset : offset + size], order, pos, sign)
        for k, group in enumerate(groups):
            blocks.append(group)
            codes.append((order[-1], part * 4 + k, offset, size))
        offset += size
    where = jnp.concatenate([axis_places(pos[order[-1]], sign) for order in ORDERS])

    def at_basis(i, w):
        axis, entry, start, size = codes[i]
        index = index_of(axis, w[entry])
        return index + (slice(None),) * (3 - len(index)) + (pl.ds(start, size),)

    full = place(blocks, where, (4, 4, 4, brows, half), at_basis).reshape(64 * brows, half)
    proj_own, proj_other = project(activations, act_other, full)
    partial = partials(out_grads, og_other, proj_own, proj_other).reshape(4, 4, 4, shard, half)

    sums, offset = [], 0
    for size, order in zip(split_rows(shard), ORDERS):
        third, second, first = order
        mine = partial[:, :, :, offset : offset + size]
        offset += size
        dim = "yxz".index(first)
        take = lambda k: lax.dynamic_index_in_dim(mine, lax.rem(pos[first] - k * sign + 8, 4), dim, keepdims=False)
        acc = take(1)
        for k in (2, 3, 4):
            acc = (shift(acc, first, 1).astype(F32) + take(k).astype(F32)).astype(BF)
        left = [a for a in "yxz" if a != first]
        for axis in (second, third):
            dim = left.index(axis)
            left.remove(axis)
            pick = lambda k: lax.dynamic_index_in_dim(
                acc, lax.rem(pos[axis] + k * sign + 8, 4), dim, keepdims=False
            )
            terms = [pick(0)] + [shift(pick(k), axis, k) for k in (1, 2, 3)]
            acc = sum(t.astype(F32) for t in terms).astype(BF)
        sums.append(acc)
    reduced = jnp.concatenate(sums, axis=0)

    def adam(first, second, red):
        new_first = beta_one * first + (1.0 - beta_one) * red
        new_second = beta_two * second + (1.0 - beta_two) * red * red
        return new_first, new_second

    at = (low * shard, core * half)
    new_first, new_second = adam(
        lax.dynamic_slice(first_moment, at, (shard, half)),
        lax.dynamic_slice(second_moment, at, (shard, half)),
        reduced.astype(F32),
    )
    corrected = new_first / (1.0 - beta_one**STEP)
    normalized = (corrected / (jnp.sqrt(new_second / (1.0 - beta_two**STEP)) + eps)).astype(BF)

    blocks, codes, offset = [], [], 0
    for part, (size, order) in enumerate(zip(split_rows(shard), ORDERS)):
        groups = gather_part(normalized[offset : offset + size], order, pos, sign)
        for k, group in enumerate(groups):
            blocks.append(group)
            codes.append((order[-1], part * 4 + k, offset, size, 12))
            blocks.append(swap_core(group))
            codes.append((order[-1], 14 + part * 4 + k, offset, size, 13))
        offset += size
    where = jnp.concatenate(
        [axis_places(pos[order[-1]], sign) for order in ORDERS]
        + [jnp.stack([core * half, half - core * half]).astype(jnp.int32)]
        + [axis_places(pos[order[-1]], -sign) for order in ORDERS]
    )

    def at_norm(i, w):
        axis, entry, start, size, column = codes[i]
        index = index_of(axis, w[entry])
        return index + (slice(None),) * (3 - len(index)) + (
            pl.ds(start, size),
            pl.ds(pl.multiple_of(w[column], half), half),
        )

    norm = place(blocks, where, (4, 4, 4, shard, rank), at_norm).reshape(ffw, rank)
    update = updates(basis, norm)

    other = swap_core(reduced)
    row = jnp.where(core == 0, jnp.concatenate([reduced, other], 1), jnp.concatenate([other, reduced], 1))
    other = swap_low(row)
    rows = jnp.where(low == 0, jnp.concatenate([row, other], 0), jnp.concatenate([other, row], 0))
    out_first, out_second = adam(first_moment, second_moment, rows.astype(F32))
    return (update, out_first, out_second)


def solution(mesh):
    in_specs = (
        P(("grp", "fsdp"), None),
        P(("grp", "fsdp"), None),
        P("fsdp", None),
        P("fsdp", None),
        P("fsdp", None),
    )
    out_specs = (P("fsdp", None), P("fsdp", None), P("fsdp", None))
    return jax.shard_map(local, mesh=mesh, in_specs=in_specs, out_specs=out_specs, check_vma=False)
```

time: 694 us -> 1010 us (1.46); the launches traced: 693 us -> 997 us
  Pallas kernels: 0 us -> 748 us
  waiting for transfers between devices: 608 us -> 58 us
  starting transfers between devices: 0.16 us -> 145 us
  matrix products: 29.4 us -> 0 us
  other arithmetic: 2.92 us -> 21.5 us
  local copies, waits for them, and re-layouts: 38 us -> 22.6 us
  between operations: 13.8 us -> 1.94 us
    pallas_call x0 -> x17, Pallas kernels: none -> 748 us  [the longest x14 706 us: place(): pl.pallas_call(kernel, out_shape=jax.ShapeDtypeStruct(shape, blocks[0].dt...]
    unnamed x5 -> x0, waiting for transfers between devices: 316 us -> none
    all_gather x2 -> x0, waiting for transfers between devices: 252 us -> none  [the longest x1 141 us: local(): lax.all_gather(normalized, 'fsdp', axis=0, tiled=True)]
    ppermute x0 -> x97, starting transfers between devices: none -> 145 us  [permute(): return lax.ppermute(arr, AXES, pairs)]
    ppermute x0 -> x97, waiting for transfers between devices: none -> 58 us  [permute(): return lax.ppermute(arr, AXES, pairs)]
    psum x1 -> x0, waiting for transfers between devices: 39.8 us -> none  [local(): reduced = lax.psum(own_rows, 'grp').astype(jnp.float32)]
    dot_general x3 -> x0, matrix products: 29.4 us -> none  [the longest x1 12.1 us: local(): lax.dot_general(basis, lax.all_gather(normalized, 'fsdp', axis=0, tiled=T...]
    unnamed x13 -> x127, local copies, waits for them, and re-layouts: 36 us -> 8.01 us
  transfers between devices with their start and end apart: 4 -> 97, of which waited for: 4 -> 27; matrix products, arithmetic and copies ran while one was open for 1% -> 3% of each run, Pallas kernels for 0% -> 27%
where the time goes in v1:
time: 1010 us; the launch traced here: 997 us
  Pallas kernels  748 us (74%)
  starting transfers between devices  145 us (14%)
  waiting for transfers between devices  58 us (6%)
  local copies, waits for them, and re-layouts  22.6 us (2%)
  other arithmetic  21.5 us (2%)
    pallas_call x14, Pallas kernels, place(): pl.pallas_call(kernel, out_shape=jax.ShapeDtypeStruct(shape, blocks[0].dt...  706 us
    ppermute x97, starting transfers between devices, permute(): return lax.ppermute(arr, AXES, pairs)  145 us
    ppermute x97, waiting for transfers between devices, permute(): return lax.ppermute(arr, AXES, pairs)  58 us
  transfers between devices with their start and end apart: 97, of which 27 were waited for; matrix products, arithmetic and copies ran while one was open for 3% of the time, Pallas kernels for 27%

profile of v1, /device:TPU:1, one launch (start us, length us, event | category | flops | bytes accessed | tf_op | source)
XLA Modules:
  0.0 996.7 jit_solution(13780039449083995431)
XLA Ops:
  3.0 2.9 collective-permute-start.2
  6.9 3.7 collective-permute-start.11
  10.7 3.0 collective-permute-start.12
  15.0 4.8 shard_map.76.refs_0_
  23.2 4.8 shard_map.78.refs_0_
  28.0 2.5 collective-permute-start.14
  32.2 13.7 %shard_map.77.refs_0_ = bf16[4,4,48,256]{3,2,1,0:T(8,128)(2,1)} custom-call(s32[4]{0:T(128)} %pad_add_fusion.where_ref, bf16[4,48,256]{2,1,0:T(8,128)(2,1)} %shard_map.76.refs_0_, bf16[4,48,256]{2,1,0:T(8,128)(2,1)} %copy-done.35, bf16[4,48,256]{2,1,0:T(8,128)(2,1)} %copy-done.36, bf16[4,48,256]{2,1,0:T(8,128)(2,1)} %copy-done.38), custom_call_target="tpu_custom_call" | custom-call | bytes 786432 | tf_op jit(solution)/shard_map/pallas_call | solution.py:77
  49.4 13.7 %shard_map.79.refs_4_ = bf16[4,4,48,256]{3,2,1,0:T(8,128)(2,1)} custom-call(s32[4]{0:T(128)} %pad_add_fusion.2.where_ref, bf16[4,48,256]{2,1,0:T(8,128)(2,1)} %shard_map.78.refs_0_, bf16[4,48,256]{2,1,0:T(8,128)(2,1)} %copy-done.37, bf16[4,48,256]{2,1,0:T(8,128)(2,1)} %copy-done.39, bf16[4,48,256]{2,1,0:T(8,128)(2,1)} %copy-done.40), custom_call_target="tpu_custom_call" | custom-call | bytes 786432 | tf_op jit(solution)/shard_map/pallas_call | solution.py:77
  68.7 2.9 collective-permute-done.21.refs_2_
  71.6 4.0 collective-permute-done.22.refs_3_
  76.2 3.8 shard_map.80.refs_0_
  80.1 3.3 collective-permute-done.23.refs_1_
  84.0 4.3 collective-permute-done.24.refs_2_
  88.5 4.7 collective-permute-done.25.refs_3_
  93.9 9.7 shard_map.81.refs_8_
  109.3 3.0 collective-permute-start.27
  115.6 3.3 collective-permute-start.28
  119.5 2.7 collective-permute-done.28.refs_11_
  123.8 128.9 %shard_map.82 = bf16[4,4,4,128,256]{4,3,2,1,0:T(8,128)(2,1)} custom-call(s32[12]{0:T(128)} %concatenate.22.where_ref, bf16[4,4,48,256]{3,2,1,0:T(8,128)(2,1)} %shard_map.77.refs_0_, bf16[4,4,48,256]{3,2,1,0:T(8,128)(2,1)} %copy-done.15, bf16[4,4,48,256]{3,2,1,0:T(8,128)(2,1)} %copy-done.17, bf16[4,4,48,256]{3,2,1,0:T(8,128)(2,1)} %copy-done.19, ...), custom_call_target="tpu_custom_call" | custom-call | bytes 8388608 | tf_op jit(solution)/shard_map/pallas_call | solution.py:77
  252.8 8.8 shard_map.83
  261.6 16.1 %shard_map.84 = bf16[14336,256]{1,0:T(8,128)(2,1)} custom-call(bf16[256,14336]{1,0:T(8,128)(2,1)} %g0.1, bf16[256,14336]{1,0:T(8,128)(2,1)} %collective-permute-done.g1, bf16[256,256]{1,0:T(8,128)(2,1)} %get-tuple-element.5.p0, bf16[256,256]{1,0:T(8,128)(2,1)} %get-tuple-element.6.p1), custom_call_target="tpu_custom_call" | custom-call | flops 3758096384 | bytes 22020096 | tf_op jit(solution)/shard_map/pallas_call | solution.py:180
  280.9 3.4 collective-permute-start.47
  284.3 4.5 fusion.37
  292.8 3.0 collective-permute-start.48
  295.8 3.0 constant_dynamic-slice_fusion
  304.9 2.6 collective-permute-start.49
  324.1 2.9 collective-permute-start.31
  332.1 2.7 collective-permute-done.55
  337.5 3.6 collective-permute-start.42
  356.7 2.9 collective-permute-start.83
  364.3 2.5 collective-permute-done.84.refs_3_
  367.4 5.8 shard_map.89.refs_0_
  374.5 3.4 collective-permute-start.71
  378.5 6.8 shard_map.85.refs_0_
  388.6 6.8 shard_map.87.refs_0_
  397.1 17.7 %shard_map.90.refs_16_ = bf16[4,4,64,256]{3,2,1,0:T(8,128)(2,1)} custom-call(s32[4]{0:T(128)} %pad_add_fusion.1.where_ref, bf16[4,64,256]{2,1,0:T(8,128)(2,1)} %shard_map.89.refs_0_, bf16[4,64,256]{2,1,0:T(8,128)(2,1)} %copy-done.30, bf16[4,64,256]{2,1,0:T(8,128)(2,1)} %copy-done.31, bf16[4,64,256]{2,1,0:T(8,128)(2,1)} %copy-done.32), custom_call_target="tpu_custom_call" | custom-call | bytes 1048576 | tf_op jit(solution)/shard_map/pallas_call | solution.py:77
  415.4 33.6 %collective-permute-start.88 = (bf16[4,4,64,256]{3,2,1,0:T(8,128)(2,1)}, bf16[4,4,64,256]{3,2,1,0:T(8,128)(2,1)}, u32[]{:S(2)}, u32[]{:S(2)}) collective-permute-start(bf16[4,4,64,256]{3,2,1,0:T(8,128)(2,1)} %shard_map.90.refs_16_), channel_id=1, source_target_pairs={{0,32},{64,96},{1,33},{65,97},{2,34},{66,98},{3,35},{67,99},{4,36}... | collective-permute-start | bytes 1572872 | tf_op jit(solution)/shard_map/ppermute | solution.py:37
  449.6 21.7 %shard_map.86.refs_0_ = bf16[4,4,80,256]{3,2,1,0:T(8,128)(2,1)} custom-call(s32[4]{0:T(128)} %pad_add_fusion.where_ref, bf16[4,80,256]{2,1,0:T(8,128)(2,1)} %shard_map.85.refs_0_, bf16[4,80,256]{2,1,0:T(8,128)(2,1)} %copy-done.24, bf16[4,80,256]{2,1,0:T(8,128)(2,1)} %copy-done.25, bf16[4,80,256]{2,1,0:T(8,128)(2,1)} %copy-done.26), custom_call_target="tpu_custom_call" | custom-call | bytes 1310720 | tf_op jit(solution)/shard_map/pallas_call | solution.py:77
  471.4 21.7 %shard_map.88.refs_8_ = bf16[4,4,80,256]{3,2,1,0:T(8,128)(2,1)} custom-call(s32[4]{0:T(128)} %pad_add_fusion.2.where_ref, bf16[4,80,256]{2,1,0:T(8,128)(2,1)} %shard_map.87.refs_0_, bf16[4,80,256]{2,1,0:T(8,128)(2,1)} %collective-permute-done.72.refs_1_, bf16[4,80,256]{2,1,0:T(8,128)(2,1)} %collective-permute-done.73.refs_2_, ...), custom_call_target="tpu_custom_call" | custom-call | bytes 1310720 | tf_op jit(solution)/shard_map/pallas_call | solution.py:77
  496.4 4.4 collective-permute-done.96
  500.8 3.9 collective-permute-start.62
  505.9 3.0 collective-permute-start.78
  511.1 3.5 collective-permute-done.65.refs_4_
  516.9 2.9 collective-permute-start.80
  521.9 2.8 collective-permute-done.67.refs_6_
  524.8 4.5 collective-permute-start.68
  533.2 446.7 %shard_map.91 = bf16[4,4,4,224,512]{4,3,2,1,0:T(8,128)(2,1)} custom-call(s32[26]{0:T(128)} %concatenate.21.where_ref, bf16[4,4,80,256]{3,2,1,0:T(8,128)(2,1)} %shard_map.86.refs_0_, bf16[4,4,80,256]{3,2,1,0:T(8,128)(2,1)} %copy-done.7, bf16[4,4,80,256]{3,2,1,0:T(8,128)(2,1)} %copy-done.5, bf16[4,4,80,256]{3,2,1,0:T(8,128)(2,1)} %copy-done.9, ...), custom_call_target="tpu_custom_call" | custom-call | bytes 29360128 | tf_op jit(solution)/shard_map/pallas_call | solution.py:77
  979.9 16.4 %shard_map.92 = bf16[256,14336]{1,0:T(8,128)(2,1)} custom-call(bf16[256,512]{1,0:T(8,128)(2,1)} %b.1, bf16[14336,512]{1,0:T(8,128)(2,1)} %bitcast.128), custom_call_target="tpu_custom_call" | custom-call | flops 3758096384 | bytes 22020096 | tf_op jit(solution)/shard_map/pallas_call | solution.py:208
  (329 shorter events, 113.7 us)
Async XLA Ops:
  0.6 261.0 %collective-permute-start = (bf16[256,14336]{1,0:T(8,128)(2,1)}, bf16[256,14336]{1,0:T(8,128)(2,1)}, u32[]{:S(2)}, u32[]{:S(2)}) collective-permute-start(bf16[256,14336]{1,0:T(8,128)(2,1)} %g0.1), channel_id=1, source_target_pairs={{0,32},{64,96},{1,33},{65,97},{2,34},{66,98},{3,35},{67,99},{4,36}... | collective-permute-start | bytes 22020104 | tf_op jit(solution)/shard_map/ppermute | solution.py:37
  2.1 250.6 %collective-permute-start.1 = (bf16[256,8192]{1,0:T(8,128)(2,1)}, bf16[256,8192]{1,0:T(8,128)(2,1)}, u32[]{:S(2)}, u32[]{:S(2)}) collective-permute-start(bf16[256,8192]{1,0:T(8,128)(2,1)} %a0.1), channel_id=1, source_target_pairs={{0,32},{64,96},{1,33},{65,97},{2,34},{66,98},{3,35},{67,99},{4,36}... | collective-permute-start | bytes 12582920 | tf_op jit(solution)/shard_map/ppermute | solution.py:37
  6.9 12.8 %collective-permute-start.11 = (bf16[48,256]{1,0:T(8,128)(2,1)S(1)}, bf16[48,256]{1,0:T(8,128)(2,1)S(1)}, u32[]{:S(2)}, u32[]{:S(2)}) collective-permute-start(bf16[48,256]{1,0:T(8,128)(2,1)S(1)} %get-tuple-element.24.refs_0_), channel_id=1, source_target_pairs={{0,64},{64,1},{1,65},{65,0},{2,66},{66,3},{3,67},{67,2},{4,68},{68... | collective-permute-start | bytes 73736 | tf_op jit(solution)/shard_map/ppermute | solution.py:37
  10.7 11.1 %collective-permute-start.12 = (bf16[48,256]{1,0:T(8,128)(2,1)S(1)}, bf16[48,256]{1,0:T(8,128)(2,1)S(1)}, u32[]{:S(2)}, u32[]{:S(2)}) collective-permute-start(bf16[48,256]{1,0:T(8,128)(2,1)S(1)} %get-tuple-element.24.refs_0_), channel_id=1, source_target_pairs={{0,1},{64,65},{1,0},{65,64},{2,3},{66,67},{3,2},{67,66},{4,5},{68,... | collective-permute-start | bytes 73736 | tf_op jit(solution)/shard_map/ppermute | solution.py:37
  28.0 18.0 %collective-permute-start.14 = (bf16[4,48,256]{2,1,0:T(8,128)(2,1)}, bf16[4,48,256]{2,1,0:T(8,128)(2,1)S(1)}, u32[]{:S(2)}, u32[]{:S(2)}) collective-permute-start(bf16[4,48,256]{2,1,0:T(8,128)(2,1)} %shard_map.78.refs_0_), channel_id=1, source_target_pairs={{0,2},{64,66},{1,3},{65,67},{2,4},{66,68},{3,5},{67,69},{4,6},{68,... | collective-permute-start | bytes 294920 | tf_op jit(solution)/shard_map/ppermute | solution.py:37
  30.6 17.6 %collective-permute-start.15 = (bf16[4,48,256]{2,1,0:T(8,128)(2,1)}, bf16[4,48,256]{2,1,0:T(8,128)(2,1)S(1)}, u32[]{:S(2)}, u32[]{:S(2)}) collective-permute-start(bf16[4,48,256]{2,1,0:T(8,128)(2,1)} %shard_map.78.refs_0_), channel_id=1, source_target_pairs={{0,4},{64,68},{1,5},{65,69},{2,6},{66,70},{3,7},{67,71},{4,0},{68,... | collective-permute-start | bytes 294920 | tf_op jit(solution)/shard_map/ppermute | solution.py:37
  31.1 17.1 %collective-permute-start.16 = (bf16[4,48,256]{2,1,0:T(8,128)(2,1)}, bf16[4,48,256]{2,1,0:T(8,128)(2,1)S(1)}, u32[]{:S(2)}, u32[]{:S(2)}) collective-permute-start(bf16[4,48,256]{2,1,0:T(8,128)(2,1)} %shard_map.78.refs_0_), channel_id=1, source_target_pairs={{0,6},{64,70},{1,7},{65,71},{2,0},{66,64},{3,1},{67,65},{4,2},{68,... | collective-permute-start | bytes 294920 | tf_op jit(solution)/shard_map/ppermute | solution.py:37
  46.0 59.7 %collective-permute-start.8 = (bf16[4,4,48,256]{3,2,1,0:T(8,128)(2,1)}, bf16[4,4,48,256]{3,2,1,0:T(8,128)(2,1)S(1)}, u32[]{:S(2)}, u32[]{:S(2)}) collective-permute-start(bf16[4,4,48,256]{3,2,1,0:T(8,128)(2,1)} %shard_map.77.refs_0_), channel_id=1, source_target_pairs={{0,2},{64,66},{1,3},{65,67},{2,4},{66,68},{3,5},{67,69},{4,6},{68,... | collective-permute-start | bytes 1179656 | tf_op jit(solution)/shard_map/ppermute | solution.py:37
  63.1 43.1 %collective-permute-start.17 = (bf16[4,4,48,256]{3,2,1,0:T(8,128)(2,1)}, bf16[4,4,48,256]{3,2,1,0:T(8,128)(2,1)S(1)}, u32[]{:S(2)}, u32[]{:S(2)}) collective-permute-start(bf16[4,4,48,256]{3,2,1,0:T(8,128)(2,1)} %shard_map.79.refs_4_), channel_id=1, source_target_pairs={{0,8},{64,72},{1,9},{65,73},{2,10},{66,74},{3,11},{67,75},{4,12},{... | collective-permute-start | bytes 1179656 | tf_op jit(solution)/shard_map/ppermute | solution.py:37
  112.3 9.9 collective-permute-start.10
  280.9 9.8 collective-permute-start.47
  289.7 10.4 %collective-permute-start.38 = (bf16[4,4,80,256]{3,2,1,0:T(8,128)(2,1)}, bf16[4,4,80,256]{3,2,1,0:T(8,128)(2,1)}, u32[]{:S(2)}, u32[]{:S(2)}) collective-permute-start(bf16[4,4,80,256]{3,2,1,0:T(8,128)(2,1)} %dynamic-slice_bitcast_fusion), channel_id=1, source_target_pairs={{0,8},{64,72},{1,9},{65,73},{2,10},{66,74},{3,11},{67,75},{4,12},{... | collective-permute-start | bytes 1966088 | tf_op jit(solution)/shard_map/ppermute | solution.py:37
  292.8 10.0 %collective-permute-start.48 = (bf16[4,4,64,256]{3,2,1,0:T(8,128)(2,1)}, bf16[4,4,64,256]{3,2,1,0:T(8,128)(2,1)}, u32[]{:S(2)}, u32[]{:S(2)}) collective-permute-start(bf16[4,4,64,256]{3,2,1,0:T(8,128)(2,1)} %fusion.8), channel_id=1, source_target_pairs={{0,64},{64,1},{1,65},{65,0},{2,66},{66,3},{3,67},{67,2},{4,68},{68... | collective-permute-start | bytes 1572872 | tf_op jit(solution)/shard_map/ppermute | solution.py:37
  299.6 10.0 %collective-permute-start.29 = (bf16[4,4,80,256]{3,2,0,1:T(8,128)(2,1)}, bf16[4,4,80,256]{3,2,0,1:T(8,128)(2,1)}, u32[]{:S(2)}, u32[]{:S(2)}) collective-permute-start(bf16[4,4,80,256]{3,2,0,1:T(8,128)(2,1)} %bitcast.127), channel_id=1, source_target_pairs={{0,2},{64,66},{1,3},{65,67},{2,4},{66,68},{3,5},{67,69},{4,6},{68,... | collective-permute-start | bytes 1966088 | tf_op jit(solution)/shard_map/ppermute | solution.py:37
  302.2 11.5 %collective-permute-start.39 = (bf16[4,4,80,256]{3,2,1,0:T(8,128)(2,1)}, bf16[4,4,80,256]{3,2,1,0:T(8,128)(2,1)}, u32[]{:S(2)}, u32[]{:S(2)}) collective-permute-start(bf16[4,4,80,256]{3,2,1,0:T(8,128)(2,1)} %fusion.2), channel_id=1, source_target_pairs={{0,8},{64,72},{1,9},{65,73},{2,10},{66,74},{3,11},{67,75},{4,12},{... | collective-permute-start | bytes 1966088 | tf_op jit(solution)/shard_map/ppermute | solution.py:37
  304.9 11.1 %collective-permute-start.49 = (bf16[4,4,64,256]{3,2,1,0:T(8,128)(2,1)}, bf16[4,4,64,256]{3,2,1,0:T(8,128)(2,1)}, u32[]{:S(2)}, u32[]{:S(2)}) collective-permute-start(bf16[4,4,64,256]{3,2,1,0:T(8,128)(2,1)} %fusion.7), channel_id=1, source_target_pairs={{0,64},{64,1},{1,65},{65,0},{2,66},{66,3},{3,67},{67,2},{4,68},{68... | collective-permute-start | bytes 1572872 | tf_op jit(solution)/shard_map/ppermute | solution.py:37
  312.0 10.0 %collective-permute-start.30 = (bf16[4,4,80,256]{3,2,0,1:T(8,128)(2,1)}, bf16[4,4,80,256]{3,2,0,1:T(8,128)(2,1)}, u32[]{:S(2)}, u32[]{:S(2)}) collective-permute-start(bf16[4,4,80,256]{3,2,0,1:T(8,128)(2,1)} %fusion.5), channel_id=1, source_target_pairs={{0,2},{64,66},{1,3},{65,67},{2,4},{66,68},{3,5},{67,69},{4,6},{68,... | collective-permute-start | bytes 1966088 | tf_op jit(solution)/shard_map/ppermute | solution.py:37
  315.8 19.7 %collective-permute-start.40 = (bf16[4,4,80,256]{3,2,1,0:T(8,128)(2,1)}, bf16[4,4,80,256]{3,2,1,0:T(8,128)(2,1)}, u32[]{:S(2)}, u32[]{:S(2)}) collective-permute-start(bf16[4,4,80,256]{3,2,1,0:T(8,128)(2,1)} %fusion.1), channel_id=1, source_target_pairs={{0,8},{64,72},{1,9},{65,73},{2,10},{66,74},{3,11},{67,75},{4,12},{... | collective-permute-start | bytes 1966088 | tf_op jit(solution)/shard_map/ppermute | solution.py:37
  317.5 9.6 collective-permute-start.52
  318.8 10.0 collective-permute-start.50
  324.1 17.1 %collective-permute-start.31 = (bf16[4,4,80,256]{3,2,0,1:T(8,128)(2,1)}, bf16[4,4,80,256]{3,2,0,1:T(8,128)(2,1)}, u32[]{:S(2)}, u32[]{:S(2)}) collective-permute-start(bf16[4,4,80,256]{3,2,0,1:T(8,128)(2,1)} %fusion.4), channel_id=1, source_target_pairs={{0,2},{64,66},{1,3},{65,67},{2,4},{66,68},{3,5},{67,69},{4,6},{68,... | collective-permute-start | bytes 1966088 | tf_op jit(solution)/shard_map/ppermute | solution.py:37
  359.6 14.4 %collective-permute-start.56 = (bf16[80,256]{1,0:T(8,128)(2,1)S(1)}, bf16[80,256]{1,0:T(8,128)(2,1)S(1)}, u32[]{:S(2)}, u32[]{:S(2)}) collective-permute-start(bf16[80,256]{1,0:T(8,128)(2,1)S(1)} %get-tuple-element.36.refs_0_), channel_id=1, source_target_pairs={{0,8},{64,72},{1,9},{65,73},{2,10},{66,74},{3,11},{67,75},{4,12},{... | collective-permute-start | bytes 122888 | tf_op jit(solution)/shard_map/ppermute | solution.py:37
  361.8 12.8 %collective-permute-start.57 = (bf16[80,256]{1,0:T(8,128)(2,1)S(1)}, bf16[80,256]{1,0:T(8,128)(2,1)S(1)}, u32[]{:S(2)}, u32[]{:S(2)}) collective-permute-start(bf16[80,256]{1,0:T(8,128)(2,1)S(1)} %get-tuple-element.36.refs_0_), channel_id=1, source_target_pairs={{0,16},{64,80},{1,17},{65,81},{2,18},{66,82},{3,19},{67,83},{4,20}... | collective-permute-start | bytes 122888 | tf_op jit(solution)/shard_map/ppermute | solution.py:37
  362.5 15.4 %collective-permute-start.58 = (bf16[80,256]{1,0:T(8,128)(2,1)S(1)}, bf16[80,256]{1,0:T(8,128)(2,1)S(1)}, u32[]{:S(2)}, u32[]{:S(2)}) collective-permute-start(bf16[80,256]{1,0:T(8,128)(2,1)S(1)} %get-tuple-element.36.refs_0_), channel_id=1, source_target_pairs={{0,24},{64,88},{1,25},{65,89},{2,26},{66,90},{3,27},{67,91},{4,28}... | collective-permute-start | bytes 122888 | tf_op jit(solution)/shard_map/ppermute | solution.py:37
  362.6 22.8 %collective-permute-start.69 = (bf16[80,256]{1,0:T(8,128)(2,1)S(1)}, bf16[80,256]{1,0:T(8,128)(2,1)S(1)}, u32[]{:S(2)}, u32[]{:S(2)}) collective-permute-start(bf16[80,256]{1,0:T(8,128)(2,1)S(1)} %get-tuple-element.35.refs_0_), channel_id=1, source_target_pairs={{0,64},{64,1},{1,65},{65,0},{2,66},{66,3},{3,67},{67,2},{4,68},{68... | collective-permute-start | bytes 122888 | tf_op jit(solution)/shard_map/ppermute | solution.py:37
  373.2 15.2 %collective-permute-start.85 = (bf16[4,64,256]{2,1,0:T(8,128)(2,1)}, bf16[4,64,256]{2,1,0:T(8,128)(2,1)S(1)}, u32[]{:S(2)}, u32[]{:S(2)}) collective-permute-start(bf16[4,64,256]{2,1,0:T(8,128)(2,1)} %shard_map.89.refs_0_), channel_id=1, source_target_pairs={{0,8},{64,72},{1,9},{65,73},{2,10},{66,74},{3,11},{67,75},{4,12},{... | collective-permute-start | bytes 393224 | tf_op jit(solution)/shard_map/ppermute | solution.py:37
  374.0 13.8 %collective-permute-start.70 = (bf16[80,256]{1,0:T(8,128)(2,1)S(1)}, bf16[80,256]{1,0:T(8,128)(2,1)S(1)}, u32[]{:S(2)}, u32[]{:S(2)}) collective-permute-start(bf16[80,256]{1,0:T(8,128)(2,1)S(1)} %get-tuple-element.35.refs_0_), channel_id=1, source_target_pairs={{0,1},{64,65},{1,0},{65,64},{2,3},{66,67},{3,2},{67,66},{4,5},{68,... | collective-permute-start | bytes 122888 | tf_op jit(solution)/shard_map/ppermute | solution.py:37
  374.5 13.2 %collective-permute-start.71 = (bf16[80,256]{1,0:T(8,128)(2,1)S(1)}, bf16[80,256]{1,0:T(8,128)(2,1)S(1)}, u32[]{:S(2)}, u32[]{:S(2)}) collective-permute-start(bf16[80,256]{1,0:T(8,128)(2,1)S(1)} %get-tuple-element.35.refs_0_), channel_id=1, source_target_pairs={{0,65},{64,0},{1,64},{65,1},{2,67},{66,2},{3,66},{67,3},{4,69},{68... | collective-permute-start | bytes 122888 | tf_op jit(solution)/shard_map/ppermute | solution.py:37
  385.3 29.5 %collective-permute-start.59 = (bf16[4,80,256]{2,1,0:T(8,128)(2,1)}, bf16[4,80,256]{2,1,0:T(8,128)(2,1)S(1)}, u32[]{:S(2)}, u32[]{:S(2)}) collective-permute-start(bf16[4,80,256]{2,1,0:T(8,128)(2,1)} %shard_map.85.refs_0_), channel_id=1, source_target_pairs={{0,64},{64,1},{1,65},{65,0},{2,66},{66,3},{3,67},{67,2},{4,68},{68... | collective-permute-start | bytes 491528 | tf_op jit(solution)/shard_map/ppermute | solution.py:37
  385.4 30.0 %collective-permute-start.60 = (bf16[4,80,256]{2,1,0:T(8,128)(2,1)}, bf16[4,80,256]{2,1,0:T(8,128)(2,1)S(1)}, u32[]{:S(2)}, u32[]{:S(2)}) collective-permute-start(bf16[4,80,256]{2,1,0:T(8,128)(2,1)} %shard_map.85.refs_0_), channel_id=1, source_target_pairs={{0,1},{64,65},{1,0},{65,64},{2,3},{66,67},{3,2},{67,66},{4,5},{68,... | collective-permute-start | bytes 491528 | tf_op jit(solution)/shard_map/ppermute | solution.py:37
  388.4 60.5 %collective-permute-start.61 = (bf16[4,80,256]{2,1,0:T(8,128)(2,1)}, bf16[4,80,256]{2,1,0:T(8,128)(2,1)S(1)}, u32[]{:S(2)}, u32[]{:S(2)}) collective-permute-start(bf16[4,80,256]{2,1,0:T(8,128)(2,1)} %shard_map.85.refs_0_), channel_id=1, source_target_pairs={{0,65},{64,0},{1,64},{65,1},{2,67},{66,2},{3,66},{67,3},{4,69},{68... | collective-permute-start | bytes 491528 | tf_op jit(solution)/shard_map/ppermute | solution.py:37
  395.4 75.9 %collective-permute-start.72 = (bf16[4,80,256]{2,1,0:T(8,128)(2,1)}, bf16[4,80,256]{2,1,0:T(8,128)(2,1)}, u32[]{:S(2)}, u32[]{:S(2)}) collective-permute-start(bf16[4,80,256]{2,1,0:T(8,128)(2,1)} %shard_map.87.refs_0_), channel_id=1, source_target_pairs={{0,2},{64,66},{1,3},{65,67},{2,4},{66,68},{3,5},{67,69},{4,6},{68,... | collective-permute-start | bytes 491528 | tf_op jit(solution)/shard_map/ppermute | solution.py:37
  396.4 75.0 %collective-permute-start.73 = (bf16[4,80,256]{2,1,0:T(8,128)(2,1)}, bf16[4,80,256]{2,1,0:T(8,128)(2,1)}, u32[]{:S(2)}, u32[]{:S(2)}) collective-permute-start(bf16[4,80,256]{2,1,0:T(8,128)(2,1)} %shard_map.87.refs_0_), channel_id=1, source_target_pairs={{0,4},{64,68},{1,5},{65,69},{2,6},{66,70},{3,7},{67,71},{4,0},{68,... | collective-permute-start | bytes 491528 | tf_op jit(solution)/shard_map/ppermute | solution.py:37
  414.8 56.6 %collective-permute-start.74 = (bf16[4,80,256]{2,1,0:T(8,128)(2,1)}, bf16[4,80,256]{2,1,0:T(8,128)(2,1)}, u32[]{:S(2)}, u32[]{:S(2)}) collective-permute-start(bf16[4,80,256]{2,1,0:T(8,128)(2,1)} %shard_map.87.refs_0_), channel_id=1, source_target_pairs={{0,6},{64,70},{1,7},{65,71},{2,0},{66,64},{3,1},{67,65},{4,2},{68,... | collective-permute-start | bytes 491528 | tf_op jit(solution)/shard_map/ppermute | solution.py:37
  415.4 89.4 %collective-permute-start.88 = (bf16[4,4,64,256]{3,2,1,0:T(8,128)(2,1)}, bf16[4,4,64,256]{3,2,1,0:T(8,128)(2,1)}, u32[]{:S(2)}, u32[]{:S(2)}) collective-permute-start(bf16[4,4,64,256]{3,2,1,0:T(8,128)(2,1)} %shard_map.90.refs_16_), channel_id=1, source_target_pairs={{0,32},{64,96},{1,33},{65,97},{2,34},{66,98},{3,35},{67,99},{4,36}... | collective-permute-start | bytes 1572872 | tf_op jit(solution)/shard_map/ppermute | solution.py:37
  449.0 44.8 %collective-permute-start.95 = (bf16[224,256]{1,0:T(8,128)(2,1)S(1)}, bf16[224,256]{1,0:T(8,128)(2,1)}, u32[]{:S(2)}, u32[]{:S(2)}) collective-permute-start(bf16[224,256]{1,0:T(8,128)(2,1)S(1)} %pad_maximum_fusion), channel_id=1, source_target_pairs={{0,32},{64,96},{1,33},{65,97},{2,34},{66,98},{3,35},{67,99},{4,36}... | collective-permute-start | bytes 344072 | tf_op jit(solution)/shard_map/ppermute | solution.py:37
  471.3 33.4 %collective-permute-start.63 = (bf16[4,4,80,256]{3,2,1,0:T(8,128)(2,1)}, bf16[4,4,80,256]{3,2,1,0:T(8,128)(2,1)S(1)}, u32[]{:S(2)}, u32[]{:S(2)}) collective-permute-start(bf16[4,4,80,256]{3,2,1,0:T(8,128)(2,1)} %shard_map.86.refs_0_), channel_id=1, source_target_pairs={{0,2},{64,66},{1,3},{65,67},{2,4},{66,68},{3,5},{67,69},{4,6},{68,... | collective-permute-start | bytes 1966088 | tf_op jit(solution)/shard_map/ppermute | solution.py:37
  493.1 12.8 %collective-permute-start.76 = (bf16[4,4,80,256]{3,2,1,0:T(8,128)(2,1)}, bf16[4,4,80,256]{3,2,1,0:T(8,128)(2,1)S(1)}, u32[]{:S(2)}, u32[]{:S(2)}) collective-permute-start(bf16[4,4,80,256]{3,2,1,0:T(8,128)(2,1)} %shard_map.88.refs_8_), channel_id=1, source_target_pairs={{0,8},{64,72},{1,9},{65,73},{2,10},{66,74},{3,11},{67,75},{4,12},{... | collective-permute-start | bytes 1966088 | tf_op jit(solution)/shard_map/ppermute | solution.py:37
  495.5 13.4 %collective-permute-start.89 = (bf16[4,4,64,256]{3,2,1,0:T(8,128)(2,1)S(1)}, bf16[4,4,64,256]{3,2,1,0:T(8,128)(2,1)S(1)}, u32[]{:S(2)}, u32[]{:S(2)}) collective-permute-start(bf16[4,4,64,256]{3,2,1,0:T(8,128)(2,1)S(1)} %copy-done.2), channel_id=1, source_target_pairs={{0,64},{64,1},{1,65},{65,0},{2,66},{66,3},{3,67},{67,2},{4,68},{68... | collective-permute-start | bytes 1572872 | tf_op jit(solution)/shard_map/ppermute | solution.py:37
  504.7 9.9 collective-permute-start.65
  505.9 11.0 %collective-permute-start.78 = (bf16[4,4,80,256]{3,2,1,0:T(8,128)(2,1)S(1)}, bf16[4,4,80,256]{3,2,1,0:T(8,128)(2,1)}, u32[]{:S(2)}, u32[]{:S(2)}) collective-permute-start(bf16[4,4,80,256]{3,2,1,0:T(8,128)(2,1)S(1)} %collective-permute-done.76.refs_10_), channel_id=1, source_target_pairs={{0,8},{64,72},{1,9},{65,73},{2,10},{66,74},{3,11},{67,75},{4,12},{... | collective-permute-start | bytes 1966088 | tf_op jit(solution)/shard_map/ppermute | solution.py:37
  509.1 10.7 %collective-permute-start.91 = (bf16[4,4,64,256]{3,2,1,0:T(8,128)(2,1)S(1)}, bf16[4,4,64,256]{3,2,1,0:T(8,128)(2,1)S(1)}, u32[]{:S(2)}, u32[]{:S(2)}) collective-permute-start(bf16[4,4,64,256]{3,2,1,0:T(8,128)(2,1)S(1)} %collective-permute-done.89.refs_18_), channel_id=1, source_target_pairs={{0,64},{64,1},{1,65},{65,0},{2,66},{66,3},{3,67},{67,2},{4,68},{68... | collective-permute-start | bytes 1572872 | tf_op jit(solution)/shard_map/ppermute | solution.py:37
  509.4 10.6 %collective-permute-start.64 = (bf16[4,4,80,256]{3,2,1,0:T(8,128)(2,1)S(1)}, bf16[4,4,80,256]{3,2,1,0:T(8,128)(2,1)S(1)}, u32[]{:S(2)}, u32[]{:S(2)}) collective-permute-start(bf16[4,4,80,256]{3,2,1,0:T(8,128)(2,1)S(1)} %collective-permute-done.63.refs_2_), channel_id=1, source_target_pairs={{0,32},{64,96},{1,33},{65,97},{2,34},{66,98},{3,35},{67,99},{4,36}... | collective-permute-start | bytes 1966088 | tf_op jit(solution)/shard_map/ppermute | solution.py:37
  514.6 10.1 %collective-permute-start.67 = (bf16[4,4,80,256]{3,2,1,0:T(8,128)(2,1)}, bf16[4,4,80,256]{3,2,1,0:T(8,128)(2,1)}, u32[]{:S(2)}, u32[]{:S(2)}) collective-permute-start(bf16[4,4,80,256]{3,2,1,0:T(8,128)(2,1)} %collective-permute-done.65.refs_4_), channel_id=1, source_target_pairs={{0,2},{64,66},{1,3},{65,67},{2,4},{66,68},{3,5},{67,69},{4,6},{68,... | collective-permute-start | bytes 1966088 | tf_op jit(solution)/shard_map/ppermute | solution.py:37
  516.9 12.3 %collective-permute-start.80 = (bf16[4,4,80,256]{3,2,1,0:T(8,128)(2,1)}, bf16[4,4,80,256]{3,2,1,0:T(8,128)(2,1)}, u32[]{:S(2)}, u32[]{:S(2)}) collective-permute-start(bf16[4,4,80,256]{3,2,1,0:T(8,128)(2,1)} %collective-permute-done.78.refs_12_), channel_id=1, source_target_pairs={{0,8},{64,72},{1,9},{65,73},{2,10},{66,74},{3,11},{67,75},{4,12},{... | collective-permute-start | bytes 1966088 | tf_op jit(solution)/shard_map/ppermute | solution.py:37
  520.0 9.9 collective-permute-start.93
  520.1 13.0 %collective-permute-start.66 = (bf16[4,4,80,256]{3,2,1,0:T(8,128)(2,1)}, bf16[4,4,80,256]{3,2,1,0:T(8,128)(2,1)}, u32[]{:S(2)}, u32[]{:S(2)}) collective-permute-start(bf16[4,4,80,256]{3,2,1,0:T(8,128)(2,1)} %collective-permute-done.65.refs_4_), channel_id=1, source_target_pairs={{0,32},{64,96},{1,33},{65,97},{2,34},{66,98},{3,35},{67,99},{4,36}... | collective-permute-start | bytes 1966088 | tf_op jit(solution)/shard_map/ppermute | solution.py:37
  521.7 11.4 %collective-permute-start.79 = (bf16[4,4,80,256]{3,2,1,0:T(8,128)(2,1)}, bf16[4,4,80,256]{3,2,1,0:T(8,128)(2,1)}, u32[]{:S(2)}, u32[]{:S(2)}) collective-permute-start(bf16[4,4,80,256]{3,2,1,0:T(8,128)(2,1)} %collective-permute-done.78.refs_12_), channel_id=1, source_target_pairs={{0,32},{64,96},{1,33},{65,97},{2,34},{66,98},{3,35},{67,99},{4,36}... | collective-permute-start | bytes 1966088 | tf_op jit(solution)/shard_map/ppermute | solution.py:37
  (112 other events, 866.4 us)

commit v2 on v0

v2 whole, which is shorter than its diff:
```python
import itertools

import jax
import jax.numpy as jnp
from jax import lax
from jax.experimental import pallas as pl
from jax.experimental.pallas import tpu as pltpu
from jax.sharding import Mesh
from jax.sharding import PartitionSpec as P

STEP = 10


beta_one = 0.9
beta_two = 0.99
eps = 1e-08
galore_scale = 4.0

BF = jnp.bfloat16
F32 = jnp.float32
AXES = ("zl", "c", "y1", "y0", "x1", "x0", "zh")
FSDP = ("y1", "y0", "x1", "x0", "zh")
ORDERS = ("xyz", "yzx", "zxy")


def flat(co):
    return ((co["z"] % 2) * 2 + co["c"]) * 32 + (co["y"] * 4 + co["x"]) * 2 + co["z"] // 2


def permute(arr, move):
    pairs = []
    for c in range(2):
        for y in range(4):
            for x in range(4):
                for z in range(4):
                    co = {"c": c, "y": y, "x": x, "z": z}
                    pairs.append((flat(co), flat(move(dict(co)))))
    return lax.ppermute(arr, AXES, pairs)


def swap(arr, axis, late=0):
    def move(co):
        co[axis] ^= 3 if co["c"] != late else 1
        return co

    return permute(arr, move)


def swap_core(arr):
    def move(co):
        co["c"] ^= 1
        return co

    return permute(arr, move)


def swap_low(arr):
    def move(co):
        co["z"] ^= 1
        return co

    return permute(arr, move)


def split_rows(rows):
    tiles = rows // 16
    a = -(-tiles // 3)
    b = -(-(tiles - a) // 2)
    return (a * 16, b * 16, rows - (a + b) * 16)


def starts(sizes):
    return (0, sizes[0], sizes[0] + sizes[1])


def join(arrays, gots, extra):
    n = len(arrays)
    *both, extra = lax.optimization_barrier((*arrays, *gots, extra))
    return [jnp.stack(pair) for pair in zip(both[:n], both[n:])], extra


def gather(piece, extra):
    for axis in "zxy":
        (piece,), extra = join([piece], [swap(piece, axis, late=1)], extra)
    sizes = split_rows(piece.shape[3])
    parts = [piece[:, :, :, begin : begin + size] for size, begin in zip(sizes, starts(sizes))]
    for stage in (2, 1):
        gots = [swap(part, order[stage]) for order, part in zip(ORDERS, parts)]
        parts, extra = join(parts, gots, extra)
    return [(part, swap(part, order[0])) for order, part in zip(ORDERS, parts)], extra


def bits(place, core):
    high = place // 2
    low = lax.bitwise_xor(place % 2, high)
    return low + core * (high - low), high + core * (low - high)


def place_of(u, v, core):
    high, low = v + core * (u - v), u + core * (v - u)
    return high * 2 + lax.bitwise_xor(high, low)


def load_block(parts, y, x, pos_ref, core):
    y, x = bits(lax.bitwise_xor(pos_ref[0], y), core), bits(lax.bitwise_xor(pos_ref[1], x), core)
    rows = []
    for place in range(4):
        z = bits(lax.bitwise_xor(pos_ref[2], place), core)
        by = {"y": y, "x": x, "z": z}
        for order, part in zip(ORDERS, parts):
            rows.append(part[tuple(by[a][0] for a in order) + (y[1], x[1], z[1])])
    return jnp.concatenate(rows, axis=0)


def part_scratch(sizes, cols):
    return [pltpu.VMEM((2, 2, 2, 2, 2, 2, size, cols), BF) for size in sizes]


def load_copies(arrays, parts, sem):
    return [
        pltpu.make_async_copy(arrays[2 * i + u], part.at[u], sem.at[2 * i + u])
        for i, part in enumerate(parts)
        for u in range(2)
    ]


def project(a0, a1, parts, pos):
    tok, depth = a0.shape
    arrays = [a for pair in parts for a in pair]
    cols = arrays[0].shape[-1]
    kb = 1024
    steps = depth // kb

    def kernel(pos_ref, *refs):
        srcs, (a0_ref, a1_ref, o0, o1, s0, s1), scratch, sem = refs[:6], refs[6:12], refs[12:15], refs[15]
        step = pl.program_id(0)

        @pl.when(step == 0)
        def _():
            copies = load_copies(srcs, scratch, sem)
            for copy in copies:
                copy.start()
            s0[...] = jnp.zeros_like(s0)
            s1[...] = jnp.zeros_like(s1)
            for copy in copies:
                copy.wait()

        y, x = step // 2, step % 2 * 2
        b = jnp.concatenate([load_block(scratch, y, x + k, pos_ref, pos_ref[3]) for k in range(2)], axis=0)
        s0[...] += jnp.dot(a0_ref[...], b, preferred_element_type=F32)
        s1[...] += jnp.dot(a1_ref[...], b, preferred_element_type=F32)

        @pl.when(step == steps - 1)
        def _():
            o0[...] = s0[...].astype(BF)
            o1[...] = s1[...].astype(BF)

    return pl.pallas_call(
        kernel,
        out_shape=[jax.ShapeDtypeStruct((tok, cols), BF)] * 2,
        grid_spec=pltpu.PrefetchScalarGridSpec(
            num_scalar_prefetch=1,
            grid=(steps,),
            in_specs=[pl.BlockSpec(memory_space=pl.ANY)] * 6
            + [pl.BlockSpec((tok, kb), lambda i, w: (0, i))] * 2,
            out_specs=[pl.BlockSpec((tok, cols), lambda i, w: (0, 0))] * 2,
            scratch_shapes=[pltpu.VMEM((tok, cols), F32)] * 2
            + part_scratch([p[0].shape[-2] for p in parts], cols)
            + [pltpu.SemaphoreType.DMA((6,))],
        ),
        compiler_params=pltpu.CompilerParams(vmem_limit_bytes=32 * 2**20),
        cost_estimate=pl.CostEstimate(
            flops=4 * tok * depth * cols, bytes_accessed=4 * tok * depth + 2 * depth * cols, transcendentals=0
        ),
    )(pos, *arrays, a0, a1)


def partials(g0, g1, p0, p1, pos):
    tok, ffw = g0.shape
    cols = p0.shape[1]
    nb = ffw // 16
    rows = nb // 4
    sizes = split_rows(rows)

    def block(i, w):
        y, x = place_of(i // 8, i // 2 % 2, w[3]), place_of(i // 4 % 2, i % 2, w[3])
        return 0, lax.bitwise_xor(w[0], y) * 4 + lax.bitwise_xor(w[1], x)

    def kernel(pos_ref, g0_ref, g1_ref, p0_ref, p1_ref, *refs):
        outs, scratch = refs[:6], refs[6]
        dims = (((0,), (0,)), ((), ()))
        i = pl.program_id(0)
        u = {"y": i // 8, "x": i // 4 % 2}
        vy, vx = i // 2 % 2, i % 2
        scratch[...] = (
            (
                lax.dot_general(g0_ref[...], p0_ref[...], dims, preferred_element_type=F32)
                + lax.dot_general(g1_ref[...], p1_ref[...], dims, preferred_element_type=F32)
            )
            .astype(BF)
            .reshape(4, rows, cols)
        )
        for part, (order, size, begin) in enumerate(zip(ORDERS, sizes, starts(sizes))):
            for first in range(2):
                ref = outs[2 * part + first]

                def store(uz, ref=ref, order=order, size=size, begin=begin):
                    at = {**u, "z": uz}
                    for vz in range(2):
                        z = lax.bitwise_xor(pos_ref[2], place_of(uz, vz, pos_ref[3]))
                        ref[at[order[1]], at[order[2]], vy, vx, vz] = scratch[z, pl.ds(begin, size)]

                if order[0] == "z":
                    store(first)
                else:

                    @pl.when(u[order[0]] == first)
                    def _(store=store):
                        store(0)
                        store(1)

    shapes = [(2, 2, 2, 2, 2, size, cols) for size in sizes for _ in range(2)]
    return pl.pallas_call(
        kernel,
        out_shape=[jax.ShapeDtypeStruct(s, BF) for s in shapes],
        grid_spec=pltpu.PrefetchScalarGridSpec(
            num_scalar_prefetch=1,
            grid=(16,),
            in_specs=[
                pl.BlockSpec((tok, nb), block),
                pl.BlockSpec((tok, nb), block),
                pl.BlockSpec((tok, cols), lambda i, w: (0, 0)),
                pl.BlockSpec((tok, cols), lambda i, w: (0, 0)),
            ],
            out_specs=[pl.BlockSpec(s, lambda i, w: (0,) * 7) for s in shapes],
            scratch_shapes=[pltpu.VMEM((4, rows, cols), BF)],
        ),
        compiler_params=pltpu.CompilerParams(vmem_limit_bytes=40 * 2**20),
        cost_estimate=pl.CostEstimate(
            flops=4 * tok * ffw * cols, bytes_accessed=4 * tok * ffw + 2 * ffw * cols, transcendentals=0
        ),
    )(pos, g0, g1, p0, p1)


def updates(basis, own, other, pos):
    rows, rank = basis.shape
    arrays = [a for parts in (own, other) for pair in parts for a in pair]
    half = arrays[0].shape[-1]
    sizes = [parts[0].shape[-2] for parts in own]
    nb = 4 * sum(sizes)
    ffw = 16 * nb

    def kernel(pos_ref, *refs):
        srcs, (b_ref, o), s0, s1, sem = refs[:12], refs[12:14], refs[14:17], refs[17:20], refs[20]
        step = pl.program_id(0)

        @pl.when(step == 0)
        def _():
            copies = load_copies(srcs[:6], s0, sem.at[0]) + load_copies(srcs[6:], s1, sem.at[1])
            for copy in copies:
                copy.start()
            for copy in copies:
                copy.wait()

        dims = (((1,), (1,)), ((), ()))
        core = pos_ref[3]
        y, x = step // 4, step % 4
        total = lax.dot_general(
            b_ref[core], load_block(s0, y, x, pos_ref, core), dims, preferred_element_type=F32
        ) + lax.dot_general(
            b_ref[1 - core], load_block(s1, y, x, pos_ref, 1 - core), dims, preferred_element_type=F32
        )
        o[...] = (-galore_scale * total).astype(BF)

    halves = jnp.stack([basis[:, :half], basis[:, half:]])
    return pl.pallas_call(
        kernel,
        out_shape=jax.ShapeDtypeStruct((rows, ffw), BF),
        grid_spec=pltpu.PrefetchScalarGridSpec(
            num_scalar_prefetch=1,
            grid=(16,),
            in_specs=[pl.BlockSpec(memory_space=pl.ANY)] * 12
            + [pl.BlockSpec((2, rows, half), lambda i, w: (0, 0, 0))],
            out_specs=pl.BlockSpec((rows, nb), lambda i, w: (0, i)),
            scratch_shapes=part_scratch(sizes, half) * 2 + [pltpu.SemaphoreType.DMA((2, 6))],
        ),
        compiler_params=pltpu.CompilerParams(vmem_limit_bytes=40 * 2**20),
        cost_estimate=pl.CostEstimate(
            flops=2 * rows * ffw * rank, bytes_accessed=2 * (ffw * rank + rows * ffw), transcendentals=0
        ),
    )(pos, *arrays, halves)


def add(a, b):
    return (a.astype(F32) + b.astype(F32)).astype(BF)


def local(activations, out_grads, basis, first_moment, second_moment):
    core, zl = lax.axis_index("c"), lax.axis_index("zl")
    places = [lax.axis_index(a + "1") * 2 + lax.axis_index(a + "0") for a in "yx"] + [lax.axis_index("zh") * 2 + zl]
    pos = jnp.stack(places + [core]).astype(jnp.int32)
    rank = basis.shape[1]
    half = rank // 2
    shard = out_grads.shape[1] // 64
    brows = basis.shape[0] // 2

    act_other = swap_core(activations)
    g_other = swap_core(out_grads)

    parts, zl = gather(lax.dynamic_slice(basis, (zl * brows, core * half), (brows, half)), zl)
    proj_own, proj_other = project(activations, act_other, parts, pos)
    sums = partials(out_grads, g_other, proj_own, proj_other, pos)

    keeps, sends = sums[0::2], sums[1::2]
    for stage in range(3):
        gots = [swap(send, order[stage]) for order, send in zip(ORDERS, sends)]
        sends = [add(keep[1], got[1]) for keep, got in zip(keeps, gots)]
        keeps = [add(keep[0], got[0]) for keep, got in zip(keeps, gots)]
    keep, send = jnp.concatenate(keeps, axis=-2), jnp.concatenate(sends, axis=-2)
    for axis in "yx":
        got = swap(send, axis, late=1)
        send = add(keep[1], got[1])
        keep = add(keep[0], got[0])
    reduced = add(keep, swap(send, "z", late=1))

    def adam(first, second, red):
        new_first = beta_one * first + (1.0 - beta_one) * red
        new_second = beta_two * second + (1.0 - beta_two) * red * red
        return new_first, new_second

    at = (zl * shard, core * half)
    new_first, new_second = adam(
        lax.dynamic_slice(first_moment, at, (shard, half)),
        lax.dynamic_slice(second_moment, at, (shard, half)),
        reduced.astype(F32),
    )
    corrected = new_first / (1.0 - beta_one**STEP)
    normalized = (corrected / (jnp.sqrt(new_second / (1.0 - beta_two**STEP)) + eps)).astype(BF)

    other = swap_core(reduced)
    row = jnp.where(core == 0, jnp.concatenate([reduced, other], 1), jnp.concatenate([other, reduced], 1))
    other = swap_low(row)
    rows = jnp.where(zl == 0, jnp.concatenate([row, other], 0), jnp.concatenate([other, row], 0))

    own, rows = gather(normalized, rows)
    other = [(swap_core(a), swap_core(b)) for a, b in own]
    update = updates(basis, own, other, pos)
    out_first, out_second = adam(first_moment, second_moment, rows.astype(F32))
    return (update, out_first, out_second)


def solution(mesh):
    chips = Mesh(mesh.devices.reshape(2, 2, 2, 2, 2, 2, 2), AXES)
    in_specs = (P(AXES, None), P(AXES, None), P(FSDP, None), P(FSDP, None), P(FSDP, None))
    out_specs = (P(FSDP, None), P(FSDP, None), P(FSDP, None))
    return jax.shard_map(local, mesh=chips, in_specs=in_specs, out_specs=out_specs, check_vma=False)
```

time: 694 us -> 231 us (0.33)
  waiting for transfers between devices: 608 us -> 118 us
  starting transfers between devices: 0.16 us -> 65.1 us
  Pallas kernels: 0 us -> 37.4 us
  local copies, waits for them, and re-layouts: 38 us -> 4.15 us
  matrix products: 29.4 us -> 0 us
  between operations: 13.8 us -> 1.1 us
    unnamed x5 -> x0, waiting for transfers between devices: 316 us -> none
    all_gather x2 -> x0, waiting for transfers between devices: 252 us -> none  [the longest x1 141 us: local(): lax.all_gather(normalized, 'fsdp', axis=0, tiled=True)]
    ppermute x0 -> x46, waiting for transfers between devices: none -> 118 us  [permute(): return lax.ppermute(arr, AXES, pairs)]
    ppermute x0 -> x46, starting transfers between devices: none -> 65.1 us  [permute(): return lax.ppermute(arr, AXES, pairs)]
    psum x1 -> x0, waiting for transfers between devices: 39.8 us -> none  [local(): reduced = lax.psum(own_rows, 'grp').astype(jnp.float32)]
    pallas_call x0 -> x3, Pallas kernels: none -> 37.4 us  [the longest x1 15.4 us: partials(): pl.pallas_call(kernel, out_shape=[jax.ShapeDtypeStruct(s, BF) for s in sh...]
    unnamed x13 -> x10, local copies, waits for them, and re-layouts: 36 us -> 3.29 us
    dot_general x3 -> x0, matrix products: 29.4 us -> none  [the longest x1 12.1 us: local(): lax.dot_general(basis, lax.all_gather(normalized, 'fsdp', axis=0, tiled=T...]
  transfers between devices with their start and end apart: 4 -> 46, of which waited for: 4 -> 27; matrix products, arithmetic and copies ran while one was open for 1% -> 2% of each run, Pallas kernels for 0% -> 4%
where the time goes in v2:
time: 231 us
  waiting for transfers between devices  118 us (51%)
  starting transfers between devices  65.1 us (28%)
  Pallas kernels  37.4 us (16%)
  other arithmetic  5.42 us (2%)
  local copies, waits for them, and re-layouts  4.15 us (2%)
    ppermute x46, waiting for transfers between devices, permute(): return lax.ppermute(arr, AXES, pairs)  118 us
    ppermute x46, starting transfers between devices, permute(): return lax.ppermute(arr, AXES, pairs)  65.1 us
    pallas_call x1, Pallas kernels, partials(): pl.pallas_call(kernel, out_shape=[jax.ShapeDtypeStruct(s, BF) for s in sh...  15.4 us
    pallas_call x1, Pallas kernels, updates(): pl.pallas_call(kernel, out_shape=jax.ShapeDtypeStruct((rows, ffw), BF), g...  13.3 us
    pallas_call x1, Pallas kernels, project(): pl.pallas_call(kernel, out_shape=[jax.ShapeDtypeStruct((tok, cols), BF)]...  8.71 us
  transfers between devices with their start and end apart: 46, of which 27 were waited for; matrix products, arithmetic and copies ran while one was open for 2% of the time, Pallas kernels for 4%

profile of v2, /device:TPU:1, one launch (start us, length us, event | category | flops | bytes accessed | tf_op | source)
XLA Modules:
  0.0 230.8 jit_solution(8258185057691311703)
XLA Ops:
  0.6 1.5 collective-permute-start.9
  3.1 1.7 collective-permute-start
  4.8 1.7 collective-permute-done
  7.8 2.6 %collective-permute-done.1 = bf16[2,128,256]{2,1,0:T(8,128)(2,1)S(1)} collective-permute-done((bf16[2,128,256]{2,1,0:T(8,128)(2,1)S(1)}, bf16[2,128,256]{2,1,0:T(8,128)(2,1)S(1)}, u32[]{:S(2)}, u32[]{:S(2)}) %collective-permute-start.1) | collective-permute-done | bytes 131104 | tf_op jit(solution)/shard_map/ppermute | solution.py:38
  11.8 4.0 %collective-permute-done.2 = bf16[2,2,128,256]{3,2,1,0:T(8,128)(2,1)S(1)} collective-permute-done((bf16[2,2,128,256]{3,2,1,0:T(8,128)(2,1)S(1)}, bf16[2,2,128,256]{3,2,1,0:T(8,128)(2,1)S(1)}, u32[]{:S(2)}, u32[]{:S(2)}) %collective-permute-start.2) | collective-permute-done | bytes 262176 | tf_op jit(solution)/shard_map/ppermute | solution.py:38
  15.8 2.6 %collective-permute-start.4 = (bf16[2,2,2,48,256]{4,3,2,1,0:T(8,128)(2,1)S(1)}, bf16[2,2,2,48,256]{4,3,2,1,0:T(8,128)(2,1)S(1)}, u32[]{:S(2)}, u32[]{:S(2)}) collective-permute-start(bf16[2,2,2,48,256]{4,3,2,1,0:T(8,128)(2,1)S(1)} %get-tuple-element.68), channel_id=1, source_target_pairs={{0,2},{64,66},{1,3},{65,67},{2,0},{66,64},{3,1},{67,65},{4,6},{68,... | collective-permute-start | bytes 589832 | tf_op jit(solution)/shard_map/ppermute | solution.py:38
  18.3 3.5 %collective-permute-start.3 = (bf16[2,2,2,48,256]{4,3,2,1,0:T(8,128)(2,1)S(1)}, bf16[2,2,2,48,256]{4,3,2,1,0:T(8,128)(2,1)S(1)}, u32[]{:S(2)}, u32[]{:S(2)}) collective-permute-start(bf16[2,2,2,48,256]{4,3,2,1,0:T(8,128)(2,1)S(1)} %get-tuple-element.66), channel_id=1, source_target_pairs={{0,64},{64,0},{1,65},{65,1},{2,66},{66,2},{3,67},{67,3},{4,68},{68... | collective-permute-start | bytes 589832 | tf_op jit(solution)/shard_map/ppermute | solution.py:38
  21.9 2.8 %collective-permute-start.5 = (bf16[2,2,2,32,256]{4,3,2,1,0:T(8,128)(2,1)S(1)}, bf16[2,2,2,32,256]{4,3,2,1,0:T(8,128)(2,1)S(1)}, u32[]{:S(2)}, u32[]{:S(2)}) collective-permute-start(bf16[2,2,2,32,256]{4,3,2,1,0:T(8,128)(2,1)S(1)} %pad_maximum_fusion.19), channel_id=1, source_target_pairs={{0,8},{64,72},{1,9},{65,73},{2,10},{66,74},{3,11},{67,75},{4,12},{... | collective-permute-start | bytes 393224 | tf_op jit(solution)/shard_map/ppermute | solution.py:38
  24.7 2.4 %collective-permute-done.5 = bf16[2,2,2,32,256]{4,3,2,1,0:T(8,128)(2,1)S(1)} collective-permute-done((bf16[2,2,2,32,256]{4,3,2,1,0:T(8,128)(2,1)S(1)}, bf16[2,2,2,32,256]{4,3,2,1,0:T(8,128)(2,1)S(1)}, u32[]{:S(2)}, u32[]{:S(2)}) %collective-permute-start.5) | collective-permute-done | bytes 131104 | tf_op jit(solution)/shard_map/ppermute | solution.py:38
  27.8 2.8 %collective-permute-start.6 = (bf16[2,2,2,2,48,256]{5,4,3,2,1,0:T(8,128)(2,1)S(1)}, bf16[2,2,2,2,48,256]{5,4,3,2,1,0:T(8,128)(2,1)S(1)}, u32[]{:S(2)}, u32[]{:S(2)}) collective-permute-start(bf16[2,2,2,2,48,256]{5,4,3,2,1,0:T(8,128)(2,1)S(1)} %pad_maximum_fusion.12), channel_id=1, source_target_pairs={{0,8},{64,72},{1,9},{65,73},{2,10},{66,74},{3,11},{67,75},{4,12},{... | collective-permute-start | bytes 1179656 | tf_op jit(solution)/shard_map/ppermute | solution.py:38
  32.0 5.1 %collective-permute-done.8 = bf16[2,2,2,2,32,256]{5,4,3,2,1,0:T(8,128)(2,1)S(1)} collective-permute-done((bf16[2,2,2,2,32,256]{5,4,3,2,1,0:T(8,128)(2,1)S(1)}, bf16[2,2,2,2,32,256]{5,4,3,2,1,0:T(8,128)(2,1)S(1)}, u32[]{:S(2)}, u32[]{:S(2)}) %collective-permute-start.8) | collective-permute-done | bytes 262176 | tf_op jit(solution)/shard_map/ppermute | solution.py:38
  41.2 8.2 %collective-permute-done.12.refs_5_ = bf16[2,2,2,2,2,32,256]{6,5,4,3,2,1,0:T(8,128)(2,1)S(1)} collective-permute-done((bf16[2,2,2,2,2,32,256]{6,5,4,3,2,1,0:T(8,128)(2,1)S(1)}, bf16[2,2,2,2,2,32,256]{6,5,4,3,2,1,0:T(8,128)(2,1)S(1)}, u32[]{:S(2)}, u32[]{:S(2)}) %collective-permute-start.12) | collective-permute-done | bytes 524320 | tf_op jit(solution)/shard_map/ppermute | solution.py:38
  49.4 1.5 collective-permute-done.10.refs_1_
  50.9 2.2 copy-done
  53.1 8.7 %shard_map.76 = (bf16[256,256]{1,0:T(8,128)(2,1)S(1)}, bf16[256,256]{1,0:T(8,128)(2,1)S(1)}) custom-call(s32[4]{0:T(128)S(1)} %pad_add_fusion.pos_ref, bf16[2,2,2,2,2,48,256]{6,5,4,3,2,1,0:T(8,128)(2,1)S(1)} %pad_maximum_fusion.3.refs_0_, bf16[2,2,2,2,2,48,256]{6,5,4,3,2,1,0:T(8,128)(2,1)} %collective-permute-done.10.refs_1_, ...), custom_call_target="tpu_custom_call" | custom-call | flops 2147483648 | bytes 12582912 | tf_op jit(solution)/shard_map/pallas_call | solution.py:158
  61.8 15.4 %shard_map.77 = (bf16[2,2,2,2,2,80,256]{6,5,4,3,2,1,0:T(8,128)(2,1)S(1)}, bf16[2,2,2,2,2,80,256]{6,5,4,3,2,1,0:T(8,128)(2,1)S(1)}, bf16[2,2,2,2,2,80,256]{6,5,4,...) custom-call(s32[4]{0:T(128)S(1)} %pad_add_fusion.pos_ref, ...), custom_call_target="tpu_custom_call" | custom-call | flops 3758096384 | bytes 22020096 | tf_op jit(solution)/shard_map/pallas_call | solution.py:223
  77.2 2.1 collective-permute-start.20
  79.6 1.4 collective-permute-start.17
  81.0 11.2 %collective-permute-done.20 = bf16[2,2,2,2,2,64,256]{6,5,4,3,2,1,0:T(8,128)(2,1)S(1)} collective-permute-done((bf16[2,2,2,2,2,64,256]{6,5,4,3,2,1,0:T(8,128)(2,1)S(1)}, bf16[2,2,2,2,2,64,256]{6,5,4,3,2,1,0:T(8,128)(2,1)S(1)}, u32[]{:S(2)}, u32[]{:S(2)}) %collective-permute-start.20) | collective-permute-done | bytes 1048608 | tf_op jit(solution)/shard_map/ppermute | solution.py:38
  94.0 3.1 %collective-permute-done.14 = bf16[2,2,2,2,2,80,256]{6,5,4,3,2,1,0:T(8,128)(2,1)S(1)} collective-permute-done((bf16[2,2,2,2,2,80,256]{6,5,4,3,2,1,0:T(8,128)(2,1)S(1)}, bf16[2,2,2,2,2,80,256]{6,5,4,3,2,1,0:T(8,128)(2,1)S(1)}, u32[]{:S(2)}, u32[]{:S(2)}) %collective-permute-start.14) | collective-permute-done | bytes 1310752 | tf_op jit(solution)/shard_map/ppermute | solution.py:38
  97.5 1.5 collective-permute-start.15
  100.1 2.6 %collective-permute-done.21 = bf16[2,2,2,2,64,256]{5,4,3,2,1,0:T(8,128)(2,1)S(1)} collective-permute-done((bf16[2,2,2,2,64,256]{5,4,3,2,1,0:T(8,128)(2,1)S(1)}, bf16[2,2,2,2,64,256]{5,4,3,2,1,0:T(8,128)(2,1)S(1)}, u32[]{:S(2)}, u32[]{:S(2)}) %collective-permute-start.21) | collective-permute-done | bytes 524320 | tf_op jit(solution)/shard_map/ppermute | solution.py:38
  102.8 1.5 collective-permute-start.22
  104.3 3.9 %collective-permute-done.15 = bf16[2,2,2,2,80,256]{5,4,3,2,1,0:T(8,128)(2,1)S(1)} collective-permute-done((bf16[2,2,2,2,80,256]{5,4,3,2,1,0:T(8,128)(2,1)S(1)}, bf16[2,2,2,2,80,256]{5,4,3,2,1,0:T(8,128)(2,1)S(1)}, u32[]{:S(2)}, u32[]{:S(2)}) %collective-permute-start.15) | collective-permute-done | bytes 655392 | tf_op jit(solution)/shard_map/ppermute | solution.py:38
  111.2 4.4 %collective-permute-done.16 = bf16[2,2,2,80,256]{4,3,2,1,0:T(8,128)(2,1)S(1)} collective-permute-done((bf16[2,2,2,80,256]{4,3,2,1,0:T(8,128)(2,1)S(1)}, bf16[2,2,2,80,256]{4,3,2,1,0:T(8,128)(2,1)S(1)}, u32[]{:S(2)}, u32[]{:S(2)}) %collective-permute-start.16) | collective-permute-done | bytes 327712 | tf_op jit(solution)/shard_map/ppermute | solution.py:38
  115.7 1.8 collective-permute-done.19
  117.8 7.5 %collective-permute-done.23 = bf16[2,2,224,256]{3,2,1,0:T(8,128)(2,1)S(1)} collective-permute-done((bf16[2,2,224,256]{3,2,1,0:T(8,128)(2,1)S(1)}, bf16[2,2,224,256]{3,2,1,0:T(8,128)(2,1)S(1)}, u32[]{:S(2)}, u32[]{:S(2)}) %collective-permute-start.23) | collective-permute-done | bytes 458784 | tf_op jit(solution)/shard_map/ppermute | solution.py:38
  125.6 4.9 %collective-permute-done.24 = bf16[2,224,256]{2,1,0:T(8,128)(2,1)S(1)} collective-permute-done((bf16[2,224,256]{2,1,0:T(8,128)(2,1)S(1)}, bf16[2,224,256]{2,1,0:T(8,128)(2,1)S(1)}, u32[]{:S(2)}, u32[]{:S(2)}) %collective-permute-start.24) | collective-permute-done | bytes 229408 | tf_op jit(solution)/shard_map/ppermute | solution.py:38
  130.6 3.7 %collective-permute-done.25 = bf16[224,256]{1,0:T(8,128)(2,1)S(1)} collective-permute-done((bf16[224,256]{1,0:T(8,128)(2,1)S(1)}, bf16[224,256]{1,0:T(8,128)(2,1)S(1)}, u32[]{:S(2)}, u32[]{:S(2)}) %collective-permute-start.25) | collective-permute-done | bytes 114720 | tf_op jit(solution)/shard_map/ppermute | solution.py:38
  134.5 8.7 %collective-permute-start.27 = (bf16[224,256]{1,0:T(8,128)(2,1)S(1)}, bf16[224,256]{1,0:T(8,128)(2,1)S(1)}, u32[]{:S(2)}, u32[]{:S(2)}) collective-permute-start(bf16[224,256]{1,0:T(8,128)(2,1)S(1)} %get-tuple-element.112), channel_id=1, source_target_pairs={{0,32},{64,96},{1,33},{65,97},{2,34},{66,98},{3,35},{67,99},{4,36}... | collective-permute-start | bytes 344072 | tf_op jit(solution)/shard_map/ppermute | solution.py:38
  144.6 1.4 collective-permute-start.26
  146.1 5.4 %collective-permute-done.28 = bf16[224,512]{1,0:T(8,128)(2,1)S(1)} collective-permute-done((bf16[224,512]{1,0:T(8,128)(2,1)S(1)}, bf16[224,512]{1,0:T(8,128)(2,1)S(1)}, u32[]{:S(2)}, u32[]{:S(2)}) %collective-permute-start.28) | collective-permute-done | bytes 229408 | tf_op jit(solution)/shard_map/ppermute | solution.py:38
  151.6 1.6 collective-permute-done.26
  154.4 4.0 %collective-permute-done.29 = bf16[2,224,256]{2,1,0:T(8,128)(2,1)S(1)} collective-permute-done((bf16[2,224,256]{2,1,0:T(8,128)(2,1)S(1)}, bf16[2,224,256]{2,1,0:T(8,128)(2,1)S(1)}, u32[]{:S(2)}, u32[]{:S(2)}) %collective-permute-start.29) | collective-permute-done | bytes 229408 | tf_op jit(solution)/shard_map/ppermute | solution.py:38
  158.5 1.5 collective-permute-start.30
  160.0 6.2 %collective-permute-done.30 = bf16[2,2,224,256]{3,2,1,0:T(8,128)(2,1)S(1)} collective-permute-done((bf16[2,2,224,256]{3,2,1,0:T(8,128)(2,1)S(1)}, bf16[2,2,224,256]{3,2,1,0:T(8,128)(2,1)S(1)}, u32[]{:S(2)}, u32[]{:S(2)}) %collective-permute-start.30) | collective-permute-done | bytes 458784 | tf_op jit(solution)/shard_map/ppermute | solution.py:38
  166.2 3.0 %collective-permute-start.32 = (bf16[2,2,2,80,256]{4,3,2,1,0:T(8,128)(2,1)S(1)}, bf16[2,2,2,80,256]{4,3,2,1,0:T(8,128)(2,1)S(1)}, u32[]{:S(2)}, u32[]{:S(2)}) collective-permute-start(bf16[2,2,2,80,256]{4,3,2,1,0:T(8,128)(2,1)S(1)} %get-tuple-element.99), channel_id=1, source_target_pairs={{0,2},{64,66},{1,3},{65,67},{2,0},{66,64},{3,1},{67,65},{4,6},{68,... | collective-permute-start | bytes 983048 | tf_op jit(solution)/shard_map/ppermute | solution.py:38
  169.3 3.0 %collective-permute-start.31 = (bf16[2,2,2,80,256]{4,3,2,1,0:T(8,128)(2,1)S(1)}, bf16[2,2,2,80,256]{4,3,2,1,0:T(8,128)(2,1)S(1)}, u32[]{:S(2)}, u32[]{:S(2)}) collective-permute-start(bf16[2,2,2,80,256]{4,3,2,1,0:T(8,128)(2,1)S(1)} %get-tuple-element.97), channel_id=1, source_target_pairs={{0,64},{64,0},{1,65},{65,1},{2,66},{66,2},{3,67},{67,3},{4,68},{68... | collective-permute-start | bytes 983048 | tf_op jit(solution)/shard_map/ppermute | solution.py:38
  172.2 3.0 %collective-permute-start.33 = (bf16[2,2,2,64,256]{4,3,2,1,0:T(8,128)(2,1)S(1)}, bf16[2,2,2,64,256]{4,3,2,1,0:T(8,128)(2,1)S(1)}, u32[]{:S(2)}, u32[]{:S(2)}) collective-permute-start(bf16[2,2,2,64,256]{4,3,2,1,0:T(8,128)(2,1)S(1)} %pad_maximum_fusion.14), channel_id=1, source_target_pairs={{0,8},{64,72},{1,9},{65,73},{2,10},{66,74},{3,11},{67,75},{4,12},{... | collective-permute-start | bytes 786440 | tf_op jit(solution)/shard_map/ppermute | solution.py:38
  175.3 3.8 %collective-permute-done.33 = bf16[2,2,2,64,256]{4,3,2,1,0:T(8,128)(2,1)S(1)} collective-permute-done((bf16[2,2,2,64,256]{4,3,2,1,0:T(8,128)(2,1)S(1)}, bf16[2,2,2,64,256]{4,3,2,1,0:T(8,128)(2,1)S(1)}, u32[]{:S(2)}, u32[]{:S(2)}) %collective-permute-start.33) | collective-permute-done | bytes 262176 | tf_op jit(solution)/shard_map/ppermute | solution.py:38
  179.6 3.0 %collective-permute-start.34 = (bf16[2,2,2,2,80,256]{5,4,3,2,1,0:T(8,128)(2,1)S(1)}, bf16[2,2,2,2,80,256]{5,4,3,2,1,0:T(8,128)(2,1)S(1)}, u32[]{:S(2)}, u32[]{:S(2)}) collective-permute-start(bf16[2,2,2,2,80,256]{5,4,3,2,1,0:T(8,128)(2,1)S(1)} %pad_maximum_fusion.5), channel_id=1, source_target_pairs={{0,8},{64,72},{1,9},{65,73},{2,10},{66,74},{3,11},{67,75},{4,12},{... | collective-permute-start | bytes 1966088 | tf_op jit(solution)/shard_map/ppermute | solution.py:38
  182.8 9.1 %collective-permute-done.36 = bf16[2,2,2,2,64,256]{5,4,3,2,1,0:T(8,128)(2,1)S(1)} collective-permute-done((bf16[2,2,2,2,64,256]{5,4,3,2,1,0:T(8,128)(2,1)S(1)}, bf16[2,2,2,2,64,256]{5,4,3,2,1,0:T(8,128)(2,1)S(1)}, u32[]{:S(2)}, u32[]{:S(2)}) %collective-permute-start.36) | collective-permute-done | bytes 524320 | tf_op jit(solution)/shard_map/ppermute | solution.py:38
  193.9 2.7 %collective-permute-start.39 = (bf16[2,2,2,2,2,64,256]{6,5,4,3,2,1,0:T(8,128)(2,1)S(1)}, bf16[2,2,2,2,2,64,256]{6,5,4,3,2,1,0:T(8,128)(2,1)S(1)}, u32[]{:S(2)}, u32[]{:S(2)}) collective-permute-start(bf16[2,2,2,2,2,64,256]{6,5,4,3,2,1,0:T(8,128)(2,1)S(1)} %pad_maximum_fusion.2.refs_4_), channel_id=1, source_target_pairs={{0,64},{64,0},{1,65},{65,1},{2,66},{66,2},{3,67},{67,3},{4,68},{68... | collective-permute-start | bytes 3145736 | tf_op jit(solution)/shard_map/ppermute | solution.py:38
  197.1 12.7 %collective-permute-done.38.refs_3_ = bf16[2,2,2,2,2,80,256]{6,5,4,3,2,1,0:T(8,128)(2,1)S(1)} collective-permute-done((bf16[2,2,2,2,2,80,256]{6,5,4,3,2,1,0:T(8,128)(2,1)S(1)}, bf16[2,2,2,2,2,80,256]{6,5,4,3,2,1,0:T(8,128)(2,1)S(1)}, u32[]{:S(2)}, u32[]{:S(2)}) %collective-permute-start.38) | collective-permute-done | bytes 1310752 | tf_op jit(solution)/shard_map/ppermute | solution.py:38
  209.9 1.5 collective-permute-done.37.refs_1_
  211.9 1.6 fusion.1
  213.5 2.8 %collective-permute-done.45.refs_11_ = bf16[2,2,2,2,2,64,256]{6,5,4,3,2,1,0:T(8,128)(2,1)S(1)} collective-permute-done((bf16[2,2,2,2,2,64,256]{6,5,4,3,2,1,0:T(8,128)(2,1)S(1)}, bf16[2,2,2,2,2,64,256]{6,5,4,3,2,1,0:T(8,128)(2,1)S(1)}, u32[]{:S(2)}, u32[]{:S(2)}) %collective-permute-start.45) | collective-permute-done | bytes 1048608 | tf_op jit(solution)/shard_map/ppermute | solution.py:38
  217.4 13.3 %shard_map.78 = bf16[256,14336]{1,0:T(8,128)(2,1)} custom-call(s32[4]{0:T(128)S(1)} %pad_add_fusion.pos_ref, bf16[2,2,2,2,2,80,256]{6,5,4,3,2,1,0:T(8,128)(2,1)S(1)} %pad_maximum_fusion.refs_0_, bf16[2,2,2,2,2,80,256]{6,5,4,3,2,1,0:T(8,128)(2,1)S(1)} %collective-permute-done.37.refs_1_, bf16[2,2,2,2,2,80,256]{6,5,4,3,2,1,0:T(8,128)(2,1)S(1)} %pad_maximum_fusion.1.refs_2_, ...), custom_call_target="tpu_custom_call" | custom-call | flops 3758096384 | bytes 22020096 | tf_op jit(solution)/shard_map/pallas_call | solution.py:276
  (98 shorter events, 25.2 us)
Async XLA Ops:
  0.6 61.2 %collective-permute-start.9 = (bf16[256,14336]{1,0:T(8,128)(2,1)}, bf16[256,14336]{1,0:T(8,128)(2,1)}, u32[]{:S(2)}, u32[]{:S(2)}) collective-permute-start(bf16[256,14336]{1,0:T(8,128)(2,1)} %g0_ref.1), channel_id=1, source_target_pairs={{0,32},{64,96},{1,33},{65,97},{2,34},{66,98},{3,35},{67,99},{4,36}... | collective-permute-start | bytes 22020104 | tf_op jit(solution)/shard_map/ppermute | solution.py:38
  2.1 48.8 %collective-permute-start.13 = (bf16[256,8192]{1,0:T(8,128)(2,1)}, bf16[256,8192]{1,0:T(8,128)(2,1)}, u32[]{:S(2)}, u32[]{:S(2)}) collective-permute-start(bf16[256,8192]{1,0:T(8,128)(2,1)} %refs_6_.1), channel_id=1, source_target_pairs={{0,32},{64,96},{1,33},{65,97},{2,34},{66,98},{3,35},{67,99},{4,36}... | collective-permute-start | bytes 12582920 | tf_op jit(solution)/shard_map/ppermute | solution.py:38
  3.1 3.4 %collective-permute-start = (bf16[128,256]{1,0:T(8,128)(2,1)S(1)}, bf16[128,256]{1,0:T(8,128)(2,1)S(1)}, u32[]{:S(2)}, u32[]{:S(2)}) collective-permute-start(bf16[128,256]{1,0:T(8,128)(2,1)S(1)} %dynamic_slice.9), channel_id=1, source_target_pairs={{0,65},{64,1},{1,64},{65,0},{2,67},{66,3},{3,66},{67,2},{4,69},{68... | collective-permute-start | bytes 196616 | tf_op jit(solution)/shard_map/ppermute | solution.py:38
  6.5 3.9 %collective-permute-start.1 = (bf16[2,128,256]{2,1,0:T(8,128)(2,1)S(1)}, bf16[2,128,256]{2,1,0:T(8,128)(2,1)S(1)}, u32[]{:S(2)}, u32[]{:S(2)}) collective-permute-start(bf16[2,128,256]{2,1,0:T(8,128)(2,1)S(1)} %pad_maximum_fusion.20), channel_id=1, source_target_pairs={{0,6},{64,70},{1,7},{65,71},{2,4},{66,68},{3,5},{67,69},{4,2},{68,... | collective-permute-start | bytes 393224 | tf_op jit(solution)/shard_map/ppermute | solution.py:38
  10.4 5.3 %collective-permute-start.2 = (bf16[2,2,128,256]{3,2,1,0:T(8,128)(2,1)S(1)}, bf16[2,2,128,256]{3,2,1,0:T(8,128)(2,1)S(1)}, u32[]{:S(2)}, u32[]{:S(2)}) collective-permute-start(bf16[2,2,128,256]{3,2,1,0:T(8,128)(2,1)S(1)} %pad_maximum_fusion.15), channel_id=1, source_target_pairs={{0,24},{64,88},{1,25},{65,89},{2,26},{66,90},{3,27},{67,91},{4,28}... | collective-permute-start | bytes 786440 | tf_op jit(solution)/shard_map/ppermute | solution.py:38
  15.8 11.3 %collective-permute-start.4 = (bf16[2,2,2,48,256]{4,3,2,1,0:T(8,128)(2,1)S(1)}, bf16[2,2,2,48,256]{4,3,2,1,0:T(8,128)(2,1)S(1)}, u32[]{:S(2)}, u32[]{:S(2)}) collective-permute-start(bf16[2,2,2,48,256]{4,3,2,1,0:T(8,128)(2,1)S(1)} %get-tuple-element.68), channel_id=1, source_target_pairs={{0,2},{64,66},{1,3},{65,67},{2,0},{66,64},{3,1},{67,65},{4,6},{68,... | collective-permute-start | bytes 589832 | tf_op jit(solution)/shard_map/ppermute | solution.py:38
  18.3 8.7 %collective-permute-start.3 = (bf16[2,2,2,48,256]{4,3,2,1,0:T(8,128)(2,1)S(1)}, bf16[2,2,2,48,256]{4,3,2,1,0:T(8,128)(2,1)S(1)}, u32[]{:S(2)}, u32[]{:S(2)}) collective-permute-start(bf16[2,2,2,48,256]{4,3,2,1,0:T(8,128)(2,1)S(1)} %get-tuple-element.66), channel_id=1, source_target_pairs={{0,64},{64,0},{1,65},{65,1},{2,66},{66,2},{3,67},{67,3},{4,68},{68... | collective-permute-start | bytes 589832 | tf_op jit(solution)/shard_map/ppermute | solution.py:38
  21.9 5.2 %collective-permute-start.5 = (bf16[2,2,2,32,256]{4,3,2,1,0:T(8,128)(2,1)S(1)}, bf16[2,2,2,32,256]{4,3,2,1,0:T(8,128)(2,1)S(1)}, u32[]{:S(2)}, u32[]{:S(2)}) collective-permute-start(bf16[2,2,2,32,256]{4,3,2,1,0:T(8,128)(2,1)S(1)} %pad_maximum_fusion.19), channel_id=1, source_target_pairs={{0,8},{64,72},{1,9},{65,73},{2,10},{66,74},{3,11},{67,75},{4,12},{... | collective-permute-start | bytes 393224 | tf_op jit(solution)/shard_map/ppermute | solution.py:38
  27.1 10.0 %collective-permute-start.7 = (bf16[2,2,2,2,48,256]{5,4,3,2,1,0:T(8,128)(2,1)S(1)}, bf16[2,2,2,2,48,256]{5,4,3,2,1,0:T(8,128)(2,1)S(1)}, u32[]{:S(2)}, u32[]{:S(2)}) collective-permute-start(bf16[2,2,2,2,48,256]{5,4,3,2,1,0:T(8,128)(2,1)S(1)} %pad_maximum_fusion.13), channel_id=1, source_target_pairs={{0,64},{64,0},{1,65},{65,1},{2,66},{66,2},{3,67},{67,3},{4,68},{68... | collective-permute-start | bytes 1179656 | tf_op jit(solution)/shard_map/ppermute | solution.py:38
  27.8 9.4 %collective-permute-start.6 = (bf16[2,2,2,2,48,256]{5,4,3,2,1,0:T(8,128)(2,1)S(1)}, bf16[2,2,2,2,48,256]{5,4,3,2,1,0:T(8,128)(2,1)S(1)}, u32[]{:S(2)}, u32[]{:S(2)}) collective-permute-start(bf16[2,2,2,2,48,256]{5,4,3,2,1,0:T(8,128)(2,1)S(1)} %pad_maximum_fusion.12), channel_id=1, source_target_pairs={{0,8},{64,72},{1,9},{65,73},{2,10},{66,74},{3,11},{67,75},{4,12},{... | collective-permute-start | bytes 1179656 | tf_op jit(solution)/shard_map/ppermute | solution.py:38
  30.6 6.5 %collective-permute-start.8 = (bf16[2,2,2,2,32,256]{5,4,3,2,1,0:T(8,128)(2,1)S(1)}, bf16[2,2,2,2,32,256]{5,4,3,2,1,0:T(8,128)(2,1)S(1)}, u32[]{:S(2)}, u32[]{:S(2)}) collective-permute-start(bf16[2,2,2,2,32,256]{5,4,3,2,1,0:T(8,128)(2,1)S(1)} %pad_maximum_fusion.16), channel_id=1, source_target_pairs={{0,2},{64,66},{1,3},{65,67},{2,0},{66,64},{3,1},{67,65},{4,6},{68,... | collective-permute-start | bytes 786440 | tf_op jit(solution)/shard_map/ppermute | solution.py:38
  37.2 12.2 %collective-permute-start.11 = (bf16[2,2,2,2,2,48,256]{6,5,4,3,2,1,0:T(8,128)(2,1)S(1)}, bf16[2,2,2,2,2,48,256]{6,5,4,3,2,1,0:T(8,128)(2,1)S(1)}, u32[]{:S(2)}, u32[]{:S(2)}) collective-permute-start(bf16[2,2,2,2,2,48,256]{6,5,4,3,2,1,0:T(8,128)(2,1)S(1)} %pad_maximum_fusion.4.refs_2_), channel_id=1, source_target_pairs={{0,8},{64,72},{1,9},{65,73},{2,10},{66,74},{3,11},{67,75},{4,12},{... | collective-permute-start | bytes 2359304 | tf_op jit(solution)/shard_map/ppermute | solution.py:38
  38.7 12.2 %collective-permute-start.10 = (bf16[2,2,2,2,2,48,256]{6,5,4,3,2,1,0:T(8,128)(2,1)S(1)}, bf16[2,2,2,2,2,48,256]{6,5,4,3,2,1,0:T(8,128)(2,1)}, u32[]{:S(2)}, u32[]{:S(2)}) collective-permute-start(bf16[2,2,2,2,2,48,256]{6,5,4,3,2,1,0:T(8,128)(2,1)S(1)} %pad_maximum_fusion.3.refs_0_), channel_id=1, source_target_pairs={{0,2},{64,66},{1,3},{65,67},{2,0},{66,64},{3,1},{67,65},{4,6},{68,... | collective-permute-start | bytes 2359304 | tf_op jit(solution)/shard_map/ppermute | solution.py:38
  40.1 9.3 %collective-permute-start.12 = (bf16[2,2,2,2,2,32,256]{6,5,4,3,2,1,0:T(8,128)(2,1)S(1)}, bf16[2,2,2,2,2,32,256]{6,5,4,3,2,1,0:T(8,128)(2,1)S(1)}, u32[]{:S(2)}, u32[]{:S(2)}) collective-permute-start(bf16[2,2,2,2,2,32,256]{6,5,4,3,2,1,0:T(8,128)(2,1)S(1)} %pad_maximum_fusion.7.refs_4_), channel_id=1, source_target_pairs={{0,64},{64,0},{1,65},{65,1},{2,66},{66,2},{3,67},{67,3},{4,68},{68... | collective-permute-start | bytes 1572872 | tf_op jit(solution)/shard_map/ppermute | solution.py:38
  77.2 14.9 %collective-permute-start.20 = (bf16[2,2,2,2,2,64,256]{6,5,4,3,2,1,0:T(8,128)(2,1)S(1)}, bf16[2,2,2,2,2,64,256]{6,5,4,3,2,1,0:T(8,128)(2,1)S(1)}, u32[]{:S(2)}, u32[]{:S(2)}) collective-permute-start(bf16[2,2,2,2,2,64,256]{6,5,4,3,2,1,0:T(8,128)(2,1)S(1)} %get-tuple-element.87), channel_id=1, source_target_pairs={{0,64},{64,0},{1,65},{65,1},{2,66},{66,2},{3,67},{67,3},{4,68},{68... | collective-permute-start | bytes 3145736 | tf_op jit(solution)/shard_map/ppermute | solution.py:38
  79.4 17.7 %collective-permute-start.14 = (bf16[2,2,2,2,2,80,256]{6,5,4,3,2,1,0:T(8,128)(2,1)S(1)}, bf16[2,2,2,2,2,80,256]{6,5,4,3,2,1,0:T(8,128)(2,1)S(1)}, u32[]{:S(2)}, u32[]{:S(2)}) collective-permute-start(bf16[2,2,2,2,2,80,256]{6,5,4,3,2,1,0:T(8,128)(2,1)S(1)} %get-tuple-element.83), channel_id=1, source_target_pairs={{0,2},{64,66},{1,3},{65,67},{2,0},{66,64},{3,1},{67,65},{4,6},{68,... | collective-permute-start | bytes 3932168 | tf_op jit(solution)/shard_map/ppermute | solution.py:38
  79.6 19.4 %collective-permute-start.17 = (bf16[2,2,2,2,2,80,256]{6,5,4,3,2,1,0:T(8,128)(2,1)S(1)}, bf16[2,2,2,2,2,80,256]{6,5,4,3,2,1,0:T(8,128)(2,1)S(1)}, u32[]{:S(2)}, u32[]{:S(2)}) collective-permute-start(bf16[2,2,2,2,2,80,256]{6,5,4,3,2,1,0:T(8,128)(2,1)S(1)} %get-tuple-element.85), channel_id=1, source_target_pairs={{0,8},{64,72},{1,9},{65,73},{2,10},{66,74},{3,11},{67,75},{4,12},{... | collective-permute-start | bytes 3932168 | tf_op jit(solution)/shard_map/ppermute | solution.py:38
  92.6 10.1 %collective-permute-start.21 = (bf16[2,2,2,2,64,256]{5,4,3,2,1,0:T(8,128)(2,1)S(1)}, bf16[2,2,2,2,64,256]{5,4,3,2,1,0:T(8,128)(2,1)S(1)}, u32[]{:S(2)}, u32[]{:S(2)}) collective-permute-start(bf16[2,2,2,2,64,256]{5,4,3,2,1,0:T(8,128)(2,1)S(1)} %get-tuple-element.118), channel_id=1, source_target_pairs={{0,2},{64,66},{1,3},{65,67},{2,0},{66,64},{3,1},{67,65},{4,6},{68,... | collective-permute-start | bytes 1572872 | tf_op jit(solution)/shard_map/ppermute | solution.py:38
  97.5 10.7 %collective-permute-start.15 = (bf16[2,2,2,2,80,256]{5,4,3,2,1,0:T(8,128)(2,1)S(1)}, bf16[2,2,2,2,80,256]{5,4,3,2,1,0:T(8,128)(2,1)S(1)}, u32[]{:S(2)}, u32[]{:S(2)}) collective-permute-start(bf16[2,2,2,2,80,256]{5,4,3,2,1,0:T(8,128)(2,1)S(1)} %get-tuple-element.114), channel_id=1, source_target_pairs={{0,8},{64,72},{1,9},{65,73},{2,10},{66,74},{3,11},{67,75},{4,12},{... | collective-permute-start | bytes 1966088 | tf_op jit(solution)/shard_map/ppermute | solution.py:38
  99.4 10.7 %collective-permute-start.18 = (bf16[2,2,2,2,80,256]{5,4,3,2,1,0:T(8,128)(2,1)S(1)}, bf16[2,2,2,2,80,256]{5,4,3,2,1,0:T(8,128)(2,1)S(1)}, u32[]{:S(2)}, u32[]{:S(2)}) collective-permute-start(bf16[2,2,2,2,80,256]{5,4,3,2,1,0:T(8,128)(2,1)S(1)} %get-tuple-element.116), channel_id=1, source_target_pairs={{0,64},{64,0},{1,65},{65,1},{2,66},{66,2},{3,67},{67,3},{4,68},{68... | collective-permute-start | bytes 1966088 | tf_op jit(solution)/shard_map/ppermute | solution.py:38
  102.8 8.3 %collective-permute-start.22 = (bf16[2,2,2,64,256]{4,3,2,1,0:T(8,128)(2,1)S(1)}, bf16[2,2,2,64,256]{4,3,2,1,0:T(8,128)(2,1)S(1)}, u32[]{:S(2)}, u32[]{:S(2)}) collective-permute-start(bf16[2,2,2,64,256]{4,3,2,1,0:T(8,128)(2,1)S(1)} %get-tuple-element.124), channel_id=1, source_target_pairs={{0,8},{64,72},{1,9},{65,73},{2,10},{66,74},{3,11},{67,75},{4,12},{... | collective-permute-start | bytes 786440 | tf_op jit(solution)/shard_map/ppermute | solution.py:38
  108.4 7.2 %collective-permute-start.16 = (bf16[2,2,2,80,256]{4,3,2,1,0:T(8,128)(2,1)S(1)}, bf16[2,2,2,80,256]{4,3,2,1,0:T(8,128)(2,1)S(1)}, u32[]{:S(2)}, u32[]{:S(2)}) collective-permute-start(bf16[2,2,2,80,256]{4,3,2,1,0:T(8,128)(2,1)S(1)} %get-tuple-element.120), channel_id=1, source_target_pairs={{0,64},{64,0},{1,65},{65,1},{2,66},{66,2},{3,67},{67,3},{4,68},{68... | collective-permute-start | bytes 983048 | tf_op jit(solution)/shard_map/ppermute | solution.py:38
  110.3 7.2 %collective-permute-start.19 = (bf16[2,2,2,80,256]{4,3,2,1,0:T(8,128)(2,1)S(1)}, bf16[2,2,2,80,256]{4,3,2,1,0:T(8,128)(2,1)S(1)}, u32[]{:S(2)}, u32[]{:S(2)}) collective-permute-start(bf16[2,2,2,80,256]{4,3,2,1,0:T(8,128)(2,1)S(1)} %get-tuple-element.122), channel_id=1, source_target_pairs={{0,2},{64,66},{1,3},{65,67},{2,0},{66,64},{3,1},{67,65},{4,6},{68,... | collective-permute-start | bytes 983048 | tf_op jit(solution)/shard_map/ppermute | solution.py:38
  117.7 7.7 %collective-permute-start.23 = (bf16[2,2,224,256]{3,2,1,0:T(8,128)(2,1)S(1)}, bf16[2,2,224,256]{3,2,1,0:T(8,128)(2,1)S(1)}, u32[]{:S(2)}, u32[]{:S(2)}) collective-permute-start(bf16[2,2,224,256]{3,2,1,0:T(8,128)(2,1)S(1)} %pad_maximum_fusion.10), channel_id=1, source_target_pairs={{0,24},{64,88},{1,25},{65,89},{2,26},{66,90},{3,27},{67,91},{4,28}... | collective-permute-start | bytes 1376264 | tf_op jit(solution)/shard_map/ppermute | solution.py:38
  117.8 16.5 %copy-start.1 = (f32[448,512]{1,0:T(8,128)S(1)}, f32[448,512]{1,0:T(8,128)}, u32[]{:S(2)}) copy-start(f32[448,512]{1,0:T(8,128)} %param.9) | copy-start | bytes 2752516
  125.5 5.0 %collective-permute-start.24 = (bf16[2,224,256]{2,1,0:T(8,128)(2,1)S(1)}, bf16[2,224,256]{2,1,0:T(8,128)(2,1)S(1)}, u32[]{:S(2)}, u32[]{:S(2)}) collective-permute-start(bf16[2,224,256]{2,1,0:T(8,128)(2,1)S(1)} %get-tuple-element.128), channel_id=1, source_target_pairs={{0,6},{64,70},{1,7},{65,71},{2,4},{66,68},{3,5},{67,69},{4,2},{68,... | collective-permute-start | bytes 688136 | tf_op jit(solution)/shard_map/ppermute | solution.py:38
  130.5 3.8 %collective-permute-start.25 = (bf16[224,256]{1,0:T(8,128)(2,1)S(1)}, bf16[224,256]{1,0:T(8,128)(2,1)S(1)}, u32[]{:S(2)}, u32[]{:S(2)}) collective-permute-start(bf16[224,256]{1,0:T(8,128)(2,1)S(1)} %fusion.43), channel_id=1, source_target_pairs={{0,65},{64,1},{1,64},{65,0},{2,67},{66,3},{3,66},{67,2},{4,69},{68... | collective-permute-start | bytes 344072 | tf_op jit(solution)/shard_map/ppermute | solution.py:38
  134.5 9.7 %collective-permute-start.27 = (bf16[224,256]{1,0:T(8,128)(2,1)S(1)}, bf16[224,256]{1,0:T(8,128)(2,1)S(1)}, u32[]{:S(2)}, u32[]{:S(2)}) collective-permute-start(bf16[224,256]{1,0:T(8,128)(2,1)S(1)} %get-tuple-element.112), channel_id=1, source_target_pairs={{0,32},{64,96},{1,33},{65,97},{2,34},{66,98},{3,35},{67,99},{4,36}... | collective-permute-start | bytes 344072 | tf_op jit(solution)/shard_map/ppermute | solution.py:38
  144.3 7.1 %collective-permute-start.28 = (bf16[224,512]{1,0:T(8,128)(2,1)S(1)}, bf16[224,512]{1,0:T(8,128)(2,1)S(1)}, u32[]{:S(2)}, u32[]{:S(2)}) collective-permute-start(bf16[224,512]{1,0:T(8,128)(2,1)S(1)} %maximum_select_fusion.1), channel_id=1, source_target_pairs={{0,64},{64,0},{1,65},{65,1},{2,66},{66,2},{3,67},{67,3},{4,68},{68... | collective-permute-start | bytes 688136 | tf_op jit(solution)/shard_map/ppermute | solution.py:38
  144.6 8.5 %collective-permute-start.26 = (bf16[224,256]{1,0:T(8,128)(2,1)S(1)}, bf16[224,256]{1,0:T(8,128)(2,1)S(1)}, u32[]{:S(2)}, u32[]{:S(2)}) collective-permute-start(bf16[224,256]{1,0:T(8,128)(2,1)S(1)} %get-tuple-element.88), channel_id=1, source_target_pairs={{0,65},{64,1},{1,64},{65,0},{2,67},{66,3},{3,66},{67,2},{4,69},{68... | collective-permute-start | bytes 344072 | tf_op jit(solution)/shard_map/ppermute | solution.py:38
  153.2 5.2 %collective-permute-start.29 = (bf16[2,224,256]{2,1,0:T(8,128)(2,1)S(1)}, bf16[2,224,256]{2,1,0:T(8,128)(2,1)S(1)}, u32[]{:S(2)}, u32[]{:S(2)}) collective-permute-start(bf16[2,224,256]{2,1,0:T(8,128)(2,1)S(1)} %pad_maximum_fusion.18), channel_id=1, source_target_pairs={{0,6},{64,70},{1,7},{65,71},{2,4},{66,68},{3,5},{67,69},{4,2},{68,... | collective-permute-start | bytes 688136 | tf_op jit(solution)/shard_map/ppermute | solution.py:38
  158.5 7.7 %collective-permute-start.30 = (bf16[2,2,224,256]{3,2,1,0:T(8,128)(2,1)S(1)}, bf16[2,2,224,256]{3,2,1,0:T(8,128)(2,1)S(1)}, u32[]{:S(2)}, u32[]{:S(2)}) collective-permute-start(bf16[2,2,224,256]{3,2,1,0:T(8,128)(2,1)S(1)} %pad_maximum_fusion.11), channel_id=1, source_target_pairs={{0,24},{64,88},{1,25},{65,89},{2,26},{66,90},{3,27},{67,91},{4,28}... | collective-permute-start | bytes 1376264 | tf_op jit(solution)/shard_map/ppermute | solution.py:38
  166.2 12.8 %collective-permute-start.32 = (bf16[2,2,2,80,256]{4,3,2,1,0:T(8,128)(2,1)S(1)}, bf16[2,2,2,80,256]{4,3,2,1,0:T(8,128)(2,1)S(1)}, u32[]{:S(2)}, u32[]{:S(2)}) collective-permute-start(bf16[2,2,2,80,256]{4,3,2,1,0:T(8,128)(2,1)S(1)} %get-tuple-element.99), channel_id=1, source_target_pairs={{0,2},{64,66},{1,3},{65,67},{2,0},{66,64},{3,1},{67,65},{4,6},{68,... | collective-permute-start | bytes 983048 | tf_op jit(solution)/shard_map/ppermute | solution.py:38
  169.3 9.8 %collective-permute-start.31 = (bf16[2,2,2,80,256]{4,3,2,1,0:T(8,128)(2,1)S(1)}, bf16[2,2,2,80,256]{4,3,2,1,0:T(8,128)(2,1)S(1)}, u32[]{:S(2)}, u32[]{:S(2)}) collective-permute-start(bf16[2,2,2,80,256]{4,3,2,1,0:T(8,128)(2,1)S(1)} %get-tuple-element.97), channel_id=1, source_target_pairs={{0,64},{64,0},{1,65},{65,1},{2,66},{66,2},{3,67},{67,3},{4,68},{68... | collective-permute-start | bytes 983048 | tf_op jit(solution)/shard_map/ppermute | solution.py:38
  172.2 6.8 %collective-permute-start.33 = (bf16[2,2,2,64,256]{4,3,2,1,0:T(8,128)(2,1)S(1)}, bf16[2,2,2,64,256]{4,3,2,1,0:T(8,128)(2,1)S(1)}, u32[]{:S(2)}, u32[]{:S(2)}) collective-permute-start(bf16[2,2,2,64,256]{4,3,2,1,0:T(8,128)(2,1)S(1)} %pad_maximum_fusion.14), channel_id=1, source_target_pairs={{0,8},{64,72},{1,9},{65,73},{2,10},{66,74},{3,11},{67,75},{4,12},{... | collective-permute-start | bytes 786440 | tf_op jit(solution)/shard_map/ppermute | solution.py:38
  179.1 12.9 %collective-permute-start.35 = (bf16[2,2,2,2,80,256]{5,4,3,2,1,0:T(8,128)(2,1)S(1)}, bf16[2,2,2,2,80,256]{5,4,3,2,1,0:T(8,128)(2,1)S(1)}, u32[]{:S(2)}, u32[]{:S(2)}) collective-permute-start(bf16[2,2,2,2,80,256]{5,4,3,2,1,0:T(8,128)(2,1)S(1)} %pad_maximum_fusion.6), channel_id=1, source_target_pairs={{0,64},{64,0},{1,65},{65,1},{2,66},{66,2},{3,67},{67,3},{4,68},{68... | collective-permute-start | bytes 1966088 | tf_op jit(solution)/shard_map/ppermute | solution.py:38
  179.6 12.4 %collective-permute-start.34 = (bf16[2,2,2,2,80,256]{5,4,3,2,1,0:T(8,128)(2,1)S(1)}, bf16[2,2,2,2,80,256]{5,4,3,2,1,0:T(8,128)(2,1)S(1)}, u32[]{:S(2)}, u32[]{:S(2)}) collective-permute-start(bf16[2,2,2,2,80,256]{5,4,3,2,1,0:T(8,128)(2,1)S(1)} %pad_maximum_fusion.5), channel_id=1, source_target_pairs={{0,8},{64,72},{1,9},{65,73},{2,10},{66,74},{3,11},{67,75},{4,12},{... | collective-permute-start | bytes 1966088 | tf_op jit(solution)/shard_map/ppermute | solution.py:38
  182.6 9.3 %collective-permute-start.36 = (bf16[2,2,2,2,64,256]{5,4,3,2,1,0:T(8,128)(2,1)S(1)}, bf16[2,2,2,2,64,256]{5,4,3,2,1,0:T(8,128)(2,1)S(1)}, u32[]{:S(2)}, u32[]{:S(2)}) collective-permute-start(bf16[2,2,2,2,64,256]{5,4,3,2,1,0:T(8,128)(2,1)S(1)} %pad_maximum_fusion.8), channel_id=1, source_target_pairs={{0,2},{64,66},{1,3},{65,67},{2,0},{66,64},{3,1},{67,65},{4,6},{68,... | collective-permute-start | bytes 1572872 | tf_op jit(solution)/shard_map/ppermute | solution.py:38
  192.1 17.7 %collective-permute-start.38 = (bf16[2,2,2,2,2,80,256]{6,5,4,3,2,1,0:T(8,128)(2,1)S(1)}, bf16[2,2,2,2,2,80,256]{6,5,4,3,2,1,0:T(8,128)(2,1)S(1)}, u32[]{:S(2)}, u32[]{:S(2)}) collective-permute-start(bf16[2,2,2,2,2,80,256]{6,5,4,3,2,1,0:T(8,128)(2,1)S(1)} %pad_maximum_fusion.1.refs_2_), channel_id=1, source_target_pairs={{0,8},{64,72},{1,9},{65,73},{2,10},{66,74},{3,11},{67,75},{4,12},{... | collective-permute-start | bytes 3932168 | tf_op jit(solution)/shard_map/ppermute | solution.py:38
  193.6 18.3 %copy-start.4 = (bf16[256,512]{1,0:T(8,128)(2,1)S(1)}, bf16[256,512]{1,0:T(8,128)(2,1)}, u32[]{:S(2)}) copy-start(bf16[256,512]{1,0:T(8,128)(2,1)} %param.7) | copy-start | bytes 786436
  193.6 17.7 %collective-permute-start.37 = (bf16[2,2,2,2,2,80,256]{6,5,4,3,2,1,0:T(8,128)(2,1)S(1)}, bf16[2,2,2,2,2,80,256]{6,5,4,3,2,1,0:T(8,128)(2,1)S(1)}, u32[]{:S(2)}, u32[]{:S(2)}) collective-permute-start(bf16[2,2,2,2,2,80,256]{6,5,4,3,2,1,0:T(8,128)(2,1)S(1)} %pad_maximum_fusion.refs_0_), channel_id=1, source_target_pairs={{0,2},{64,66},{1,3},{65,67},{2,0},{66,64},{3,1},{67,65},{4,6},{68,... | collective-permute-start | bytes 3932168 | tf_op jit(solution)/shard_map/ppermute | solution.py:38
  193.9 2.8 %collective-permute-start.44 = (bf16[2,2,2,2,2,64,256]{6,5,4,3,2,1,0:T(8,128)(2,1)S(1)}, bf16[2,2,2,2,2,64,256]{6,5,4,3,2,1,0:T(8,128)(2,1)S(1)}, u32[]{:S(2)}, u32[]{:S(2)}) collective-permute-start(bf16[2,2,2,2,2,64,256]{6,5,4,3,2,1,0:T(8,128)(2,1)S(1)} %pad_maximum_fusion.2.refs_4_), channel_id=1, source_target_pairs={{0,32},{64,96},{1,33},{65,97},{2,34},{66,98},{3,35},{67,99},{4,36}... | collective-permute-start | bytes 3145736 | tf_op jit(solution)/shard_map/ppermute | solution.py:38
  193.9 17.4 %collective-permute-start.39 = (bf16[2,2,2,2,2,64,256]{6,5,4,3,2,1,0:T(8,128)(2,1)S(1)}, bf16[2,2,2,2,2,64,256]{6,5,4,3,2,1,0:T(8,128)(2,1)S(1)}, u32[]{:S(2)}, u32[]{:S(2)}) collective-permute-start(bf16[2,2,2,2,2,64,256]{6,5,4,3,2,1,0:T(8,128)(2,1)S(1)} %pad_maximum_fusion.2.refs_4_), channel_id=1, source_target_pairs={{0,64},{64,0},{1,65},{65,1},{2,66},{66,2},{3,67},{67,3},{4,68},{68... | collective-permute-start | bytes 3145736 | tf_op jit(solution)/shard_map/ppermute | solution.py:38
  196.6 16.9 %collective-permute-start.42 = (bf16[2,2,2,2,2,80,256]{6,5,4,3,2,1,0:T(8,128)(2,1)S(1)}, bf16[2,2,2,2,2,80,256]{6,5,4,3,2,1,0:T(8,128)(2,1)S(1)}, u32[]{:S(2)}, u32[]{:S(2)}) collective-permute-start(bf16[2,2,2,2,2,80,256]{6,5,4,3,2,1,0:T(8,128)(2,1)S(1)} %pad_maximum_fusion.1.refs_2_), channel_id=1, source_target_pairs={{0,32},{64,96},{1,33},{65,97},{2,34},{66,98},{3,35},{67,99},{4,36}... | collective-permute-start | bytes 3932168 | tf_op jit(solution)/shard_map/ppermute | solution.py:38
  196.6 16.9 %collective-permute-start.40 = (bf16[2,2,2,2,2,80,256]{6,5,4,3,2,1,0:T(8,128)(2,1)S(1)}, bf16[2,2,2,2,2,80,256]{6,5,4,3,2,1,0:T(8,128)(2,1)S(1)}, u32[]{:S(2)}, u32[]{:S(2)}) collective-permute-start(bf16[2,2,2,2,2,80,256]{6,5,4,3,2,1,0:T(8,128)(2,1)S(1)} %pad_maximum_fusion.refs_0_), channel_id=1, source_target_pairs={{0,32},{64,96},{1,33},{65,97},{2,34},{66,98},{3,35},{67,99},{4,36}... | collective-permute-start | bytes 3932168 | tf_op jit(solution)/shard_map/ppermute | solution.py:38
  209.9 6.4 %collective-permute-start.43 = (bf16[2,2,2,2,2,80,256]{6,5,4,3,2,1,0:T(8,128)(2,1)S(1)}, bf16[2,2,2,2,2,80,256]{6,5,4,3,2,1,0:T(8,128)(2,1)S(1)}, u32[]{:S(2)}, u32[]{:S(2)}) collective-permute-start(bf16[2,2,2,2,2,80,256]{6,5,4,3,2,1,0:T(8,128)(2,1)S(1)} %collective-permute-done.38.refs_3_), channel_id=1, source_target_pairs={{0,32},{64,96},{1,33},{65,97},{2,34},{66,98},{3,35},{67,99},{4,36}... | collective-permute-start | bytes 3932168 | tf_op jit(solution)/shard_map/ppermute | solution.py:38
  211.3 4.9 %collective-permute-start.41 = (bf16[2,2,2,2,2,80,256]{6,5,4,3,2,1,0:T(8,128)(2,1)S(1)}, bf16[2,2,2,2,2,80,256]{6,5,4,3,2,1,0:T(8,128)(2,1)S(1)}, u32[]{:S(2)}, u32[]{:S(2)}) collective-permute-start(bf16[2,2,2,2,2,80,256]{6,5,4,3,2,1,0:T(8,128)(2,1)S(1)} %collective-permute-done.37.refs_1_), channel_id=1, source_target_pairs={{0,32},{64,96},{1,33},{65,97},{2,34},{66,98},{3,35},{67,99},{4,36}... | collective-permute-start | bytes 3932168 | tf_op jit(solution)/shard_map/ppermute | solution.py:38
  211.3 4.9 %collective-permute-start.45 = (bf16[2,2,2,2,2,64,256]{6,5,4,3,2,1,0:T(8,128)(2,1)S(1)}, bf16[2,2,2,2,2,64,256]{6,5,4,3,2,1,0:T(8,128)(2,1)S(1)}, u32[]{:S(2)}, u32[]{:S(2)}) collective-permute-start(bf16[2,2,2,2,2,64,256]{6,5,4,3,2,1,0:T(8,128)(2,1)S(1)} %collective-permute-done.39.refs_5_), channel_id=1, source_target_pairs={{0,32},{64,96},{1,33},{65,97},{2,34},{66,98},{3,35},{67,99},{4,36}... | collective-permute-start | bytes 3145736 | tf_op jit(solution)/shard_map/ppermute | solution.py:38
  (3 other events, 19.8 us)

commit v3 on v0

v3 whole, which is shorter than its diff:
```python
import itertools

import jax
import jax.numpy as jnp
from jax import lax
from jax.experimental import pallas as pl
from jax.experimental.pallas import tpu as pltpu
from jax.sharding import Mesh
from jax.sharding import PartitionSpec as P

STEP = 10


beta_one = 0.9
beta_two = 0.99
eps = 1e-08
galore_scale = 4.0

BF = jnp.bfloat16
F32 = jnp.float32
AXES = ("zl", "c", "y1", "y0", "x1", "x0", "zh")
FSDP = ("y1", "y0", "x1", "x0", "zh")
ORDERS = ("xyz", "yzx", "zxy")


def flat(co):
    return ((co["z"] % 2) * 2 + co["c"]) * 32 + (co["y"] * 4 + co["x"]) * 2 + co["z"] // 2


def permute(arr, move):
    pairs = []
    for c in range(2):
        for y in range(4):
            for x in range(4):
                for z in range(4):
                    co = {"c": c, "y": y, "x": x, "z": z}
                    pairs.append((flat(co), flat(move(dict(co)))))
    return lax.ppermute(arr, AXES, pairs)


def swap(arr, axis, late=0):
    def move(co):
        co[axis] ^= 3 if co["c"] != late else 1
        return co

    return permute(arr, move)


def swap_core(arr):
    def move(co):
        co["c"] ^= 1
        return co

    return permute(arr, move)


def swap_low(arr):
    def move(co):
        co["z"] ^= 1
        return co

    return permute(arr, move)


PARTS = ((0, 3), (3, 6), (6, 8))


def join(arrays, gots, *extra):
    n = len(arrays)
    both = lax.optimization_barrier((*arrays, *gots, *extra))
    return [jnp.stack(pair) for pair in zip(both[:n], both[n : 2 * n])], *both[2 * n :]


def gather(piece, beside):
    tied = ()
    for axis in "zxy"[piece.ndim - 2 :]:
        got = swap(piece, axis, late=1)
        if beside:
            tied = beside[0](*tied)
        (piece,), *tied = join([piece], [got], *tied)
        beside = beside[1:]
    piece = piece.reshape(8, *piece.shape[3:])
    parts = [piece[begin:end] for begin, end in PARTS]
    for stage in (2, 1):
        gots = [swap(part, order[stage]) for order, part in zip(ORDERS, parts)]
        if beside:
            tied = beside[0](*tied)
        parts, *tied = join(parts, gots, *tied)
        beside = beside[1:]
    return parts, [swap(part, order[0]) for order, part in zip(ORDERS, parts)], tied


def bits(place, core):
    high = place // 2
    low = lax.bitwise_xor(place % 2, high)
    return low + core * (high - low), high + core * (low - high)


def place_of(u, v, core):
    high, low = v + core * (u - v), u + core * (v - u)
    return high * 2 + lax.bitwise_xor(high, low)


def chips():
    for uy, ux, vy, vx in itertools.product(range(2), repeat=4):
        yield [({"y": uy, "x": ux, "z": uz}, vy * 4 + vx * 2 + vz) for uz in range(2) for vz in range(2)]


def absolute(u, v, axis, pos_ref, core):
    j = "yxz".index(axis)
    return lax.bitwise_xor(pos_ref[j], place_of(u[axis], v // (4, 2, 1)[j] % 2, core))


def part_of(v):
    return next((i, v - begin) for i, (begin, end) in enumerate(PARTS) if v < end)


SMEM = pl.BlockSpec(memory_space=pltpu.SMEM)
VMEM = pl.BlockSpec(memory_space=pltpu.VMEM)
HBM = pl.BlockSpec(memory_space=pltpu.HBM)


def place(whole, arrays, which, pos, core):
    rows, cols = arrays[0].shape[-2:]
    size = 64 * rows * cols

    def kernel(pos_ref, core_ref, *refs):
        out = refs[-1]
        for run in chips():
            for u, v in run:
                part, w = part_of(v)
                first, second, third = (u[a] for a in ORDERS[part])
                if first == which:
                    y, x, z = (absolute(u, v, a, pos_ref, core_ref[0]) for a in "yxz")
                    out[(y * 4 + x) * 4 + z] = refs[part][second, third, w]

    return pl.pallas_call(
        kernel,
        out_shape=jax.ShapeDtypeStruct((64, rows, cols), BF),
        in_specs=[SMEM] * 2 + [VMEM] * (3 if whole is None else 4),
        out_specs=VMEM,
        input_output_aliases={} if whole is None else {5: 0},
        compiler_params=pltpu.CompilerParams(vmem_limit_bytes=8 * 2**20),
        cost_estimate=pl.CostEstimate(flops=0, bytes_accessed=2 * size, transcendentals=0),
    )(pos, core, *arrays, *(() if whole is None else (whole,)))


def load(*arrays):
    n, cuts = len(arrays), 4

    def kernel(*refs):
        sem = refs[-1]
        copies = []
        for src, dst in zip(refs[:n], refs[n:]):
            rows = src.shape[0] // cuts
            for i in range(cuts):
                at = pl.ds(i * rows, rows)
                copies.append(pltpu.make_async_copy(src.at[at], dst.at[at], sem.at[len(copies)]))
        for copy in copies:
            copy.start()
        for copy in copies:
            copy.wait()

    return pl.pallas_call(
        kernel,
        out_shape=[jax.ShapeDtypeStruct(a.shape, a.dtype) for a in arrays],
        in_specs=[HBM] * n,
        out_specs=[VMEM] * n,
        scratch_shapes=[pltpu.SemaphoreType.DMA((n * cuts,))],
        compiler_params=pltpu.CompilerParams(vmem_limit_bytes=8 * 2**20),
        cost_estimate=pl.CostEstimate(flops=0, bytes_accessed=sum(2 * a.size for a in arrays), transcendentals=0),
    )(*arrays)


def project(a0, a1, whole):
    tok, depth = a0.shape
    cols = whole.shape[2]

    def kernel(a0_ref, a1_ref, b_ref, o0, o1):
        a = jnp.concatenate([a0_ref[...], a1_ref[...]])
        out = jnp.dot(a, b_ref[...].reshape(depth, cols), preferred_element_type=F32).astype(BF)
        o0[...] = out[:tok]
        o1[...] = out[tok:]

    return pl.pallas_call(
        kernel,
        out_shape=[jax.ShapeDtypeStruct((tok, cols), BF)] * 2,
        in_specs=[VMEM] * 3,
        out_specs=[VMEM] * 2,
        compiler_params=pltpu.CompilerParams(vmem_limit_bytes=8 * 2**20),
        cost_estimate=pl.CostEstimate(
            flops=4 * tok * depth * cols, bytes_accessed=4 * tok * depth + 2 * depth * cols, transcendentals=0
        ),
    )(a0, a1, whole)


def partials(g0, g1, p0, p1, pos, keeps=None):
    tok, ffw = g0.shape
    cols = p0.shape[1]
    nb = ffw // 16
    rows = nb // 4

    def sent(u, v):
        return u[ORDERS[part_of(v)[0]][0]]

    runs = [run for run in chips() if any(sent(u, v) for u, v in run) == (keeps is None)]

    def kernel(pos_ref, g0_ref, g1_ref, p0_ref, p1_ref, *refs):
        dims = (((0,), (0,)), ((), ()))
        columns = []
        for run in runs:
            y, x = (absolute(*run[0], a, pos_ref, pos_ref[3]) for a in "yx")
            columns.append(pl.ds(pl.multiple_of((y * 4 + x) * nb, nb), nb))
        if keeps is None:
            *send_refs, keep_x, keep_y, keep_z, scratch = refs
            keep_refs = keep_x, keep_y, keep_z
        else:
            *_, keep_x, keep_y, keep_z, scratch, held, sem = refs
            keep_refs = keep_x, keep_y, keep_z
            copies = [
                [pltpu.make_async_copy(g.at[:, at], held.at[i, j], sem.at[i, j]) for j, g in enumerate((g0_ref, g1_ref))]
                for i, at in enumerate(columns)
            ]
            for copy in itertools.chain(*copies):
                copy.start()
        for i, (run, at) in enumerate(zip(runs, columns)):
            if keeps is None:
                terms = g0_ref[:, at], g1_ref[:, at]
            else:
                for copy in copies[i]:
                    copy.wait()
                terms = held[i, 0], held[i, 1]
            scratch[i % 2] = (
                (
                    lax.dot_general(terms[0], p0_ref[...], dims, preferred_element_type=F32)
                    + lax.dot_general(terms[1], p1_ref[...], dims, preferred_element_type=F32)
                )
                .astype(BF)
                .reshape(4, rows, cols)
            )
            for u, v in run:
                part, w = part_of(v)
                _, second, third = (u[a] for a in ORDERS[part])
                outs = send_refs if sent(u, v) else keep_refs
                outs[part][second, third, w] = scratch[i % 2, absolute(u, v, "z", pos_ref, pos_ref[3])]

    shapes = [(2, 2, end - begin, rows, cols) for begin, end in PARTS] * (2 if keeps is None else 1)
    share = len(runs) / 16
    return pl.pallas_call(
        kernel,
        out_shape=[jax.ShapeDtypeStruct(s, BF) for s in shapes],
        in_specs=[SMEM] + ([VMEM] * 4 if keeps is None else [HBM] * 2 + [VMEM] * 5),
        out_specs=[VMEM] * len(shapes),
        input_output_aliases={} if keeps is None else {5: 0, 6: 1, 7: 2},
        scratch_shapes=[pltpu.VMEM((2, 4, rows, cols), BF)]
        + ([] if keeps is None else [pltpu.VMEM((len(runs), 2, tok, nb), BF), pltpu.SemaphoreType.DMA((len(runs), 2))]),
        compiler_params=pltpu.CompilerParams(vmem_limit_bytes=(6 if keeps is None else 12) * 2**20),
        cost_estimate=pl.CostEstimate(
            flops=int(4 * tok * ffw * cols * share),
            bytes_accessed=int((4 * tok * ffw + 2 * ffw * cols) * share),
            transcendentals=0,
        ),
    )(pos, g0, g1, p0, p1, *(keeps or ()))


def updates(basis, own, other, core):
    rows, rank = basis.shape
    shard, half = own.shape[1:]
    nb = 4 * shard
    ffw = 16 * nb

    def kernel(core_ref, own_ref, other_ref, b_ref, out, stage, sem):
        dims = (((1,), (1,)), ((), ()))
        core = core_ref[0]
        copies = []
        for i in range(16):
            at = pl.ds(i * nb, nb)
            total = lax.dot_general(
                b_ref[core], own_ref[4 * i : 4 * i + 4].reshape(nb, half), dims, preferred_element_type=F32
            ) + lax.dot_general(
                b_ref[1 - core], other_ref[4 * i : 4 * i + 4].reshape(nb, half), dims, preferred_element_type=F32
            )
            stage[:, at] = (-galore_scale * total).astype(BF)
            copies.append(pltpu.make_async_copy(stage.at[:, at], out.at[:, at], sem.at[i]))
            copies[-1].start()
        for copy in copies:
            copy.wait()

    halves = jnp.stack([basis[:, :half], basis[:, half:]])
    return pl.pallas_call(
        kernel,
        out_shape=jax.ShapeDtypeStruct((rows, ffw), BF),
        in_specs=[SMEM] + [VMEM] * 3,
        out_specs=pl.BlockSpec(memory_space=pl.ANY),
        scratch_shapes=[pltpu.VMEM((rows, ffw), BF), pltpu.SemaphoreType.DMA((16,))],
        compiler_params=pltpu.CompilerParams(vmem_limit_bytes=12 * 2**20),
        cost_estimate=pl.CostEstimate(
            flops=2 * rows * ffw * rank, bytes_accessed=2 * (ffw * rank + rows * ffw), transcendentals=0
        ),
    )(core, own, other, halves)


def add(a, b):
    return (a.astype(F32) + b.astype(F32)).astype(BF)


def local(activations, out_grads, basis, first_moment, second_moment):
    core, zl = lax.axis_index("c"), lax.axis_index("zl")
    places = [lax.axis_index(a + "1") * 2 + lax.axis_index(a + "0") for a in "yx"] + [lax.axis_index("zh") * 2 + zl]
    pos = jnp.stack(places + [core]).astype(jnp.int32)
    rank = basis.shape[1]
    half = rank // 2
    shard = out_grads.shape[1] // 64
    brows = basis.shape[0] // 2

    act_other = swap_core(activations)
    g_other = swap_core(out_grads)

    mine, theirs = pos[3:], 1 - pos[3:]
    swapped = [lambda: ()] * 4 + [lambda: (act_other, g_other)]
    near, far, (act_other, g_other) = gather(
        lax.dynamic_slice(basis, (zl * brows, core * half), (brows, half)), swapped
    )
    whole = place(place(None, near, 0, pos, mine), far, 1, pos, mine)
    near_acts = load(activations, act_other)
    near_gs = load(out_grads, g_other)
    terms = (*project(*near_acts, whole), pos)
    *sends, keep_x, keep_y, keep_z = partials(*near_gs, *terms)
    keeps = partials(out_grads, g_other, *terms, [keep_x, keep_y, keep_z])

    at = (zl * shard, core * half)
    moments = [lax.dynamic_slice(m, at, (shard, half)) for m in (first_moment, second_moment)]
    moments = lax.optimization_barrier((jnp.stack(moments), *sends))[0]

    for stage in range(3):
        gots = [swap(send, order[stage]) for order, send in zip(ORDERS, sends)]
        if stage == 0:
            *gots, theirs_moments = lax.optimization_barrier((*gots, swap(moments, "z", late=1)))
        if stage < 2:
            sends = [add(keep[1], got[1]) for keep, got in zip(keeps, gots)]
            keeps = [add(keep[0], got[0]) for keep, got in zip(keeps, gots)]
        else:
            keeps = [add(keep, got) for keep, got in zip(keeps, gots)]
    keep = jnp.concatenate(keeps).reshape(2, 2, 2, shard, half)
    keep, send = keep[0], keep[1]
    for axis in "yx":
        got = swap(send, axis, late=1)
        send = add(keep[1], got[1])
        keep = add(keep[0], got[0])
    keep = jnp.stack([keep, send])
    blocks = add(keep, swap(keep, "z", late=1)[::-1])
    reduced = blocks[0]

    def adam(first, second, red):
        new_first = beta_one * first + (1.0 - beta_one) * red
        new_second = beta_two * second + (1.0 - beta_two) * red * red
        return new_first, new_second

    new_first, new_second = adam(*jnp.stack([moments, theirs_moments], axis=1), blocks.astype(F32))
    corrected = new_first / (1.0 - beta_one**STEP)
    normalized = (corrected / (jnp.sqrt(new_second / (1.0 - beta_two**STEP)) + eps)).astype(BF)

    def columns():
        other = swap_core(reduced)
        both = jnp.concatenate([reduced, other], 1), jnp.concatenate([other, reduced], 1)
        return (jnp.where(core == 0, *both),)

    def rows(own):
        other = swap_low(own)
        return (jnp.where(zl == 0, jnp.concatenate([own, other]), jnp.concatenate([other, own])),)

    near, far, (rows,) = gather(normalized, [columns, rows])
    own = place(None, near, 0, pos, mine)
    near = lax.optimization_barrier((*near, own))[:3]
    other = place(None, [swap_core(a) for a in near], 0, pos, theirs)
    update = updates(
        basis, place(own, far, 1, pos, mine), place(other, [swap_core(a) for a in far], 1, pos, theirs), mine
    )
    out_first, out_second = adam(first_moment, second_moment, rows.astype(F32))
    return (update, out_first, out_second)


def solution(mesh):
    chips = Mesh(mesh.devices.reshape(2, 2, 2, 2, 2, 2, 2), AXES)
    in_specs = (P(AXES, None), P(AXES, None), P(FSDP, None), P(FSDP, None), P(FSDP, None))
    out_specs = (P(FSDP, None), P(FSDP, None), P(FSDP, None))
    return jax.shard_map(local, mesh=chips, in_specs=in_specs, out_specs=out_specs, check_vma=False)
```

time: 694 us -> 202 us (0.29)
  waiting for transfers between devices: 608 us -> 82.6 us
  starting transfers between devices: 0.16 us -> 70 us
  Pallas kernels: 0 us -> 29.8 us
  matrix products: 29.4 us -> 0 us
  local copies, waits for them, and re-layouts: 38 us -> 9.2 us
  between operations: 13.8 us -> 1.29 us
    unnamed x5 -> x0, waiting for transfers between devices: 316 us -> none
    all_gather x2 -> x0, waiting for transfers between devices: 252 us -> none  [the longest x1 141 us: local(): lax.all_gather(normalized, 'fsdp', axis=0, tiled=True)]
    ppermute x0 -> x46, waiting for transfers between devices: none -> 82.6 us  [permute(): return lax.ppermute(arr, AXES, pairs)]
    ppermute x0 -> x46, starting transfers between devices: none -> 70 us  [permute(): return lax.ppermute(arr, AXES, pairs)]
    psum x1 -> x0, waiting for transfers between devices: 39.8 us -> none  [local(): reduced = lax.psum(own_rows, 'grp').astype(jnp.float32)]
    pallas_call x0 -> x12, Pallas kernels: none -> 29.8 us  [the longest x2 10.5 us: partials(): pl.pallas_call(kernel, out_shape=[jax.ShapeDtypeStruct(s, BF) for s in sh...]
    dot_general x3 -> x0, matrix products: 29.4 us -> none  [the longest x1 12.1 us: local(): lax.dot_general(basis, lax.all_gather(normalized, 'fsdp', axis=0, tiled=T...]
    unnamed x13 -> x18, local copies, waits for them, and re-layouts: 36 us -> 7.07 us
  transfers between devices with their start and end apart: 4 -> 46, of which waited for: 4 -> 23; matrix products, arithmetic and copies ran while one was open for 1% -> 4% of each run, Pallas kernels for 0% -> 7%
where the time goes in v3:
time: 202 us
  waiting for transfers between devices  82.6 us (41%)
  starting transfers between devices  70 us (35%)
  Pallas kernels  29.8 us (15%)
  local copies, waits for them, and re-layouts  9.2 us (5%)
  other arithmetic  8.98 us (4%)
    ppermute x46, waiting for transfers between devices, permute(): return lax.ppermute(arr, AXES, pairs)  82.6 us
    ppermute x46, starting transfers between devices, permute(): return lax.ppermute(arr, AXES, pairs)  70 us
    pallas_call x2, Pallas kernels, partials(): pl.pallas_call(kernel, out_shape=[jax.ShapeDtypeStruct(s, BF) for s in sh...  10.5 us
    unnamed x18, local copies, waits for them, and re-layouts  7.07 us
    pallas_call x2, Pallas kernels, load(): pl.pallas_call(kernel, out_shape=[jax.ShapeDtypeStruct(a.shape, a.dtype)...  6.38 us
    convert_element_type x11, other arithmetic, add(): return (a.astype(F32) + b.astype(F32)).astype(BF)  5.57 us
    pallas_call x1, Pallas kernels, updates(): pl.pallas_call(kernel, out_shape=jax.ShapeDtypeStruct((rows, ffw), BF), i...  5.47 us
    pallas_call x6, Pallas kernels, place(): pl.pallas_call(kernel, out_shape=jax.ShapeDtypeStruct((64, rows, cols), B...  5.16 us
  transfers between devices with their start and end apart: 46, of which 23 were waited for; matrix products, arithmetic and copies ran while one was open for 4% of the time, Pallas kernels for 7%

profile of v3, /device:TPU:1, one launch (start us, length us, event | category | flops | bytes accessed | tf_op | source)
XLA Modules:
  0.0 201.8 jit_solution(17031325252901101997)
XLA Ops:
  3.1 1.7 collective-permute-start
  4.8 1.7 collective-permute-done
  7.8 2.6 %collective-permute-done.1 = bf16[2,128,256]{2,1,0:T(8,128)(2,1)S(1)} collective-permute-done((bf16[2,128,256]{2,1,0:T(8,128)(2,1)S(1)}, bf16[2,128,256]{2,1,0:T(8,128)(2,1)S(1)}, u32[]{:S(2)}, u32[]{:S(2)}) %collective-permute-start.1) | collective-permute-done | bytes 131104 | tf_op jit(solution)/shard_map/ppermute | solution.py:38
  11.8 4.0 %collective-permute-done.2 = bf16[2,2,128,256]{3,2,1,0:T(8,128)(2,1)S(1)} collective-permute-done((bf16[2,2,128,256]{3,2,1,0:T(8,128)(2,1)S(1)}, bf16[2,2,128,256]{3,2,1,0:T(8,128)(2,1)S(1)}, u32[]{:S(2)}, u32[]{:S(2)}) %collective-permute-start.2) | collective-permute-done | bytes 262176 | tf_op jit(solution)/shard_map/ppermute | solution.py:38
  15.8 3.6 %collective-permute-start.3 = (bf16[3,128,256]{2,1,0:T(8,128)(2,1)S(1)}, bf16[3,128,256]{2,1,0:T(8,128)(2,1)S(1)}, u32[]{:S(2)}, u32[]{:S(2)}) collective-permute-start(bf16[3,128,256]{2,1,0:T(8,128)(2,1)S(1)} %get-tuple-element.72), channel_id=1, source_target_pairs={{0,64},{64,0},{1,65},{65,1},{2,66},{66,2},{3,67},{67,3},{4,68},{68... | collective-permute-start | bytes 589832 | tf_op jit(solution)/shard_map/ppermute | solution.py:38
  19.4 2.5 %collective-permute-start.4 = (bf16[3,128,256]{2,1,0:T(8,128)(2,1)S(1)}, bf16[3,128,256]{2,1,0:T(8,128)(2,1)S(1)}, u32[]{:S(2)}, u32[]{:S(2)}) collective-permute-start(bf16[3,128,256]{2,1,0:T(8,128)(2,1)S(1)} %get-tuple-element.74), channel_id=1, source_target_pairs={{0,2},{64,66},{1,3},{65,67},{2,0},{66,64},{3,1},{67,65},{4,6},{68,... | collective-permute-start | bytes 589832 | tf_op jit(solution)/shard_map/ppermute | solution.py:38
  21.9 2.8 %collective-permute-start.5 = (bf16[2,128,256]{2,1,0:T(8,128)(2,1)S(1)}, bf16[2,128,256]{2,1,0:T(8,128)(2,1)S(1)}, u32[]{:S(2)}, u32[]{:S(2)}) collective-permute-start(bf16[2,128,256]{2,1,0:T(8,128)(2,1)S(1)} %slice.186), channel_id=1, source_target_pairs={{0,8},{64,72},{1,9},{65,73},{2,10},{66,74},{3,11},{67,75},{4,12},{... | collective-permute-start | bytes 393224 | tf_op jit(solution)/shard_map/ppermute | solution.py:38
  24.8 2.4 %collective-permute-done.5 = bf16[2,128,256]{2,1,0:T(8,128)(2,1)S(1)} collective-permute-done((bf16[2,128,256]{2,1,0:T(8,128)(2,1)S(1)}, bf16[2,128,256]{2,1,0:T(8,128)(2,1)S(1)}, u32[]{:S(2)}, u32[]{:S(2)}) %collective-permute-start.5) | collective-permute-done | bytes 131104 | tf_op jit(solution)/shard_map/ppermute | solution.py:38
  27.7 2.8 %collective-permute-start.6 = (bf16[2,3,128,256]{3,2,1,0:T(8,128)(2,1)S(1)}, bf16[2,3,128,256]{3,2,1,0:T(8,128)(2,1)S(1)}, u32[]{:S(2)}, u32[]{:S(2)}) collective-permute-start(bf16[2,3,128,256]{3,2,1,0:T(8,128)(2,1)S(1)} %pad_maximum_fusion.15), channel_id=1, source_target_pairs={{0,8},{64,72},{1,9},{65,73},{2,10},{66,74},{3,11},{67,75},{4,12},{... | collective-permute-start | bytes 1179656 | tf_op jit(solution)/shard_map/ppermute | solution.py:38
  30.5 1.6 collective-permute-start.8
  32.1 4.9 %collective-permute-done.8 = bf16[2,2,128,256]{3,2,1,0:T(8,128)(2,1)S(1)} collective-permute-done((bf16[2,2,128,256]{3,2,1,0:T(8,128)(2,1)S(1)}, bf16[2,2,128,256]{3,2,1,0:T(8,128)(2,1)S(1)}, u32[]{:S(2)}, u32[]{:S(2)}) %collective-permute-start.8) | collective-permute-done | bytes 262176 | tf_op jit(solution)/shard_map/ppermute | solution.py:38
  37.1 1.6 collective-permute-start.11
  42.4 2.5 %copy-done.1 = bf16[256,8192]{1,0:T(8,128)(2,1)S(1)} copy-done((bf16[256,8192]{1,0:T(8,128)(2,1)S(1)}, bf16[256,8192]{1,0:T(8,128)(2,1)}, u32[]{:S(2)}) %copy-start.1) | copy-done | bytes 4194328
  44.9 2.7 %shard_map.77 = (bf16[256,8192]{1,0:T(8,128)(2,1)S(1)}, bf16[256,8192]{1,0:T(8,128)(2,1)S(1)}) custom-call(bf16[256,8192]{1,0:T(8,128)(2,1)S(1)} %copy-done.1, bf16[256,8192]{1,0:T(8,128)(2,1)} %collective-permute-done.9.refs_1_), custom_call_target="tpu_custom_call" | custom-call | bytes 8388608 | tf_op jit(solution)/shard_map/pallas_call | solution.py:164
  48.1 3.7 %shard_map.76 = (bf16[256,14336]{1,0:T(8,128)(2,1)S(1)}, bf16[256,14336]{1,0:T(8,128)(2,1)S(1)}) custom-call(bf16[256,14336]{1,0:T(8,128)(2,1)S(1)} %bitcast.135, bf16[256,14336]{1,0:T(8,128)(2,1)} %collective-permute-done.10.refs_1_.g1_ref), custom_call_target="tpu_custom_call" | custom-call | bytes 14680064 | tf_op jit(solution)/shard_map/pallas_call | solution.py:164
  53.2 2.3 %shard_map.80 = (bf16[256,256]{1,0:T(8,128)(2,1)S(1)}, bf16[256,256]{1,0:T(8,128)(2,1)S(1)}) custom-call(bf16[256,8192]{1,0:T(8,128)(2,1)S(1)} %get-tuple-element.82.a0_ref, bf16[256,8192]{1,0:T(8,128)(2,1)S(1)} %get-tuple-element.83.a1_ref, bf16[64,128,256]{2,1,0:T(8,128)(2,1)S(1)} %shard_map.79.b_ref), custom_call_target="tpu_custom_call" | custom-call | flops 2147483648 | bytes 12582912 | tf_op jit(solution)/shard_map/pallas_call | solution.py:185
  55.5 5.5 %shard_map.81 = (bf16[2,2,3,224,256]{4,3,2,1,0:T(8,128)(2,1)}, bf16[2,2,3,224,256]{4,3,2,1,0:T(8,128)(2,1)}, bf16[2,2,2,224,256]{4,3,2,1,0:T(8,128)(2,1)}, bf16[...) custom-call(s32[4]{0:T(128)S(1)} %pad_add_fusion.pos_ref, ...), custom_call_target="tpu_custom_call" | custom-call | flops 2583691264 | bytes 15138816 | tf_op jit(solution)/shard_map/pallas_call | solution.py:249
  62.0 2.1 %collective-permute-start.14 = (bf16[2,2,3,224,256]{4,3,2,1,0:T(8,128)(2,1)}, bf16[2,2,3,224,256]{4,3,2,1,0:T(8,128)(2,1)}, u32[]{:S(2)}, u32[]{:S(2)}) collective-permute-start(bf16[2,2,3,224,256]{4,3,2,1,0:T(8,128)(2,1)} %get-tuple-element.92), channel_id=1, source_target_pairs={{0,2},{64,66},{1,3},{65,67},{2,0},{66,64},{3,1},{67,65},{4,6},{68,... | collective-permute-start | bytes 4128776 | tf_op jit(solution)/shard_map/ppermute | solution.py:38
  67.4 3.1 %copy-done = bf16[256,14336]{1,0:T(8,128)(2,1)S(1)} copy-done((bf16[256,14336]{1,0:T(8,128)(2,1)S(1)}, bf16[256,14336]{1,0:T(8,128)(2,1)}, u32[]{:S(2)}) %copy-start) | copy-done | bytes 7340056
  70.5 4.9 %shard_map.82 = (bf16[2,2,3,224,256]{4,3,2,1,0:T(8,128)(2,1)S(1)}, bf16[2,2,3,224,256]{4,3,2,1,0:T(8,128)(2,1)S(1)}, bf16[2,2,2,224,256]{4,3,2,1,0:T(8,128)(2,1)S(1)}) custom-call(s32[4]{0:T(128)S(1)} %pad_add_fusion.pos_ref, bf16[256,14336]{1,0:T(8,128)(2,1)S(1)} %copy-done, ...), custom_call_target="tpu_custom_call", output_to_operand_aliasing={{0}: (5, {}), {1}: (6, {}), {2}: (7, {})} | custom-call | flops 1174405120 | bytes 6881280 | tf_op jit(solution)/shard_map/pallas_call | solution.py:249
  75.4 4.6 %collective-permute-done.17 = f32[2,224,256]{2,1,0:T(8,128)S(1)} collective-permute-done((f32[2,224,256]{2,1,0:T(8,128)S(1)}, f32[2,224,256]{2,1,0:T(8,128)S(1)}, u32[]{:S(2)}, u32[]{:S(2)}) %collective-permute-start.17) | collective-permute-done | bytes 458784 | tf_op jit(solution)/shard_map/ppermute | solution.py:38
  80.1 4.1 %collective-permute-done.16 = bf16[2,2,2,224,256]{4,3,2,1,0:T(8,128)(2,1)} collective-permute-done((bf16[2,2,2,224,256]{4,3,2,1,0:T(8,128)(2,1)}, bf16[2,2,2,224,256]{4,3,2,1,0:T(8,128)(2,1)}, u32[]{:S(2)}, u32[]{:S(2)}) %collective-permute-start.16) | collective-permute-done | bytes 917536 | tf_op jit(solution)/shard_map/ppermute | solution.py:38
  84.1 1.7 add_convert_fusion.1
  88.2 1.7 add_convert_fusion.3
  91.4 4.6 %collective-permute-done.22 = bf16[2,2,224,256]{3,2,1,0:T(8,128)(2,1)S(1)} collective-permute-done((bf16[2,2,224,256]{3,2,1,0:T(8,128)(2,1)S(1)}, bf16[2,2,224,256]{3,2,1,0:T(8,128)(2,1)S(1)}, u32[]{:S(2)}, u32[]{:S(2)}) %collective-permute-start.22) | collective-permute-done | bytes 458784 | tf_op jit(solution)/shard_map/ppermute | solution.py:38
  98.4 2.5 %collective-permute-done.18 = bf16[2,3,224,256]{3,2,1,0:T(8,128)(2,1)S(1)} collective-permute-done((bf16[2,3,224,256]{3,2,1,0:T(8,128)(2,1)S(1)}, bf16[2,3,224,256]{3,2,1,0:T(8,128)(2,1)S(1)}, u32[]{:S(2)}, u32[]{:S(2)}) %collective-permute-start.18) | collective-permute-done | bytes 688160 | tf_op jit(solution)/shard_map/ppermute | solution.py:38
  101.1 2.0 collective-permute-start.19
  105.1 3.3 %collective-permute-done.19 = bf16[3,224,256]{2,1,0:T(8,128)(2,1)S(1)} collective-permute-done((bf16[3,224,256]{2,1,0:T(8,128)(2,1)S(1)}, bf16[3,224,256]{2,1,0:T(8,128)(2,1)S(1)}, u32[]{:S(2)}, u32[]{:S(2)}) %collective-permute-start.19) | collective-permute-done | bytes 344096 | tf_op jit(solution)/shard_map/ppermute | solution.py:38
  108.6 4.2 %collective-permute-done.24 = bf16[2,2,224,256]{3,2,1,0:T(8,128)(2,1)S(1)} collective-permute-done((bf16[2,2,224,256]{3,2,1,0:T(8,128)(2,1)S(1)}, bf16[2,2,224,256]{3,2,1,0:T(8,128)(2,1)S(1)}, u32[]{:S(2)}, u32[]{:S(2)}) %collective-permute-start.24) | collective-permute-done | bytes 458784 | tf_op jit(solution)/shard_map/ppermute | solution.py:38
  113.0 4.9 %collective-permute-done.25 = bf16[2,224,256]{2,1,0:T(8,128)(2,1)S(1)} collective-permute-done((bf16[2,224,256]{2,1,0:T(8,128)(2,1)S(1)}, bf16[2,224,256]{2,1,0:T(8,128)(2,1)S(1)}, u32[]{:S(2)}, u32[]{:S(2)}) %collective-permute-start.25) | collective-permute-done | bytes 229408 | tf_op jit(solution)/shard_map/ppermute | solution.py:38
  118.0 4.9 %collective-permute-done.26 = bf16[2,224,256]{2,1,0:T(8,128)(2,1)S(1)} collective-permute-done((bf16[2,224,256]{2,1,0:T(8,128)(2,1)S(1)}, bf16[2,224,256]{2,1,0:T(8,128)(2,1)S(1)}, u32[]{:S(2)}, u32[]{:S(2)}) %collective-permute-start.26) | collective-permute-done | bytes 229408 | tf_op jit(solution)/shard_map/ppermute | solution.py:38
  123.3 7.5 %collective-permute-start.28 = (bf16[224,256]{1,0:T(8,128)(2,1)S(1)}, bf16[224,256]{1,0:T(8,128)(2,1)S(1)}, u32[]{:S(2)}, u32[]{:S(2)}) collective-permute-start(bf16[224,256]{1,0:T(8,128)(2,1)S(1)} %slice_bitcast_fusion.10), channel_id=1, source_target_pairs={{0,32},{64,96},{1,33},{65,97},{2,34},{66,98},{3,35},{67,99},{4,36}... | collective-permute-start | bytes 344072 | tf_op jit(solution)/shard_map/ppermute | solution.py:38
  130.8 3.7 %collective-permute-start.27 = (bf16[2,224,256]{2,1,0:T(8,128)(2,1)S(1)}, bf16[2,224,256]{2,1,0:T(8,128)(2,1)S(1)}, u32[]{:S(2)}, u32[]{:S(2)}) collective-permute-start(bf16[2,224,256]{2,1,0:T(8,128)(2,1)S(1)} %get-tuple-element.106), channel_id=1, source_target_pairs={{0,6},{64,70},{1,7},{65,71},{2,4},{66,68},{3,5},{67,69},{4,2},{68,... | collective-permute-start | bytes 688136 | tf_op jit(solution)/shard_map/ppermute | solution.py:38
  134.6 3.3 %collective-permute-done.27 = bf16[2,224,256]{2,1,0:T(8,128)(2,1)S(1)} collective-permute-done((bf16[2,224,256]{2,1,0:T(8,128)(2,1)S(1)}, bf16[2,224,256]{2,1,0:T(8,128)(2,1)S(1)}, u32[]{:S(2)}, u32[]{:S(2)}) %collective-permute-start.27) | collective-permute-done | bytes 229408 | tf_op jit(solution)/shard_map/ppermute | solution.py:38
  140.1 3.9 %collective-permute-done.30 = bf16[224,512]{1,0:T(8,128)(2,1)S(1)} collective-permute-done((bf16[224,512]{1,0:T(8,128)(2,1)S(1)}, bf16[224,512]{1,0:T(8,128)(2,1)S(1)}, u32[]{:S(2)}, u32[]{:S(2)}) %collective-permute-start.30) | collective-permute-done | bytes 229408 | tf_op jit(solution)/shard_map/ppermute | solution.py:38
  144.1 1.5 collective-permute-done.29
  145.8 3.0 %collective-permute-start.31 = (bf16[3,224,256]{2,1,0:T(8,128)(2,1)S(1)}, bf16[3,224,256]{2,1,0:T(8,128)(2,1)S(1)}, u32[]{:S(2)}, u32[]{:S(2)}) collective-permute-start(bf16[3,224,256]{2,1,0:T(8,128)(2,1)S(1)} %get-tuple-element.112), channel_id=1, source_target_pairs={{0,64},{64,0},{1,65},{65,1},{2,66},{66,2},{3,67},{67,3},{4,68},{68... | collective-permute-start | bytes 1032200 | tf_op jit(solution)/shard_map/ppermute | solution.py:38
  148.8 2.6 %collective-permute-start.32 = (bf16[3,224,256]{2,1,0:T(8,128)(2,1)S(1)}, bf16[3,224,256]{2,1,0:T(8,128)(2,1)S(1)}, u32[]{:S(2)}, u32[]{:S(2)}) collective-permute-start(bf16[3,224,256]{2,1,0:T(8,128)(2,1)S(1)} %get-tuple-element.114), channel_id=1, source_target_pairs={{0,2},{64,66},{1,3},{65,67},{2,0},{66,64},{3,1},{67,65},{4,6},{68,... | collective-permute-start | bytes 1032200 | tf_op jit(solution)/shard_map/ppermute | solution.py:38
  151.5 3.0 %collective-permute-start.33 = (bf16[2,224,256]{2,1,0:T(8,128)(2,1)S(1)}, bf16[2,224,256]{2,1,0:T(8,128)(2,1)S(1)}, u32[]{:S(2)}, u32[]{:S(2)}) collective-permute-start(bf16[2,224,256]{2,1,0:T(8,128)(2,1)S(1)} %slice.209), channel_id=1, source_target_pairs={{0,8},{64,72},{1,9},{65,73},{2,10},{66,74},{3,11},{67,75},{4,12},{... | collective-permute-start | bytes 688136 | tf_op jit(solution)/shard_map/ppermute | solution.py:38
  154.4 3.4 %collective-permute-done.33 = bf16[2,224,256]{2,1,0:T(8,128)(2,1)S(1)} collective-permute-done((bf16[2,224,256]{2,1,0:T(8,128)(2,1)S(1)}, bf16[2,224,256]{2,1,0:T(8,128)(2,1)S(1)}, u32[]{:S(2)}, u32[]{:S(2)}) %collective-permute-start.33) | collective-permute-done | bytes 229408 | tf_op jit(solution)/shard_map/ppermute | solution.py:38
  158.2 2.8 %collective-permute-start.34 = (bf16[2,3,224,256]{3,2,1,0:T(8,128)(2,1)S(1)}, bf16[2,3,224,256]{3,2,1,0:T(8,128)(2,1)S(1)}, u32[]{:S(2)}, u32[]{:S(2)}) collective-permute-start(bf16[2,3,224,256]{3,2,1,0:T(8,128)(2,1)S(1)} %pad_maximum_fusion.6), channel_id=1, source_target_pairs={{0,8},{64,72},{1,9},{65,73},{2,10},{66,74},{3,11},{67,75},{4,12},{... | collective-permute-start | bytes 2064392 | tf_op jit(solution)/shard_map/ppermute | solution.py:38
  162.2 7.4 %collective-permute-done.36 = bf16[2,2,224,256]{3,2,1,0:T(8,128)(2,1)S(1)} collective-permute-done((bf16[2,2,224,256]{3,2,1,0:T(8,128)(2,1)S(1)}, bf16[2,2,224,256]{3,2,1,0:T(8,128)(2,1)S(1)}, u32[]{:S(2)}, u32[]{:S(2)}) %collective-permute-start.36) | collective-permute-done | bytes 458784 | tf_op jit(solution)/shard_map/ppermute | solution.py:38
  169.7 2.4 %collective-permute-start.38 = (bf16[2,2,3,224,256]{4,3,2,1,0:T(8,128)(2,1)S(1)}, bf16[2,2,3,224,256]{4,3,2,1,0:T(8,128)(2,1)S(1)}, u32[]{:S(2)}, u32[]{:S(2)}) collective-permute-start(bf16[2,2,3,224,256]{4,3,2,1,0:T(8,128)(2,1)S(1)} %pad_maximum_fusion.1.refs_1_), channel_id=1, source_target_pairs={{0,8},{64,72},{1,9},{65,73},{2,10},{66,74},{3,11},{67,75},{4,12},{... | collective-permute-start | bytes 4128776 | tf_op jit(solution)/shard_map/ppermute | solution.py:38
  174.7 2.7 %collective-permute-start.39 = (bf16[2,2,2,224,256]{4,3,2,1,0:T(8,128)(2,1)S(1)}, bf16[2,2,2,224,256]{4,3,2,1,0:T(8,128)(2,1)S(1)}, u32[]{:S(2)}, u32[]{:S(2)}) collective-permute-start(bf16[2,2,2,224,256]{4,3,2,1,0:T(8,128)(2,1)S(1)} %pad_maximum_fusion.3.refs_2_), channel_id=1, source_target_pairs={{0,64},{64,0},{1,65},{65,1},{2,66},{66,2},{3,67},{67,3},{4,68},{68... | collective-permute-start | bytes 2752520 | tf_op jit(solution)/shard_map/ppermute | solution.py:38
  177.9 10.3 %collective-permute-done.38.refs_1_ = bf16[2,2,3,224,256]{4,3,2,1,0:T(8,128)(2,1)S(1)} collective-permute-done((bf16[2,2,3,224,256]{4,3,2,1,0:T(8,128)(2,1)S(1)}, bf16[2,2,3,224,256]{4,3,2,1,0:T(8,128)(2,1)S(1)}, u32[]{:S(2)}, u32[]{:S(2)}) %collective-permute-start.38) | collective-permute-done | bytes 1376288 | tf_op jit(solution)/shard_map/ppermute | solution.py:38
  189.2 1.7 collective-permute-done.37.refs_0_
  191.5 1.5 fusion.1
  196.2 5.5 %shard_map.87 = bf16[256,14336]{1,0:T(8,128)(2,1)} custom-call(s32[1]{0:T(128)} %bitcast.core_ref, bf16[64,224,256]{2,1,0:T(8,128)(2,1)S(1)} %shard_map.84.own_ref, bf16[64,224,256]{2,1,0:T(8,128)(2,1)S(1)} %shard_map.86.other_ref, bf16[2,256,256]{2,1,0:T(8,128)(2,1)S(1)} %pad_maximum_fusion.19.b_ref), custom_call_target="tpu_custom_call" | custom-call | flops 3758096384 | bytes 22020096 | tf_op jit(solution)/shard_map/pallas_call | solution.py:290
  (120 shorter events, 36.8 us)
Async XLA Ops:
  0.6 36.4 %collective-permute-start.10 = (bf16[256,14336]{1,0:T(8,128)(2,1)}, bf16[256,14336]{1,0:T(8,128)(2,1)}, u32[]{:S(2)}, u32[]{:S(2)}) collective-permute-start(bf16[256,14336]{1,0:T(8,128)(2,1)} %g0_ref.1), channel_id=1, source_target_pairs={{0,32},{64,96},{1,33},{65,97},{2,34},{66,98},{3,35},{67,99},{4,36}... | collective-permute-start | bytes 22020104 | tf_op jit(solution)/shard_map/ppermute | solution.py:38
  2.1 34.9 %collective-permute-start.9 = (bf16[256,8192]{1,0:T(8,128)(2,1)}, bf16[256,8192]{1,0:T(8,128)(2,1)}, u32[]{:S(2)}, u32[]{:S(2)}) collective-permute-start(bf16[256,8192]{1,0:T(8,128)(2,1)} %refs_0_.3), channel_id=1, source_target_pairs={{0,32},{64,96},{1,33},{65,97},{2,34},{66,98},{3,35},{67,99},{4,36}... | collective-permute-start | bytes 12582920 | tf_op jit(solution)/shard_map/ppermute | solution.py:38
  3.1 3.4 %collective-permute-start = (bf16[128,256]{1,0:T(8,128)(2,1)S(1)}, bf16[128,256]{1,0:T(8,128)(2,1)S(1)}, u32[]{:S(2)}, u32[]{:S(2)}) collective-permute-start(bf16[128,256]{1,0:T(8,128)(2,1)S(1)} %dynamic_slice.11), channel_id=1, source_target_pairs={{0,65},{64,1},{1,64},{65,0},{2,67},{66,3},{3,66},{67,2},{4,69},{68... | collective-permute-start | bytes 196616 | tf_op jit(solution)/shard_map/ppermute | solution.py:38
  6.5 3.9 %collective-permute-start.1 = (bf16[2,128,256]{2,1,0:T(8,128)(2,1)S(1)}, bf16[2,128,256]{2,1,0:T(8,128)(2,1)S(1)}, u32[]{:S(2)}, u32[]{:S(2)}) collective-permute-start(bf16[2,128,256]{2,1,0:T(8,128)(2,1)S(1)} %pad_maximum_fusion.22), channel_id=1, source_target_pairs={{0,6},{64,70},{1,7},{65,71},{2,4},{66,68},{3,5},{67,69},{4,2},{68,... | collective-permute-start | bytes 393224 | tf_op jit(solution)/shard_map/ppermute | solution.py:38
  10.4 5.3 %collective-permute-start.2 = (bf16[2,2,128,256]{3,2,1,0:T(8,128)(2,1)S(1)}, bf16[2,2,128,256]{3,2,1,0:T(8,128)(2,1)S(1)}, u32[]{:S(2)}, u32[]{:S(2)}) collective-permute-start(bf16[2,2,128,256]{3,2,1,0:T(8,128)(2,1)S(1)} %pad_maximum_fusion.17), channel_id=1, source_target_pairs={{0,24},{64,88},{1,25},{65,89},{2,26},{66,90},{3,27},{67,91},{4,28}... | collective-permute-start | bytes 786440 | tf_op jit(solution)/shard_map/ppermute | solution.py:38
  15.8 11.3 %collective-permute-start.3 = (bf16[3,128,256]{2,1,0:T(8,128)(2,1)S(1)}, bf16[3,128,256]{2,1,0:T(8,128)(2,1)S(1)}, u32[]{:S(2)}, u32[]{:S(2)}) collective-permute-start(bf16[3,128,256]{2,1,0:T(8,128)(2,1)S(1)} %get-tuple-element.72), channel_id=1, source_target_pairs={{0,64},{64,0},{1,65},{65,1},{2,66},{66,2},{3,67},{67,3},{4,68},{68... | collective-permute-start | bytes 589832 | tf_op jit(solution)/shard_map/ppermute | solution.py:38
  19.4 7.7 %collective-permute-start.4 = (bf16[3,128,256]{2,1,0:T(8,128)(2,1)S(1)}, bf16[3,128,256]{2,1,0:T(8,128)(2,1)S(1)}, u32[]{:S(2)}, u32[]{:S(2)}) collective-permute-start(bf16[3,128,256]{2,1,0:T(8,128)(2,1)S(1)} %get-tuple-element.74), channel_id=1, source_target_pairs={{0,2},{64,66},{1,3},{65,67},{2,0},{66,64},{3,1},{67,65},{4,6},{68,... | collective-permute-start | bytes 589832 | tf_op jit(solution)/shard_map/ppermute | solution.py:38
  21.9 5.2 %collective-permute-start.5 = (bf16[2,128,256]{2,1,0:T(8,128)(2,1)S(1)}, bf16[2,128,256]{2,1,0:T(8,128)(2,1)S(1)}, u32[]{:S(2)}, u32[]{:S(2)}) collective-permute-start(bf16[2,128,256]{2,1,0:T(8,128)(2,1)S(1)} %slice.186), channel_id=1, source_target_pairs={{0,8},{64,72},{1,9},{65,73},{2,10},{66,74},{3,11},{67,75},{4,12},{... | collective-permute-start | bytes 393224 | tf_op jit(solution)/shard_map/ppermute | solution.py:38
  27.2 9.9 %collective-permute-start.7 = (bf16[2,3,128,256]{3,2,1,0:T(8,128)(2,1)S(1)}, bf16[2,3,128,256]{3,2,1,0:T(8,128)(2,1)S(1)}, u32[]{:S(2)}, u32[]{:S(2)}) collective-permute-start(bf16[2,3,128,256]{3,2,1,0:T(8,128)(2,1)S(1)} %pad_maximum_fusion.16), channel_id=1, source_target_pairs={{0,64},{64,0},{1,65},{65,1},{2,66},{66,2},{3,67},{67,3},{4,68},{68... | collective-permute-start | bytes 1179656 | tf_op jit(solution)/shard_map/ppermute | solution.py:38
  27.7 9.4 %collective-permute-start.6 = (bf16[2,3,128,256]{3,2,1,0:T(8,128)(2,1)S(1)}, bf16[2,3,128,256]{3,2,1,0:T(8,128)(2,1)S(1)}, u32[]{:S(2)}, u32[]{:S(2)}) collective-permute-start(bf16[2,3,128,256]{3,2,1,0:T(8,128)(2,1)S(1)} %pad_maximum_fusion.15), channel_id=1, source_target_pairs={{0,8},{64,72},{1,9},{65,73},{2,10},{66,74},{3,11},{67,75},{4,12},{... | collective-permute-start | bytes 1179656 | tf_op jit(solution)/shard_map/ppermute | solution.py:38
  30.5 6.5 %collective-permute-start.8 = (bf16[2,2,128,256]{3,2,1,0:T(8,128)(2,1)S(1)}, bf16[2,2,128,256]{3,2,1,0:T(8,128)(2,1)S(1)}, u32[]{:S(2)}, u32[]{:S(2)}) collective-permute-start(bf16[2,2,128,256]{3,2,1,0:T(8,128)(2,1)S(1)} %pad_maximum_fusion.18), channel_id=1, source_target_pairs={{0,2},{64,66},{1,3},{65,67},{2,0},{66,64},{3,1},{67,65},{4,6},{68,... | collective-permute-start | bytes 786440 | tf_op jit(solution)/shard_map/ppermute | solution.py:38
  37.1 14.7 %collective-permute-start.11 = (bf16[2,2,3,128,256]{4,3,2,1,0:T(8,128)(2,1)S(1)}, bf16[2,2,3,128,256]{4,3,2,1,0:T(8,128)(2,1)S(1)}, u32[]{:S(2)}, u32[]{:S(2)}) collective-permute-start(bf16[2,2,3,128,256]{4,3,2,1,0:T(8,128)(2,1)S(1)} %pad_maximum_fusion.4.refs_0_), channel_id=1, source_target_pairs={{0,2},{64,66},{1,3},{65,67},{2,0},{66,64},{3,1},{67,65},{4,6},{68,... | collective-permute-start | bytes 2359304 | tf_op jit(solution)/shard_map/ppermute | solution.py:38
  38.8 13.0 %collective-permute-start.12 = (bf16[2,2,3,128,256]{4,3,2,1,0:T(8,128)(2,1)S(1)}, bf16[2,2,3,128,256]{4,3,2,1,0:T(8,128)(2,1)}, u32[]{:S(2)}, u32[]{:S(2)}) collective-permute-start(bf16[2,2,3,128,256]{4,3,2,1,0:T(8,128)(2,1)S(1)} %pad_maximum_fusion.5.refs_1_), channel_id=1, source_target_pairs={{0,8},{64,72},{1,9},{65,73},{2,10},{66,74},{3,11},{67,75},{4,12},{... | collective-permute-start | bytes 2359304 | tf_op jit(solution)/shard_map/ppermute | solution.py:38
  40.2 11.6 %collective-permute-start.13 = (bf16[2,2,2,128,256]{4,3,2,1,0:T(8,128)(2,1)S(1)}, bf16[2,2,2,128,256]{4,3,2,1,0:T(8,128)(2,1)S(1)}, u32[]{:S(2)}, u32[]{:S(2)}) collective-permute-start(bf16[2,2,2,128,256]{4,3,2,1,0:T(8,128)(2,1)S(1)} %pad_maximum_fusion.9.refs_2_), channel_id=1, source_target_pairs={{0,64},{64,0},{1,65},{65,1},{2,66},{66,2},{3,67},{67,3},{4,68},{68... | collective-permute-start | bytes 1572872 | tf_op jit(solution)/shard_map/ppermute | solution.py:38
  62.0 22.2 %collective-permute-start.14 = (bf16[2,2,3,224,256]{4,3,2,1,0:T(8,128)(2,1)}, bf16[2,2,3,224,256]{4,3,2,1,0:T(8,128)(2,1)}, u32[]{:S(2)}, u32[]{:S(2)}) collective-permute-start(bf16[2,2,3,224,256]{4,3,2,1,0:T(8,128)(2,1)} %get-tuple-element.92), channel_id=1, source_target_pairs={{0,2},{64,66},{1,3},{65,67},{2,0},{66,64},{3,1},{67,65},{4,6},{68,... | collective-permute-start | bytes 4128776 | tf_op jit(solution)/shard_map/ppermute | solution.py:38
  64.0 20.1 %collective-permute-start.15 = (bf16[2,2,3,224,256]{4,3,2,1,0:T(8,128)(2,1)}, bf16[2,2,3,224,256]{4,3,2,1,0:T(8,128)(2,1)}, u32[]{:S(2)}, u32[]{:S(2)}) collective-permute-start(bf16[2,2,3,224,256]{4,3,2,1,0:T(8,128)(2,1)} %get-tuple-element.93), channel_id=1, source_target_pairs={{0,8},{64,72},{1,9},{65,73},{2,10},{66,74},{3,11},{67,75},{4,12},{... | collective-permute-start | bytes 4128776 | tf_op jit(solution)/shard_map/ppermute | solution.py:38
  65.4 18.7 %collective-permute-start.16 = (bf16[2,2,2,224,256]{4,3,2,1,0:T(8,128)(2,1)}, bf16[2,2,2,224,256]{4,3,2,1,0:T(8,128)(2,1)}, u32[]{:S(2)}, u32[]{:S(2)}) collective-permute-start(bf16[2,2,2,224,256]{4,3,2,1,0:T(8,128)(2,1)} %get-tuple-element.94), channel_id=1, source_target_pairs={{0,64},{64,0},{1,65},{65,1},{2,66},{66,2},{3,67},{67,3},{4,68},{68... | collective-permute-start | bytes 2752520 | tf_op jit(solution)/shard_map/ppermute | solution.py:38
  67.1 13.0 %collective-permute-start.17 = (f32[2,224,256]{2,1,0:T(8,128)S(1)}, f32[2,224,256]{2,1,0:T(8,128)S(1)}, u32[]{:S(2)}, u32[]{:S(2)}) collective-permute-start(f32[2,224,256]{2,1,0:T(8,128)S(1)} %pad_maximum_fusion.12), channel_id=1, source_target_pairs={{0,65},{64,1},{1,64},{65,0},{2,67},{66,3},{3,66},{67,2},{4,69},{68... | collective-permute-start | bytes 1376264 | tf_op jit(solution)/shard_map/ppermute | solution.py:38
  85.9 11.5 %collective-permute-start.20 = (bf16[2,3,224,256]{3,2,1,0:T(8,128)(2,1)S(1)}, bf16[2,3,224,256]{3,2,1,0:T(8,128)(2,1)S(1)}, u32[]{:S(2)}, u32[]{:S(2)}) collective-permute-start(bf16[2,3,224,256]{3,2,1,0:T(8,128)(2,1)S(1)} %get-tuple-element.134), channel_id=1, source_target_pairs={{0,64},{64,0},{1,65},{65,1},{2,66},{66,2},{3,67},{67,3},{4,68},{68... | collective-permute-start | bytes 2064392 | tf_op jit(solution)/shard_map/ppermute | solution.py:38
  87.3 8.6 %collective-permute-start.22 = (bf16[2,2,224,256]{3,2,1,0:T(8,128)(2,1)S(1)}, bf16[2,2,224,256]{3,2,1,0:T(8,128)(2,1)S(1)}, u32[]{:S(2)}, u32[]{:S(2)}) collective-permute-start(bf16[2,2,224,256]{3,2,1,0:T(8,128)(2,1)S(1)} %get-tuple-element.136), channel_id=1, source_target_pairs={{0,2},{64,66},{1,3},{65,67},{2,0},{66,64},{3,1},{67,65},{4,6},{68,... | collective-permute-start | bytes 1376264 | tf_op jit(solution)/shard_map/ppermute | solution.py:38
  89.9 11.1 %collective-permute-start.18 = (bf16[2,3,224,256]{3,2,1,0:T(8,128)(2,1)S(1)}, bf16[2,3,224,256]{3,2,1,0:T(8,128)(2,1)S(1)}, u32[]{:S(2)}, u32[]{:S(2)}) collective-permute-start(bf16[2,3,224,256]{3,2,1,0:T(8,128)(2,1)S(1)} %get-tuple-element.132), channel_id=1, source_target_pairs={{0,8},{64,72},{1,9},{65,73},{2,10},{66,74},{3,11},{67,75},{4,12},{... | collective-permute-start | bytes 2064392 | tf_op jit(solution)/shard_map/ppermute | solution.py:38
  96.0 7.4 %collective-permute-start.23 = (bf16[2,224,256]{2,1,0:T(8,128)(2,1)S(1)}, bf16[2,224,256]{2,1,0:T(8,128)(2,1)S(1)}, u32[]{:S(2)}, u32[]{:S(2)}) collective-permute-start(bf16[2,224,256]{2,1,0:T(8,128)(2,1)S(1)} %fusion.34), channel_id=1, source_target_pairs={{0,8},{64,72},{1,9},{65,73},{2,10},{66,74},{3,11},{67,75},{4,12},{... | collective-permute-start | bytes 688136 | tf_op jit(solution)/shard_map/ppermute | solution.py:38
  97.5 7.4 %collective-permute-start.21 = (bf16[3,224,256]{2,1,0:T(8,128)(2,1)S(1)}, bf16[3,224,256]{2,1,0:T(8,128)(2,1)S(1)}, u32[]{:S(2)}, u32[]{:S(2)}) collective-permute-start(bf16[3,224,256]{2,1,0:T(8,128)(2,1)S(1)} %fusion.32), channel_id=1, source_target_pairs={{0,2},{64,66},{1,3},{65,67},{2,0},{66,64},{3,1},{67,65},{4,6},{68,... | collective-permute-start | bytes 1032200 | tf_op jit(solution)/shard_map/ppermute | solution.py:38
  101.1 7.4 %collective-permute-start.19 = (bf16[3,224,256]{2,1,0:T(8,128)(2,1)S(1)}, bf16[3,224,256]{2,1,0:T(8,128)(2,1)S(1)}, u32[]{:S(2)}, u32[]{:S(2)}) collective-permute-start(bf16[3,224,256]{2,1,0:T(8,128)(2,1)S(1)} %fusion.30), channel_id=1, source_target_pairs={{0,64},{64,0},{1,65},{65,1},{2,66},{66,2},{3,67},{67,3},{4,68},{68... | collective-permute-start | bytes 1032200 | tf_op jit(solution)/shard_map/ppermute | solution.py:38
  105.1 7.7 %collective-permute-start.24 = (bf16[2,2,224,256]{3,2,1,0:T(8,128)(2,1)S(1)}, bf16[2,2,224,256]{3,2,1,0:T(8,128)(2,1)S(1)}, u32[]{:S(2)}, u32[]{:S(2)}) collective-permute-start(bf16[2,2,224,256]{3,2,1,0:T(8,128)(2,1)S(1)} %bitcast.162), channel_id=1, source_target_pairs={{0,24},{64,88},{1,25},{65,89},{2,26},{66,90},{3,27},{67,91},{4,28}... | collective-permute-start | bytes 1376264 | tf_op jit(solution)/shard_map/ppermute | solution.py:38
  112.9 5.0 %collective-permute-start.25 = (bf16[2,224,256]{2,1,0:T(8,128)(2,1)S(1)}, bf16[2,224,256]{2,1,0:T(8,128)(2,1)S(1)}, u32[]{:S(2)}, u32[]{:S(2)}) collective-permute-start(bf16[2,224,256]{2,1,0:T(8,128)(2,1)S(1)} %get-tuple-element.140), channel_id=1, source_target_pairs={{0,6},{64,70},{1,7},{65,71},{2,4},{66,68},{3,5},{67,69},{4,2},{68,... | collective-permute-start | bytes 688136 | tf_op jit(solution)/shard_map/ppermute | solution.py:38
  117.9 5.0 %collective-permute-start.26 = (bf16[2,224,256]{2,1,0:T(8,128)(2,1)S(1)}, bf16[2,224,256]{2,1,0:T(8,128)(2,1)S(1)}, u32[]{:S(2)}, u32[]{:S(2)}) collective-permute-start(bf16[2,224,256]{2,1,0:T(8,128)(2,1)S(1)} %pad_maximum_fusion.21), channel_id=1, source_target_pairs={{0,65},{64,1},{1,64},{65,0},{2,67},{66,3},{3,66},{67,2},{4,69},{68... | collective-permute-start | bytes 688136 | tf_op jit(solution)/shard_map/ppermute | solution.py:38
  123.3 11.2 %collective-permute-start.28 = (bf16[224,256]{1,0:T(8,128)(2,1)S(1)}, bf16[224,256]{1,0:T(8,128)(2,1)S(1)}, u32[]{:S(2)}, u32[]{:S(2)}) collective-permute-start(bf16[224,256]{1,0:T(8,128)(2,1)S(1)} %slice_bitcast_fusion.10), channel_id=1, source_target_pairs={{0,32},{64,96},{1,33},{65,97},{2,34},{66,98},{3,35},{67,99},{4,36}... | collective-permute-start | bytes 344072 | tf_op jit(solution)/shard_map/ppermute | solution.py:38
  130.8 7.1 %collective-permute-start.27 = (bf16[2,224,256]{2,1,0:T(8,128)(2,1)S(1)}, bf16[2,224,256]{2,1,0:T(8,128)(2,1)S(1)}, u32[]{:S(2)}, u32[]{:S(2)}) collective-permute-start(bf16[2,224,256]{2,1,0:T(8,128)(2,1)S(1)} %get-tuple-element.106), channel_id=1, source_target_pairs={{0,6},{64,70},{1,7},{65,71},{2,4},{66,68},{3,5},{67,69},{4,2},{68,... | collective-permute-start | bytes 688136 | tf_op jit(solution)/shard_map/ppermute | solution.py:38
  137.9 7.7 %collective-permute-start.29 = (bf16[2,2,224,256]{3,2,1,0:T(8,128)(2,1)S(1)}, bf16[2,2,224,256]{3,2,1,0:T(8,128)(2,1)S(1)}, u32[]{:S(2)}, u32[]{:S(2)}) collective-permute-start(bf16[2,2,224,256]{3,2,1,0:T(8,128)(2,1)S(1)} %pad_maximum_fusion.13), channel_id=1, source_target_pairs={{0,24},{64,88},{1,25},{65,89},{2,26},{66,90},{3,27},{67,91},{4,28}... | collective-permute-start | bytes 1376264 | tf_op jit(solution)/shard_map/ppermute | solution.py:38
  138.8 5.2 %collective-permute-start.30 = (bf16[224,512]{1,0:T(8,128)(2,1)S(1)}, bf16[224,512]{1,0:T(8,128)(2,1)S(1)}, u32[]{:S(2)}, u32[]{:S(2)}) collective-permute-start(bf16[224,512]{1,0:T(8,128)(2,1)S(1)} %maximum_select_fusion.1), channel_id=1, source_target_pairs={{0,64},{64,0},{1,65},{65,1},{2,66},{66,2},{3,67},{67,3},{4,68},{68... | collective-permute-start | bytes 688136 | tf_op jit(solution)/shard_map/ppermute | solution.py:38
  145.8 12.1 %collective-permute-start.31 = (bf16[3,224,256]{2,1,0:T(8,128)(2,1)S(1)}, bf16[3,224,256]{2,1,0:T(8,128)(2,1)S(1)}, u32[]{:S(2)}, u32[]{:S(2)}) collective-permute-start(bf16[3,224,256]{2,1,0:T(8,128)(2,1)S(1)} %get-tuple-element.112), channel_id=1, source_target_pairs={{0,64},{64,0},{1,65},{65,1},{2,66},{66,2},{3,67},{67,3},{4,68},{68... | collective-permute-start | bytes 1032200 | tf_op jit(solution)/shard_map/ppermute | solution.py:38
  148.8 9.0 %collective-permute-start.32 = (bf16[3,224,256]{2,1,0:T(8,128)(2,1)S(1)}, bf16[3,224,256]{2,1,0:T(8,128)(2,1)S(1)}, u32[]{:S(2)}, u32[]{:S(2)}) collective-permute-start(bf16[3,224,256]{2,1,0:T(8,128)(2,1)S(1)} %get-tuple-element.114), channel_id=1, source_target_pairs={{0,2},{64,66},{1,3},{65,67},{2,0},{66,64},{3,1},{67,65},{4,6},{68,... | collective-permute-start | bytes 1032200 | tf_op jit(solution)/shard_map/ppermute | solution.py:38
  151.5 6.4 %collective-permute-start.33 = (bf16[2,224,256]{2,1,0:T(8,128)(2,1)S(1)}, bf16[2,224,256]{2,1,0:T(8,128)(2,1)S(1)}, u32[]{:S(2)}, u32[]{:S(2)}) collective-permute-start(bf16[2,224,256]{2,1,0:T(8,128)(2,1)S(1)} %slice.209), channel_id=1, source_target_pairs={{0,8},{64,72},{1,9},{65,73},{2,10},{66,74},{3,11},{67,75},{4,12},{... | collective-permute-start | bytes 688136 | tf_op jit(solution)/shard_map/ppermute | solution.py:38
  157.9 11.7 %collective-permute-start.35 = (bf16[2,3,224,256]{3,2,1,0:T(8,128)(2,1)S(1)}, bf16[2,3,224,256]{3,2,1,0:T(8,128)(2,1)S(1)}, u32[]{:S(2)}, u32[]{:S(2)}) collective-permute-start(bf16[2,3,224,256]{3,2,1,0:T(8,128)(2,1)S(1)} %pad_maximum_fusion.7), channel_id=1, source_target_pairs={{0,64},{64,0},{1,65},{65,1},{2,66},{66,2},{3,67},{67,3},{4,68},{68... | collective-permute-start | bytes 2064392 | tf_op jit(solution)/shard_map/ppermute | solution.py:38
  158.2 11.4 %collective-permute-start.34 = (bf16[2,3,224,256]{3,2,1,0:T(8,128)(2,1)S(1)}, bf16[2,3,224,256]{3,2,1,0:T(8,128)(2,1)S(1)}, u32[]{:S(2)}, u32[]{:S(2)}) collective-permute-start(bf16[2,3,224,256]{3,2,1,0:T(8,128)(2,1)S(1)} %pad_maximum_fusion.6), channel_id=1, source_target_pairs={{0,8},{64,72},{1,9},{65,73},{2,10},{66,74},{3,11},{67,75},{4,12},{... | collective-permute-start | bytes 2064392 | tf_op jit(solution)/shard_map/ppermute | solution.py:38
  161.0 8.6 %collective-permute-start.36 = (bf16[2,2,224,256]{3,2,1,0:T(8,128)(2,1)S(1)}, bf16[2,2,224,256]{3,2,1,0:T(8,128)(2,1)S(1)}, u32[]{:S(2)}, u32[]{:S(2)}) collective-permute-start(bf16[2,2,224,256]{3,2,1,0:T(8,128)(2,1)S(1)} %pad_maximum_fusion.14), channel_id=1, source_target_pairs={{0,2},{64,66},{1,3},{65,67},{2,0},{66,64},{3,1},{67,65},{4,6},{68,... | collective-permute-start | bytes 1376264 | tf_op jit(solution)/shard_map/ppermute | solution.py:38
  169.7 18.5 %collective-permute-start.38 = (bf16[2,2,3,224,256]{4,3,2,1,0:T(8,128)(2,1)S(1)}, bf16[2,2,3,224,256]{4,3,2,1,0:T(8,128)(2,1)S(1)}, u32[]{:S(2)}, u32[]{:S(2)}) collective-permute-start(bf16[2,2,3,224,256]{4,3,2,1,0:T(8,128)(2,1)S(1)} %pad_maximum_fusion.1.refs_1_), channel_id=1, source_target_pairs={{0,8},{64,72},{1,9},{65,73},{2,10},{66,74},{3,11},{67,75},{4,12},{... | collective-permute-start | bytes 4128776 | tf_op jit(solution)/shard_map/ppermute | solution.py:38
  172.3 18.7 %collective-permute-start.37 = (bf16[2,2,3,224,256]{4,3,2,1,0:T(8,128)(2,1)S(1)}, bf16[2,2,3,224,256]{4,3,2,1,0:T(8,128)(2,1)S(1)}, u32[]{:S(2)}, u32[]{:S(2)}) collective-permute-start(bf16[2,2,3,224,256]{4,3,2,1,0:T(8,128)(2,1)S(1)} %pad_maximum_fusion.refs_0_), channel_id=1, source_target_pairs={{0,2},{64,66},{1,3},{65,67},{2,0},{66,64},{3,1},{67,65},{4,6},{68,... | collective-permute-start | bytes 4128776 | tf_op jit(solution)/shard_map/ppermute | solution.py:38
  173.8 17.7 %copy-start.6 = (bf16[256,512]{1,0:T(8,128)(2,1)S(1)}, bf16[256,512]{1,0:T(8,128)(2,1)}, u32[]{:S(2)}) copy-start(bf16[256,512]{1,0:T(8,128)(2,1)} %param.7) | copy-start | bytes 786436
  173.8 17.7 %copy-start.5 = (f32[448,512]{1,0:T(8,128)S(1)}, f32[448,512]{1,0:T(8,128)}, u32[]{:S(2)}) copy-start(f32[448,512]{1,0:T(8,128)} %param.8) | copy-start | bytes 2752516
  174.6 2.8 %collective-permute-start.45 = (bf16[2,2,2,224,256]{4,3,2,1,0:T(8,128)(2,1)S(1)}, bf16[2,2,2,224,256]{4,3,2,1,0:T(8,128)(2,1)S(1)}, u32[]{:S(2)}, u32[]{:S(2)}) collective-permute-start(bf16[2,2,2,224,256]{4,3,2,1,0:T(8,128)(2,1)S(1)} %pad_maximum_fusion.3.refs_2_), channel_id=1, source_target_pairs={{0,32},{64,96},{1,33},{65,97},{2,34},{66,98},{3,35},{67,99},{4,36}... | collective-permute-start | bytes 2752520 | tf_op jit(solution)/shard_map/ppermute | solution.py:38
  174.7 16.2 %collective-permute-start.39 = (bf16[2,2,2,224,256]{4,3,2,1,0:T(8,128)(2,1)S(1)}, bf16[2,2,2,224,256]{4,3,2,1,0:T(8,128)(2,1)S(1)}, u32[]{:S(2)}, u32[]{:S(2)}) collective-permute-start(bf16[2,2,2,224,256]{4,3,2,1,0:T(8,128)(2,1)S(1)} %pad_maximum_fusion.3.refs_2_), channel_id=1, source_target_pairs={{0,64},{64,0},{1,65},{65,1},{2,66},{66,2},{3,67},{67,3},{4,68},{68... | collective-permute-start | bytes 2752520 | tf_op jit(solution)/shard_map/ppermute | solution.py:38
  177.4 16.5 %collective-permute-start.43 = (bf16[2,2,3,224,256]{4,3,2,1,0:T(8,128)(2,1)S(1)}, bf16[2,2,3,224,256]{4,3,2,1,0:T(8,128)(2,1)S(1)}, u32[]{:S(2)}, u32[]{:S(2)}) collective-permute-start(bf16[2,2,3,224,256]{4,3,2,1,0:T(8,128)(2,1)S(1)} %pad_maximum_fusion.refs_0_), channel_id=1, source_target_pairs={{0,32},{64,96},{1,33},{65,97},{2,34},{66,98},{3,35},{67,99},{4,36}... | collective-permute-start | bytes 4128776 | tf_op jit(solution)/shard_map/ppermute | solution.py:38
  177.4 16.5 %collective-permute-start.44 = (bf16[2,2,3,224,256]{4,3,2,1,0:T(8,128)(2,1)S(1)}, bf16[2,2,3,224,256]{4,3,2,1,0:T(8,128)(2,1)S(1)}, u32[]{:S(2)}, u32[]{:S(2)}) collective-permute-start(bf16[2,2,3,224,256]{4,3,2,1,0:T(8,128)(2,1)S(1)} %pad_maximum_fusion.1.refs_1_), channel_id=1, source_target_pairs={{0,32},{64,96},{1,33},{65,97},{2,34},{66,98},{3,35},{67,99},{4,36}... | collective-permute-start | bytes 4128776 | tf_op jit(solution)/shard_map/ppermute | solution.py:38
  188.2 7.2 %collective-permute-start.41 = (bf16[2,2,3,224,256]{4,3,2,1,0:T(8,128)(2,1)S(1)}, bf16[2,2,3,224,256]{4,3,2,1,0:T(8,128)(2,1)S(1)}, u32[]{:S(2)}, u32[]{:S(2)}) collective-permute-start(bf16[2,2,3,224,256]{4,3,2,1,0:T(8,128)(2,1)S(1)} %collective-permute-done.38.refs_1_), channel_id=1, source_target_pairs={{0,32},{64,96},{1,33},{65,97},{2,34},{66,98},{3,35},{67,99},{4,36}... | collective-permute-start | bytes 4128776 | tf_op jit(solution)/shard_map/ppermute | solution.py:38
  190.9 4.4 %collective-permute-start.40 = (bf16[2,2,3,224,256]{4,3,2,1,0:T(8,128)(2,1)S(1)}, bf16[2,2,3,224,256]{4,3,2,1,0:T(8,128)(2,1)S(1)}, u32[]{:S(2)}, u32[]{:S(2)}) collective-permute-start(bf16[2,2,3,224,256]{4,3,2,1,0:T(8,128)(2,1)S(1)} %collective-permute-done.37.refs_0_), channel_id=1, source_target_pairs={{0,32},{64,96},{1,33},{65,97},{2,34},{66,98},{3,35},{67,99},{4,36}... | collective-permute-start | bytes 4128776 | tf_op jit(solution)/shard_map/ppermute | solution.py:38
  190.9 4.4 %collective-permute-start.42 = (bf16[2,2,2,224,256]{4,3,2,1,0:T(8,128)(2,1)S(1)}, bf16[2,2,2,224,256]{4,3,2,1,0:T(8,128)(2,1)S(1)}, u32[]{:S(2)}, u32[]{:S(2)}) collective-permute-start(bf16[2,2,2,224,256]{4,3,2,1,0:T(8,128)(2,1)S(1)} %collective-permute-done.39.refs_2_), channel_id=1, source_target_pairs={{0,32},{64,96},{1,33},{65,97},{2,34},{66,98},{3,35},{67,99},{4,36}... | collective-permute-start | bytes 2752520 | tf_op jit(solution)/shard_map/ppermute | solution.py:38
  (7 other events, 34.1 us)

commit v4 on v3

--- a/solution.py
+++ b/solution.py
@@ -38,9 +38,10 @@
     return lax.ppermute(arr, AXES, pairs)
 
 
-def swap(arr, axis, late=0):
+def swap(arr, axes, late=0):
     def move(co):
-        co[axis] ^= 3 if co["c"] != late else 1
+        for axis in axes:
+            co[axis] ^= 3 if co["c"] != late else 1
         return co
 
     return permute(arr, move)
@@ -73,13 +74,14 @@
 
 def gather(piece, beside):
     tied = ()
-    for axis in "zxy"[piece.ndim - 2 :]:
-        got = swap(piece, axis, late=1)
-        if beside:
-            tied = beside[0](*tied)
-        (piece,), *tied = join([piece], [got], *tied)
-        beside = beside[1:]
-    piece = piece.reshape(8, *piece.shape[3:])
+    if piece.ndim == 2:
+        ((piece,),) = join([piece], [swap(piece, "z", late=1)])
+    gots = [swap(piece, axes, late=1) for axes in ("x", "y", "xy")]
+    if beside:
+        tied = beside[0](*tied)
+    blocks = lax.optimization_barrier((piece, *gots, *tied))
+    tied, beside = blocks[4:], beside[1:]
+    piece = jnp.concatenate(blocks[:4])
     parts = [piece[begin:end] for begin, end in PARTS]
     for stage in (2, 1):
         gots = [swap(part, order[stage]) for order, part in zip(ORDERS, parts)]
@@ -194,73 +196,43 @@
     )(a0, a1, whole)
 
 
-def partials(g0, g1, p0, p1, pos, keeps=None):
+def partials(g0, g1, p0, p1, pos):
     tok, ffw = g0.shape
     cols = p0.shape[1]
     nb = ffw // 16
     rows = nb // 4
 
-    def sent(u, v):
-        return u[ORDERS[part_of(v)[0]][0]]
-
-    runs = [run for run in chips() if any(sent(u, v) for u, v in run) == (keeps is None)]
-
     def kernel(pos_ref, g0_ref, g1_ref, p0_ref, p1_ref, *refs):
+        outs, scratch = refs[:6], refs[6]
         dims = (((0,), (0,)), ((), ()))
-        columns = []
-        for run in runs:
+        for i, run in enumerate(chips()):
             y, x = (absolute(*run[0], a, pos_ref, pos_ref[3]) for a in "yx")
-            columns.append(pl.ds(pl.multiple_of((y * 4 + x) * nb, nb), nb))
-        if keeps is None:
-            *send_refs, keep_x, keep_y, keep_z, scratch = refs
-            keep_refs = keep_x, keep_y, keep_z
-        else:
-            *_, keep_x, keep_y, keep_z, scratch, held, sem = refs
-            keep_refs = keep_x, keep_y, keep_z
-            copies = [
-                [pltpu.make_async_copy(g.at[:, at], held.at[i, j], sem.at[i, j]) for j, g in enumerate((g0_ref, g1_ref))]
-                for i, at in enumerate(columns)
-            ]
-            for copy in itertools.chain(*copies):
-                copy.start()
-        for i, (run, at) in enumerate(zip(runs, columns)):
-            if keeps is None:
-                terms = g0_ref[:, at], g1_ref[:, at]
-            else:
-                for copy in copies[i]:
-                    copy.wait()
-                terms = held[i, 0], held[i, 1]
+            at = pl.ds(pl.multiple_of((y * 4 + x) * nb, nb), nb)
             scratch[i % 2] = (
                 (
-                    lax.dot_general(terms[0], p0_ref[...], dims, preferred_element_type=F32)
-                    + lax.dot_general(terms[1], p1_ref[...], dims, preferred_element_type=F32)
+                    lax.dot_general(g0_ref[:, at], p0_ref[...], dims, preferred_element_type=F32)
+                    + lax.dot_general(g1_ref[:, at], p1_ref[...], dims, preferred_element_type=F32)
                 )
                 .astype(BF)
                 .reshape(4, rows, cols)
             )
             for u, v in run:
                 part, w = part_of(v)
-                _, second, third = (u[a] for a in ORDERS[part])
-                outs = send_refs if sent(u, v) else keep_refs
-                outs[part][second, third, w] = scratch[i % 2, absolute(u, v, "z", pos_ref, pos_ref[3])]
-
-    shapes = [(2, 2, end - begin, rows, cols) for begin, end in PARTS] * (2 if keeps is None else 1)
-    share = len(runs) / 16
+                first, second, third = (u[a] for a in ORDERS[part])
+                outs[2 * part + first][second, third, w] = scratch[i % 2, absolute(u, v, "z", pos_ref, pos_ref[3])]
+
+    shapes = [(2, 2, end - begin, rows, cols) for begin, end in PARTS for _ in range(2)]
     return pl.pallas_call(
         kernel,
         out_shape=[jax.ShapeDtypeStruct(s, BF) for s in shapes],
-        in_specs=[SMEM] + ([VMEM] * 4 if keeps is None else [HBM] * 2 + [VMEM] * 5),
-        out_specs=[VMEM] * len(shapes),
-        input_output_aliases={} if keeps is None else {5: 0, 6: 1, 7: 2},
-        scratch_shapes=[pltpu.VMEM((2, 4, rows, cols), BF)]
-        + ([] if keeps is None else [pltpu.VMEM((len(runs), 2, tok, nb), BF), pltpu.SemaphoreType.DMA((len(runs), 2))]),
-        compiler_params=pltpu.CompilerParams(vmem_limit_bytes=(6 if keeps is None else 12) * 2**20),
+        in_specs=[SMEM] + [VMEM] * 4,
+        out_specs=[VMEM] * 6,
+        scratch_shapes=[pltpu.VMEM((2, 4, rows, cols), BF)],
+        compiler_params=pltpu.CompilerParams(vmem_limit_bytes=24 * 2**20),
         cost_estimate=pl.CostEstimate(
-            flops=int(4 * tok * ffw * cols * share),
-            bytes_accessed=int((4 * tok * ffw + 2 * ffw * cols) * share),
-            transcendentals=0,
+            flops=4 * tok * ffw * cols, bytes_accessed=4 * tok * ffw + 2 * ffw * cols, transcendentals=0
         ),
-    )(pos, g0, g1, p0, p1, *(keeps or ()))
+    )(pos, g0, g1, p0, p1)
 
 
 def updates(basis, own, other, core):
@@ -316,25 +288,25 @@
     act_other = swap_core(activations)
     g_other = swap_core(out_grads)
 
+    at = (zl * shard, core * half)
+    moments = jnp.stack([lax.dynamic_slice(m, at, (shard, half)) for m in (first_moment, second_moment)])
+
     mine, theirs = pos[3:], 1 - pos[3:]
-    swapped = [lambda: ()] * 4 + [lambda: (act_other, g_other)]
-    near, far, (act_other, g_other) = gather(
+    swapped = [lambda: ()] * 2 + [lambda: (act_other, g_other, moments)]
+    near, far, (act_other, g_other, moments) = gather(
         lax.dynamic_slice(basis, (zl * brows, core * half), (brows, half)), swapped
     )
     whole = place(place(None, near, 0, pos, mine), far, 1, pos, mine)
     near_acts = load(activations, act_other)
-    near_gs = load(out_grads, g_other)
-    terms = (*project(*near_acts, whole), pos)
-    *sends, keep_x, keep_y, keep_z = partials(*near_gs, *terms)
-    keeps = partials(out_grads, g_other, *terms, [keep_x, keep_y, keep_z])
-
-    at = (zl * shard, core * half)
-    moments = [lax.dynamic_slice(m, at, (shard, half)) for m in (first_moment, second_moment)]
-    moments = lax.optimization_barrier((jnp.stack(moments), *sends))[0]
+    projected = project(*near_acts, whole)
+    sums = partials(out_grads, g_other, *projected, pos)
+    keeps, sends = sums[0::2], sums[1::2]
+
+    moments = lax.optimization_barrier((moments, projected[0]))[0]
 
     for stage in range(3):
         gots = [swap(send, order[stage]) for order, send in zip(ORDERS, sends)]
-        if stage == 0:
+        if stage == 1:
             *gots, theirs_moments = lax.optimization_barrier((*gots, swap(moments, "z", late=1)))
         if stage < 2:
             sends = [add(keep[1], got[1]) for keep, got in zip(keeps, gots)]
@@ -342,12 +314,8 @@
         else:
             keeps = [add(keep, got) for keep, got in zip(keeps, gots)]
     keep = jnp.concatenate(keeps).reshape(2, 2, 2, shard, half)
-    keep, send = keep[0], keep[1]
-    for axis in "yx":
-        got = swap(send, axis, late=1)
-        send = add(keep[1], got[1])
-        keep = add(keep[0], got[0])
-    keep = jnp.stack([keep, send])
+    gots = [swap(keep[vy, vx], axes, late=1) for vy, vx, axes in ((0, 1, "x"), (1, 0, "y"), (1, 1, "xy"))]
+    keep = sum(term.astype(F32) for term in (keep[0, 0], *gots)).astype(BF)
     blocks = add(keep, swap(keep, "z", late=1)[::-1])
     reduced = blocks[0]
 

time: 202 us -> 193 us (0.955)
  Pallas kernels: 29.8 us -> 23.7 us
  local copies, waits for them, and re-layouts: 9.2 us -> 4.9 us
  waiting for transfers between devices: 82.6 us -> 86.4 us
  other arithmetic: 8.98 us -> 5.89 us
    unnamed x18, local copies, waits for them, and re-layouts: 7.07 us -> 2.9 us
    convert_element_type x11 -> x9, other arithmetic: 5.57 us -> 1.66 us  [add(): return (a.astype(F32) + b.astype(F32)).astype(BF)]
    ppermute x46 -> x49, waiting for transfers between devices: 82.6 us -> 86.4 us  [permute(): return lax.ppermute(arr, AXES, pairs)]
    pallas_call x2 -> x1, Pallas kernels: 6.38 us -> 2.52 us  [load(): pl.pallas_call(kernel, out_shape=[jax.ShapeDtypeStruct(a.shape, a.dtype)...]
    pallas_call x2 -> x1, Pallas kernels: 10.5 us -> 7.95 us  [partials(): pl.pallas_call(kernel, out_shape=[jax.ShapeDtypeStruct(s, BF) for s in sh...]
    ppermute x46 -> x49, starting transfers between devices: 70 us -> 71 us  [permute(): return lax.ppermute(arr, AXES, pairs)]
  transfers between devices with their start and end apart: 46 -> 49, of which waited for: 23 -> 27; matrix products, arithmetic and copies ran while one was open for 4% -> 3% of each run, Pallas kernels for 7% -> 3%
where the time goes in v4:
time: 193 us
  waiting for transfers between devices  86.4 us (45%)
  starting transfers between devices  71 us (37%)
  Pallas kernels  23.7 us (12%)
  other arithmetic  5.89 us (3%)
  local copies, waits for them, and re-layouts  4.9 us (3%)
    ppermute x49, waiting for transfers between devices, permute(): return lax.ppermute(arr, AXES, pairs)  86.4 us
    ppermute x49, starting transfers between devices, permute(): return lax.ppermute(arr, AXES, pairs)  71 us
    pallas_call x1, Pallas kernels, partials(): pl.pallas_call(kernel, out_shape=[jax.ShapeDtypeStruct(s, BF) for s in sh...  7.95 us
    pallas_call x1, Pallas kernels, updates(): pl.pallas_call(kernel, out_shape=jax.ShapeDtypeStruct((rows, ffw), BF), i...  5.57 us
    pallas_call x6, Pallas kernels, place(): pl.pallas_call(kernel, out_shape=jax.ShapeDtypeStruct((64, rows, cols), B...  5.3 us
  transfers between devices with their start and end apart: 49, of which 27 were waited for; matrix products, arithmetic and copies ran while one was open for 3% of the time, Pallas kernels for 3%

profile of v4, /device:TPU:1, one launch (start us, length us, event | category | flops | bytes accessed | tf_op | source)
XLA Modules:
  0.0 193.1 jit_solution(13824166384991450504)
XLA Ops:
  0.6 1.5 collective-permute-start.11
  3.1 1.7 collective-permute-start
  4.8 1.7 collective-permute-done
  10.4 2.0 %collective-permute-done.2 = bf16[2,128,256]{2,1,0:T(8,128)(2,1)S(1)} collective-permute-done((bf16[2,128,256]{2,1,0:T(8,128)(2,1)S(1)}, bf16[2,128,256]{2,1,0:T(8,128)(2,1)S(1)}, u32[]{:S(2)}, u32[]{:S(2)}) %collective-permute-start.2) | collective-permute-done | bytes 131104 | tf_op jit(solution)/shard_map/ppermute | solution.py:38
  13.8 4.0 %collective-permute-start.4 = (bf16[3,128,256]{2,1,0:T(8,128)(2,1)S(1)}, bf16[3,128,256]{2,1,0:T(8,128)(2,1)S(1)}, u32[]{:S(2)}, u32[]{:S(2)}) collective-permute-start(bf16[3,128,256]{2,1,0:T(8,128)(2,1)S(1)} %get-tuple-element.67), channel_id=1, source_target_pairs={{0,64},{64,0},{1,65},{65,1},{2,66},{66,2},{3,67},{67,3},{4,68},{68... | collective-permute-start | bytes 589832 | tf_op jit(solution)/shard_map/ppermute | solution.py:38
  17.8 1.5 collective-permute-start.5
  19.3 1.9 %collective-permute-start.6 = (bf16[2,128,256]{2,1,0:T(8,128)(2,1)S(1)}, bf16[2,128,256]{2,1,0:T(8,128)(2,1)S(1)}, u32[]{:S(2)}, u32[]{:S(2)}) collective-permute-start(bf16[2,128,256]{2,1,0:T(8,128)(2,1)S(1)} %collective-permute-done.3), channel_id=1, source_target_pairs={{0,8},{64,72},{1,9},{65,73},{2,10},{66,74},{3,11},{67,75},{4,12},{... | collective-permute-start | bytes 393224 | tf_op jit(solution)/shard_map/ppermute | solution.py:38
  21.2 3.6 %collective-permute-done.6 = bf16[2,128,256]{2,1,0:T(8,128)(2,1)S(1)} collective-permute-done((bf16[2,128,256]{2,1,0:T(8,128)(2,1)S(1)}, bf16[2,128,256]{2,1,0:T(8,128)(2,1)S(1)}, u32[]{:S(2)}, u32[]{:S(2)}) %collective-permute-start.6) | collective-permute-done | bytes 131104 | tf_op jit(solution)/shard_map/ppermute | solution.py:38
  24.9 1.5 collective-permute-start.7
  26.4 1.5 collective-permute-start.8
  30.7 3.8 %collective-permute-done.9 = bf16[2,2,128,256]{3,2,1,0:T(8,128)(2,1)S(1)} collective-permute-done((bf16[2,2,128,256]{3,2,1,0:T(8,128)(2,1)S(1)}, bf16[2,2,128,256]{3,2,1,0:T(8,128)(2,1)S(1)}, u32[]{:S(2)}, u32[]{:S(2)}) %collective-permute-start.9) | collective-permute-done | bytes 262176 | tf_op jit(solution)/shard_map/ppermute | solution.py:38
  37.0 1.8 collective-permute-start.14
  38.9 2.2 %copy-done = bf16[256,8192]{1,0:T(8,128)(2,1)S(1)} copy-done((bf16[256,8192]{1,0:T(8,128)(2,1)S(1)}, bf16[256,8192]{1,0:T(8,128)(2,1)}, u32[]{:S(2)}) %copy-start) | copy-done | bytes 4194328
  41.1 2.5 %shard_map.76 = (bf16[256,8192]{1,0:T(8,128)(2,1)S(1)}, bf16[256,8192]{1,0:T(8,128)(2,1)S(1)}) custom-call(bf16[256,8192]{1,0:T(8,128)(2,1)S(1)} %copy-done, bf16[256,8192]{1,0:T(8,128)(2,1)} %collective-permute-done.10.refs_1_), custom_call_target="tpu_custom_call" | custom-call | bytes 8388608 | tf_op jit(solution)/shard_map/pallas_call | solution.py:166
  44.3 2.1 %collective-permute-done.14.refs_2_ = bf16[2,2,2,128,256]{4,3,2,1,0:T(8,128)(2,1)S(1)} collective-permute-done((bf16[2,2,2,128,256]{4,3,2,1,0:T(8,128)(2,1)S(1)}, bf16[2,2,2,128,256]{4,3,2,1,0:T(8,128)(2,1)S(1)}, u32[]{:S(2)}, u32[]{:S(2)}) %collective-permute-start.14) | collective-permute-done | bytes 524320 | tf_op jit(solution)/shard_map/ppermute | solution.py:38
  49.9 2.3 %shard_map.79 = (bf16[256,256]{1,0:T(8,128)(2,1)S(1)}, bf16[256,256]{1,0:T(8,128)(2,1)S(1)}) custom-call(bf16[256,8192]{1,0:T(8,128)(2,1)S(1)} %get-tuple-element.75.a0_ref, bf16[256,8192]{1,0:T(8,128)(2,1)S(1)} %get-tuple-element.76.a1_ref, bf16[64,128,256]{2,1,0:T(8,128)(2,1)S(1)} %shard_map.78.b_ref), custom_call_target="tpu_custom_call" | custom-call | flops 2147483648 | bytes 12582912 | tf_op jit(solution)/shard_map/pallas_call | solution.py:187
  52.3 8.0 %shard_map.80 = (bf16[2,2,3,224,256]{4,3,2,1,0:T(8,128)(2,1)S(1)}, bf16[2,2,3,224,256]{4,3,2,1,0:T(8,128)(2,1)S(1)}, bf16[2,2,3,224,256]{4,3,2,1,0:T(8,128)(2,1)...) custom-call(s32[4]{0:T(128)S(1)} %pad_add_fusion.pos_ref, ...), custom_call_target="tpu_custom_call" | custom-call | flops 3758096384 | bytes 22020096 | tf_op jit(solution)/shard_map/pallas_call | solution.py:225
  60.3 2.2 %collective-permute-start.15 = (bf16[2,2,3,224,256]{4,3,2,1,0:T(8,128)(2,1)S(1)}, bf16[2,2,3,224,256]{4,3,2,1,0:T(8,128)(2,1)S(1)}, u32[]{:S(2)}, u32[]{:S(2)}) collective-permute-start(bf16[2,2,3,224,256]{4,3,2,1,0:T(8,128)(2,1)S(1)} %get-tuple-element.88), channel_id=1, source_target_pairs={{0,2},{64,66},{1,3},{65,67},{2,0},{66,64},{3,1},{67,65},{4,6},{68,... | collective-permute-start | bytes 4128776 | tf_op jit(solution)/shard_map/ppermute | solution.py:38
  62.9 2.1 %collective-permute-start.19 = (bf16[2,2,2,224,256]{4,3,2,1,0:T(8,128)(2,1)S(1)}, bf16[2,2,2,224,256]{4,3,2,1,0:T(8,128)(2,1)S(1)}, u32[]{:S(2)}, u32[]{:S(2)}) collective-permute-start(bf16[2,2,2,224,256]{4,3,2,1,0:T(8,128)(2,1)S(1)} %get-tuple-element.92), channel_id=1, source_target_pairs={{0,64},{64,0},{1,65},{65,1},{2,66},{66,2},{3,67},{67,3},{4,68},{68... | collective-permute-start | bytes 2752520 | tf_op jit(solution)/shard_map/ppermute | solution.py:38
  64.9 14.2 %collective-permute-done.15 = bf16[2,2,3,224,256]{4,3,2,1,0:T(8,128)(2,1)S(1)} collective-permute-done((bf16[2,2,3,224,256]{4,3,2,1,0:T(8,128)(2,1)S(1)}, bf16[2,2,3,224,256]{4,3,2,1,0:T(8,128)(2,1)S(1)}, u32[]{:S(2)}, u32[]{:S(2)}) %collective-permute-start.15) | collective-permute-done | bytes 1376288 | tf_op jit(solution)/shard_map/ppermute | solution.py:38
  83.1 1.8 collective-permute-start.20
  84.9 6.8 %collective-permute-done.20 = bf16[2,2,224,256]{3,2,1,0:T(8,128)(2,1)S(1)} collective-permute-done((bf16[2,2,224,256]{3,2,1,0:T(8,128)(2,1)S(1)}, bf16[2,2,224,256]{3,2,1,0:T(8,128)(2,1)S(1)}, u32[]{:S(2)}, u32[]{:S(2)}) %collective-permute-start.20) | collective-permute-done | bytes 458784 | tf_op jit(solution)/shard_map/ppermute | solution.py:38
  94.1 2.0 %collective-permute-start.23 = (bf16[3,224,256]{2,1,0:T(8,128)(2,1)S(1)}, bf16[3,224,256]{2,1,0:T(8,128)(2,1)S(1)}, u32[]{:S(2)}, u32[]{:S(2)}) collective-permute-start(bf16[3,224,256]{2,1,0:T(8,128)(2,1)S(1)} %fusion.33), channel_id=1, source_target_pairs={{0,2},{64,66},{1,3},{65,67},{2,0},{66,64},{3,1},{67,65},{4,6},{68,... | collective-permute-start | bytes 1032200 | tf_op jit(solution)/shard_map/ppermute | solution.py:38
  98.9 2.5 %collective-permute-done.23 = bf16[3,224,256]{2,1,0:T(8,128)(2,1)S(1)} collective-permute-done((bf16[3,224,256]{2,1,0:T(8,128)(2,1)S(1)}, bf16[3,224,256]{2,1,0:T(8,128)(2,1)S(1)}, u32[]{:S(2)}, u32[]{:S(2)}) %collective-permute-start.23) | collective-permute-done | bytes 344096 | tf_op jit(solution)/shard_map/ppermute | solution.py:38
  101.6 2.0 %collective-permute-done.22 = bf16[3,224,256]{2,1,0:T(8,128)(2,1)S(1)} collective-permute-done((bf16[3,224,256]{2,1,0:T(8,128)(2,1)S(1)}, bf16[3,224,256]{2,1,0:T(8,128)(2,1)S(1)}, u32[]{:S(2)}, u32[]{:S(2)}) %collective-permute-start.22) | collective-permute-done | bytes 344096 | tf_op jit(solution)/shard_map/ppermute | solution.py:38
  104.1 2.5 %collective-permute-start.25 = (bf16[2,224,256]{2,1,0:T(8,128)(2,1)S(1)}, bf16[2,224,256]{2,1,0:T(8,128)(2,1)S(1)}, u32[]{:S(2)}, u32[]{:S(2)}) collective-permute-start(bf16[2,224,256]{2,1,0:T(8,128)(2,1)S(1)} %get-tuple-element.127), channel_id=1, source_target_pairs={{0,6},{64,70},{1,7},{65,71},{2,4},{66,68},{3,5},{67,69},{4,2},{68,... | collective-permute-start | bytes 688136 | tf_op jit(solution)/shard_map/ppermute | solution.py:38
  106.6 3.2 %collective-permute-done.27 = bf16[2,224,256]{2,1,0:T(8,128)(2,1)S(1)} collective-permute-done((bf16[2,224,256]{2,1,0:T(8,128)(2,1)S(1)}, bf16[2,224,256]{2,1,0:T(8,128)(2,1)S(1)}, u32[]{:S(2)}, u32[]{:S(2)}) %collective-permute-start.27) | collective-permute-done | bytes 229408 | tf_op jit(solution)/shard_map/ppermute | solution.py:38
  109.9 1.5 collective-permute-done.26
  111.6 5.2 %collective-permute-done.28 = bf16[2,224,256]{2,1,0:T(8,128)(2,1)S(1)} collective-permute-done((bf16[2,224,256]{2,1,0:T(8,128)(2,1)S(1)}, bf16[2,224,256]{2,1,0:T(8,128)(2,1)S(1)}, u32[]{:S(2)}, u32[]{:S(2)}) %collective-permute-start.28) | collective-permute-done | bytes 229408 | tf_op jit(solution)/shard_map/ppermute | solution.py:38
  117.2 10.8 %collective-permute-start.32 = (bf16[224,256]{1,0:T(8,128)(2,1)S(1)}, bf16[224,256]{1,0:T(8,128)(2,1)S(1)}, u32[]{:S(2)}, u32[]{:S(2)}) collective-permute-start(bf16[224,256]{1,0:T(8,128)(2,1)S(1)} %slice_bitcast_fusion.12), channel_id=1, source_target_pairs={{0,32},{64,96},{1,33},{65,97},{2,34},{66,98},{3,35},{67,99},{4,36}... | collective-permute-start | bytes 344072 | tf_op jit(solution)/shard_map/ppermute | solution.py:38
  128.4 2.2 %collective-permute-start.31 = (bf16[2,224,256]{2,1,0:T(8,128)(2,1)S(1)}, bf16[2,224,256]{2,1,0:T(8,128)(2,1)S(1)}, u32[]{:S(2)}, u32[]{:S(2)}) collective-permute-start(bf16[2,224,256]{2,1,0:T(8,128)(2,1)S(1)} %get-tuple-element.97), channel_id=1, source_target_pairs={{0,30},{64,94},{1,31},{65,95},{2,28},{66,92},{3,29},{67,93},{4,26}... | collective-permute-start | bytes 688136 | tf_op jit(solution)/shard_map/ppermute | solution.py:38
  130.7 2.4 %collective-permute-done.29 = bf16[2,224,256]{2,1,0:T(8,128)(2,1)S(1)} collective-permute-done((bf16[2,224,256]{2,1,0:T(8,128)(2,1)S(1)}, bf16[2,224,256]{2,1,0:T(8,128)(2,1)S(1)}, u32[]{:S(2)}, u32[]{:S(2)}) %collective-permute-start.29) | collective-permute-done | bytes 229408 | tf_op jit(solution)/shard_map/ppermute | solution.py:38
  133.1 2.5 %collective-permute-done.30 = bf16[2,224,256]{2,1,0:T(8,128)(2,1)S(1)} collective-permute-done((bf16[2,224,256]{2,1,0:T(8,128)(2,1)S(1)}, bf16[2,224,256]{2,1,0:T(8,128)(2,1)S(1)}, u32[]{:S(2)}, u32[]{:S(2)}) %collective-permute-start.30) | collective-permute-done | bytes 229408 | tf_op jit(solution)/shard_map/ppermute | solution.py:38
  136.4 2.4 %collective-permute-start.33 = (bf16[3,224,256]{2,1,0:T(8,128)(2,1)S(1)}, bf16[3,224,256]{2,1,0:T(8,128)(2,1)S(1)}, u32[]{:S(2)}, u32[]{:S(2)}) collective-permute-start(bf16[3,224,256]{2,1,0:T(8,128)(2,1)S(1)} %get-tuple-element.102), channel_id=1, source_target_pairs={{0,64},{64,0},{1,65},{65,1},{2,66},{66,2},{3,67},{67,3},{4,68},{68... | collective-permute-start | bytes 1032200 | tf_op jit(solution)/shard_map/ppermute | solution.py:38
  140.3 1.5 collective-permute-start.35
  141.9 4.5 %collective-permute-done.35 = bf16[2,224,256]{2,1,0:T(8,128)(2,1)S(1)} collective-permute-done((bf16[2,224,256]{2,1,0:T(8,128)(2,1)S(1)}, bf16[2,224,256]{2,1,0:T(8,128)(2,1)S(1)}, u32[]{:S(2)}, u32[]{:S(2)}) %collective-permute-start.35) | collective-permute-done | bytes 229408 | tf_op jit(solution)/shard_map/ppermute | solution.py:38
  146.5 1.7 collective-permute-start.37
  148.4 1.5 collective-permute-start.39
  150.0 7.1 %collective-permute-done.39 = bf16[2,2,224,256]{3,2,1,0:T(8,128)(2,1)S(1)} collective-permute-done((bf16[2,2,224,256]{3,2,1,0:T(8,128)(2,1)S(1)}, bf16[2,2,224,256]{3,2,1,0:T(8,128)(2,1)S(1)}, u32[]{:S(2)}, u32[]{:S(2)}) %collective-permute-start.39) | collective-permute-done | bytes 458784 | tf_op jit(solution)/shard_map/ppermute | solution.py:38
  157.5 1.8 collective-permute-done.38
  159.4 1.5 collective-permute-start.40
  163.4 2.7 %collective-permute-start.48 = (bf16[2,2,2,224,256]{4,3,2,1,0:T(8,128)(2,1)S(1)}, bf16[2,2,2,224,256]{4,3,2,1,0:T(8,128)(2,1)S(1)}, u32[]{:S(2)}, u32[]{:S(2)}) collective-permute-start(bf16[2,2,2,224,256]{4,3,2,1,0:T(8,128)(2,1)S(1)} %pad_maximum_fusion.3.refs_2_), channel_id=1, source_target_pairs={{0,32},{64,96},{1,33},{65,97},{2,34},{66,98},{3,35},{67,99},{4,36}... | collective-permute-start | bytes 2752520 | tf_op jit(solution)/shard_map/ppermute | solution.py:38
  166.2 9.5 %collective-permute-done.42.refs_2_ = bf16[2,2,2,224,256]{4,3,2,1,0:T(8,128)(2,1)S(1)} collective-permute-done((bf16[2,2,2,224,256]{4,3,2,1,0:T(8,128)(2,1)S(1)}, bf16[2,2,2,224,256]{4,3,2,1,0:T(8,128)(2,1)S(1)}, u32[]{:S(2)}, u32[]{:S(2)}) %collective-permute-start.42) | collective-permute-done | bytes 917536 | tf_op jit(solution)/shard_map/ppermute | solution.py:38
  175.7 2.8 %collective-permute-start.47 = (bf16[2,2,3,224,256]{4,3,2,1,0:T(8,128)(2,1)S(1)}, bf16[2,2,3,224,256]{4,3,2,1,0:T(8,128)(2,1)S(1)}, u32[]{:S(2)}, u32[]{:S(2)}) collective-permute-start(bf16[2,2,3,224,256]{4,3,2,1,0:T(8,128)(2,1)S(1)} %pad_maximum_fusion.1.refs_1_), channel_id=1, source_target_pairs={{0,32},{64,96},{1,33},{65,97},{2,34},{66,98},{3,35},{67,99},{4,36}... | collective-permute-start | bytes 4128776 | tf_op jit(solution)/shard_map/ppermute | solution.py:38
  178.5 2.0 %collective-permute-start.43 = (bf16[2,2,3,224,256]{4,3,2,1,0:T(8,128)(2,1)S(1)}, bf16[2,2,3,224,256]{4,3,2,1,0:T(8,128)(2,1)S(1)}, u32[]{:S(2)}, u32[]{:S(2)}) collective-permute-start(bf16[2,2,3,224,256]{4,3,2,1,0:T(8,128)(2,1)S(1)} %collective-permute-done.40.refs_0_), channel_id=1, source_target_pairs={{0,32},{64,96},{1,33},{65,97},{2,34},{66,98},{3,35},{67,99},{4,36}... | collective-permute-start | bytes 4128776 | tf_op jit(solution)/shard_map/ppermute | solution.py:38
  181.3 1.5 fusion.1
  184.5 2.1 %collective-permute-done.45.refs_2_ = bf16[2,2,2,224,256]{4,3,2,1,0:T(8,128)(2,1)S(1)} collective-permute-done((bf16[2,2,2,224,256]{4,3,2,1,0:T(8,128)(2,1)S(1)}, bf16[2,2,2,224,256]{4,3,2,1,0:T(8,128)(2,1)S(1)}, u32[]{:S(2)}, u32[]{:S(2)}) %collective-permute-start.45) | collective-permute-done | bytes 917536 | tf_op jit(solution)/shard_map/ppermute | solution.py:38
  187.4 5.6 %shard_map.85 = bf16[256,14336]{1,0:T(8,128)(2,1)} custom-call(s32[1]{0:T(128)} %bitcast.core_ref, bf16[64,224,256]{2,1,0:T(8,128)(2,1)S(1)} %shard_map.82.own_ref, bf16[64,224,256]{2,1,0:T(8,128)(2,1)S(1)} %shard_map.84.other_ref, bf16[2,256,256]{2,1,0:T(8,128)(2,1)S(1)} %pad_maximum_fusion.17.b_ref), custom_call_target="tpu_custom_call" | custom-call | flops 3758096384 | bytes 22020096 | tf_op jit(solution)/shard_map/pallas_call | solution.py:262
  (117 shorter events, 36.2 us)
Async XLA Ops:
  0.6 33.9 %collective-permute-start.11 = (bf16[256,14336]{1,0:T(8,128)(2,1)}, bf16[256,14336]{1,0:T(8,128)(2,1)}, u32[]{:S(2)}, u32[]{:S(2)}) collective-permute-start(bf16[256,14336]{1,0:T(8,128)(2,1)} %g0_ref.1), channel_id=1, source_target_pairs={{0,32},{64,96},{1,33},{65,97},{2,34},{66,98},{3,35},{67,99},{4,36}... | collective-permute-start | bytes 22020104 | tf_op jit(solution)/shard_map/ppermute | solution.py:38
  2.1 32.4 %collective-permute-start.10 = (bf16[256,8192]{1,0:T(8,128)(2,1)}, bf16[256,8192]{1,0:T(8,128)(2,1)}, u32[]{:S(2)}, u32[]{:S(2)}) collective-permute-start(bf16[256,8192]{1,0:T(8,128)(2,1)} %refs_0_.1), channel_id=1, source_target_pairs={{0,32},{64,96},{1,33},{65,97},{2,34},{66,98},{3,35},{67,99},{4,36}... | collective-permute-start | bytes 12582920 | tf_op jit(solution)/shard_map/ppermute | solution.py:38
  6.5 3.9 %collective-permute-start.1 = (bf16[2,128,256]{2,1,0:T(8,128)(2,1)S(1)}, bf16[2,128,256]{2,1,0:T(8,128)(2,1)S(1)}, u32[]{:S(2)}, u32[]{:S(2)}) collective-permute-start(bf16[2,128,256]{2,1,0:T(8,128)(2,1)S(1)} %pad_maximum_fusion.20), channel_id=1, source_target_pairs={{0,6},{64,70},{1,7},{65,71},{2,4},{66,68},{3,5},{67,69},{4,2},{68,... | collective-permute-start | bytes 393224 | tf_op jit(solution)/shard_map/ppermute | solution.py:38
  7.8 4.6 %collective-permute-start.2 = (bf16[2,128,256]{2,1,0:T(8,128)(2,1)S(1)}, bf16[2,128,256]{2,1,0:T(8,128)(2,1)S(1)}, u32[]{:S(2)}, u32[]{:S(2)}) collective-permute-start(bf16[2,128,256]{2,1,0:T(8,128)(2,1)S(1)} %pad_maximum_fusion.20), channel_id=1, source_target_pairs={{0,24},{64,88},{1,25},{65,89},{2,26},{66,90},{3,27},{67,91},{4,28}... | collective-permute-start | bytes 393224 | tf_op jit(solution)/shard_map/ppermute | solution.py:38
  9.1 4.7 %collective-permute-start.3 = (bf16[2,128,256]{2,1,0:T(8,128)(2,1)S(1)}, bf16[2,128,256]{2,1,0:T(8,128)(2,1)S(1)}, u32[]{:S(2)}, u32[]{:S(2)}) collective-permute-start(bf16[2,128,256]{2,1,0:T(8,128)(2,1)S(1)} %pad_maximum_fusion.20), channel_id=1, source_target_pairs={{0,30},{64,94},{1,31},{65,95},{2,28},{66,92},{3,29},{67,93},{4,26}... | collective-permute-start | bytes 393224 | tf_op jit(solution)/shard_map/ppermute | solution.py:38
  13.8 11.0 %collective-permute-start.4 = (bf16[3,128,256]{2,1,0:T(8,128)(2,1)S(1)}, bf16[3,128,256]{2,1,0:T(8,128)(2,1)S(1)}, u32[]{:S(2)}, u32[]{:S(2)}) collective-permute-start(bf16[3,128,256]{2,1,0:T(8,128)(2,1)S(1)} %get-tuple-element.67), channel_id=1, source_target_pairs={{0,64},{64,0},{1,65},{65,1},{2,66},{66,2},{3,67},{67,3},{4,68},{68... | collective-permute-start | bytes 589832 | tf_op jit(solution)/shard_map/ppermute | solution.py:38
  17.8 7.0 %collective-permute-start.5 = (bf16[3,128,256]{2,1,0:T(8,128)(2,1)S(1)}, bf16[3,128,256]{2,1,0:T(8,128)(2,1)S(1)}, u32[]{:S(2)}, u32[]{:S(2)}) collective-permute-start(bf16[3,128,256]{2,1,0:T(8,128)(2,1)S(1)} %get-tuple-element.69), channel_id=1, source_target_pairs={{0,2},{64,66},{1,3},{65,67},{2,0},{66,64},{3,1},{67,65},{4,6},{68,... | collective-permute-start | bytes 589832 | tf_op jit(solution)/shard_map/ppermute | solution.py:38
  19.3 5.5 %collective-permute-start.6 = (bf16[2,128,256]{2,1,0:T(8,128)(2,1)S(1)}, bf16[2,128,256]{2,1,0:T(8,128)(2,1)S(1)}, u32[]{:S(2)}, u32[]{:S(2)}) collective-permute-start(bf16[2,128,256]{2,1,0:T(8,128)(2,1)S(1)} %collective-permute-done.3), channel_id=1, source_target_pairs={{0,8},{64,72},{1,9},{65,73},{2,10},{66,74},{3,11},{67,75},{4,12},{... | collective-permute-start | bytes 393224 | tf_op jit(solution)/shard_map/ppermute | solution.py:38
  24.9 9.6 %collective-permute-start.7 = (bf16[2,3,128,256]{3,2,1,0:T(8,128)(2,1)S(1)}, bf16[2,3,128,256]{3,2,1,0:T(8,128)(2,1)S(1)}, u32[]{:S(2)}, u32[]{:S(2)}) collective-permute-start(bf16[2,3,128,256]{3,2,1,0:T(8,128)(2,1)S(1)} %pad_maximum_fusion.12), channel_id=1, source_target_pairs={{0,8},{64,72},{1,9},{65,73},{2,10},{66,74},{3,11},{67,75},{4,12},{... | collective-permute-start | bytes 1179656 | tf_op jit(solution)/shard_map/ppermute | solution.py:38
  26.4 8.1 %collective-permute-start.8 = (bf16[2,3,128,256]{3,2,1,0:T(8,128)(2,1)S(1)}, bf16[2,3,128,256]{3,2,1,0:T(8,128)(2,1)S(1)}, u32[]{:S(2)}, u32[]{:S(2)}) collective-permute-start(bf16[2,3,128,256]{3,2,1,0:T(8,128)(2,1)S(1)} %pad_maximum_fusion.13), channel_id=1, source_target_pairs={{0,64},{64,0},{1,65},{65,1},{2,66},{66,2},{3,67},{67,3},{4,68},{68... | collective-permute-start | bytes 1179656 | tf_op jit(solution)/shard_map/ppermute | solution.py:38
  28.0 6.5 %collective-permute-start.9 = (bf16[2,2,128,256]{3,2,1,0:T(8,128)(2,1)S(1)}, bf16[2,2,128,256]{3,2,1,0:T(8,128)(2,1)S(1)}, u32[]{:S(2)}, u32[]{:S(2)}) collective-permute-start(bf16[2,2,128,256]{3,2,1,0:T(8,128)(2,1)S(1)} %pad_maximum_fusion.16), channel_id=1, source_target_pairs={{0,2},{64,66},{1,3},{65,67},{2,0},{66,64},{3,1},{67,65},{4,6},{68,... | collective-permute-start | bytes 786440 | tf_op jit(solution)/shard_map/ppermute | solution.py:38
  35.3 12.1 %collective-permute-start.12 = (bf16[2,2,3,128,256]{4,3,2,1,0:T(8,128)(2,1)S(1)}, bf16[2,2,3,128,256]{4,3,2,1,0:T(8,128)(2,1)S(1)}, u32[]{:S(2)}, u32[]{:S(2)}) collective-permute-start(bf16[2,2,3,128,256]{4,3,2,1,0:T(8,128)(2,1)S(1)} %pad_maximum_fusion.4.refs_0_), channel_id=1, source_target_pairs={{0,2},{64,66},{1,3},{65,67},{2,0},{66,64},{3,1},{67,65},{4,6},{68,... | collective-permute-start | bytes 2359304 | tf_op jit(solution)/shard_map/ppermute | solution.py:38
  36.2 12.2 %collective-permute-start.13 = (bf16[2,2,3,128,256]{4,3,2,1,0:T(8,128)(2,1)S(1)}, bf16[2,2,3,128,256]{4,3,2,1,0:T(8,128)(2,1)}, u32[]{:S(2)}, u32[]{:S(2)}) collective-permute-start(bf16[2,2,3,128,256]{4,3,2,1,0:T(8,128)(2,1)S(1)} %pad_maximum_fusion.5.refs_1_), channel_id=1, source_target_pairs={{0,8},{64,72},{1,9},{65,73},{2,10},{66,74},{3,11},{67,75},{4,12},{... | collective-permute-start | bytes 2359304 | tf_op jit(solution)/shard_map/ppermute | solution.py:38
  37.0 9.3 %collective-permute-start.14 = (bf16[2,2,2,128,256]{4,3,2,1,0:T(8,128)(2,1)S(1)}, bf16[2,2,2,128,256]{4,3,2,1,0:T(8,128)(2,1)S(1)}, u32[]{:S(2)}, u32[]{:S(2)}) collective-permute-start(bf16[2,2,2,128,256]{4,3,2,1,0:T(8,128)(2,1)S(1)} %pad_maximum_fusion.8.refs_2_), channel_id=1, source_target_pairs={{0,64},{64,0},{1,65},{65,1},{2,66},{66,2},{3,67},{67,3},{4,68},{68... | collective-permute-start | bytes 1572872 | tf_op jit(solution)/shard_map/ppermute | solution.py:38
  60.3 18.9 %collective-permute-start.15 = (bf16[2,2,3,224,256]{4,3,2,1,0:T(8,128)(2,1)S(1)}, bf16[2,2,3,224,256]{4,3,2,1,0:T(8,128)(2,1)S(1)}, u32[]{:S(2)}, u32[]{:S(2)}) collective-permute-start(bf16[2,2,3,224,256]{4,3,2,1,0:T(8,128)(2,1)S(1)} %get-tuple-element.88), channel_id=1, source_target_pairs={{0,2},{64,66},{1,3},{65,67},{2,0},{66,64},{3,1},{67,65},{4,6},{68,... | collective-permute-start | bytes 4128776 | tf_op jit(solution)/shard_map/ppermute | solution.py:38
  62.5 18.7 %collective-permute-start.17 = (bf16[2,2,3,224,256]{4,3,2,1,0:T(8,128)(2,1)S(1)}, bf16[2,2,3,224,256]{4,3,2,1,0:T(8,128)(2,1)S(1)}, u32[]{:S(2)}, u32[]{:S(2)}) collective-permute-start(bf16[2,2,3,224,256]{4,3,2,1,0:T(8,128)(2,1)S(1)} %get-tuple-element.90), channel_id=1, source_target_pairs={{0,8},{64,72},{1,9},{65,73},{2,10},{66,74},{3,11},{67,75},{4,12},{... | collective-permute-start | bytes 4128776 | tf_op jit(solution)/shard_map/ppermute | solution.py:38
  62.9 20.0 %collective-permute-start.19 = (bf16[2,2,2,224,256]{4,3,2,1,0:T(8,128)(2,1)S(1)}, bf16[2,2,2,224,256]{4,3,2,1,0:T(8,128)(2,1)S(1)}, u32[]{:S(2)}, u32[]{:S(2)}) collective-permute-start(bf16[2,2,2,224,256]{4,3,2,1,0:T(8,128)(2,1)S(1)} %get-tuple-element.92), channel_id=1, source_target_pairs={{0,64},{64,0},{1,65},{65,1},{2,66},{66,2},{3,67},{67,3},{4,68},{68... | collective-permute-start | bytes 2752520 | tf_op jit(solution)/shard_map/ppermute | solution.py:38
  64.9 20.0 %collective-permute-start.21 = (f32[2,224,256]{2,1,0:T(8,128)S(1)}, f32[2,224,256]{2,1,0:T(8,128)S(1)}, u32[]{:S(2)}, u32[]{:S(2)}) collective-permute-start(f32[2,224,256]{2,1,0:T(8,128)S(1)} %copy-done.1), channel_id=1, source_target_pairs={{0,65},{64,1},{1,64},{65,0},{2,67},{66,3},{3,66},{67,2},{4,69},{68... | collective-permute-start | bytes 1376264 | tf_op jit(solution)/shard_map/ppermute | solution.py:38
  79.6 12.2 %collective-permute-start.16 = (bf16[2,3,224,256]{3,2,1,0:T(8,128)(2,1)S(1)}, bf16[2,3,224,256]{3,2,1,0:T(8,128)(2,1)S(1)}, u32[]{:S(2)}, u32[]{:S(2)}) collective-permute-start(bf16[2,3,224,256]{3,2,1,0:T(8,128)(2,1)S(1)} %get-tuple-element.122), channel_id=1, source_target_pairs={{0,8},{64,72},{1,9},{65,73},{2,10},{66,74},{3,11},{67,75},{4,12},{... | collective-permute-start | bytes 2064392 | tf_op jit(solution)/shard_map/ppermute | solution.py:38
  81.5 11.1 %collective-permute-start.18 = (bf16[2,3,224,256]{3,2,1,0:T(8,128)(2,1)S(1)}, bf16[2,3,224,256]{3,2,1,0:T(8,128)(2,1)S(1)}, u32[]{:S(2)}, u32[]{:S(2)}) collective-permute-start(bf16[2,3,224,256]{3,2,1,0:T(8,128)(2,1)S(1)} %get-tuple-element.124), channel_id=1, source_target_pairs={{0,64},{64,0},{1,65},{65,1},{2,66},{66,2},{3,67},{67,3},{4,68},{68... | collective-permute-start | bytes 2064392 | tf_op jit(solution)/shard_map/ppermute | solution.py:38
  83.1 8.6 %collective-permute-start.20 = (bf16[2,2,224,256]{3,2,1,0:T(8,128)(2,1)S(1)}, bf16[2,2,224,256]{3,2,1,0:T(8,128)(2,1)S(1)}, u32[]{:S(2)}, u32[]{:S(2)}) collective-permute-start(bf16[2,2,224,256]{3,2,1,0:T(8,128)(2,1)S(1)} %get-tuple-element.126), channel_id=1, source_target_pairs={{0,2},{64,66},{1,3},{65,67},{2,0},{66,64},{3,1},{67,65},{4,6},{68,... | collective-permute-start | bytes 1376264 | tf_op jit(solution)/shard_map/ppermute | solution.py:38
  92.7 6.2 %collective-permute-start.24 = (bf16[2,224,256]{2,1,0:T(8,128)(2,1)S(1)}, bf16[2,224,256]{2,1,0:T(8,128)(2,1)S(1)}, u32[]{:S(2)}, u32[]{:S(2)}) collective-permute-start(bf16[2,224,256]{2,1,0:T(8,128)(2,1)S(1)} %fusion.35), channel_id=1, source_target_pairs={{0,8},{64,72},{1,9},{65,73},{2,10},{66,74},{3,11},{67,75},{4,12},{... | collective-permute-start | bytes 688136 | tf_op jit(solution)/shard_map/ppermute | solution.py:38
  94.1 7.4 %collective-permute-start.23 = (bf16[3,224,256]{2,1,0:T(8,128)(2,1)S(1)}, bf16[3,224,256]{2,1,0:T(8,128)(2,1)S(1)}, u32[]{:S(2)}, u32[]{:S(2)}) collective-permute-start(bf16[3,224,256]{2,1,0:T(8,128)(2,1)S(1)} %fusion.33), channel_id=1, source_target_pairs={{0,2},{64,66},{1,3},{65,67},{2,0},{66,64},{3,1},{67,65},{4,6},{68,... | collective-permute-start | bytes 1032200 | tf_op jit(solution)/shard_map/ppermute | solution.py:38
  96.2 7.4 %collective-permute-start.22 = (bf16[3,224,256]{2,1,0:T(8,128)(2,1)S(1)}, bf16[3,224,256]{2,1,0:T(8,128)(2,1)S(1)}, u32[]{:S(2)}, u32[]{:S(2)}) collective-permute-start(bf16[3,224,256]{2,1,0:T(8,128)(2,1)S(1)} %fusion.31), channel_id=1, source_target_pairs={{0,64},{64,0},{1,65},{65,1},{2,66},{66,2},{3,67},{67,3},{4,68},{68... | collective-permute-start | bytes 1032200 | tf_op jit(solution)/shard_map/ppermute | solution.py:38
  103.9 6.0 %collective-permute-start.27 = (bf16[2,224,256]{2,1,0:T(8,128)(2,1)S(1)}, bf16[2,224,256]{2,1,0:T(8,128)(2,1)S(1)}, u32[]{:S(2)}, u32[]{:S(2)}) collective-permute-start(bf16[2,224,256]{2,1,0:T(8,128)(2,1)S(1)} %get-tuple-element.128), channel_id=1, source_target_pairs={{0,30},{64,94},{1,31},{65,95},{2,28},{66,92},{3,29},{67,93},{4,26}... | collective-permute-start | bytes 688136 | tf_op jit(solution)/shard_map/ppermute | solution.py:38
  104.0 7.4 %collective-permute-start.26 = (bf16[2,224,256]{2,1,0:T(8,128)(2,1)S(1)}, bf16[2,224,256]{2,1,0:T(8,128)(2,1)S(1)}, u32[]{:S(2)}, u32[]{:S(2)}) collective-permute-start(bf16[2,224,256]{2,1,0:T(8,128)(2,1)S(1)} %get-tuple-element.129), channel_id=1, source_target_pairs={{0,24},{64,88},{1,25},{65,89},{2,26},{66,90},{3,27},{67,91},{4,28}... | collective-permute-start | bytes 688136 | tf_op jit(solution)/shard_map/ppermute | solution.py:38
  104.1 7.3 %collective-permute-start.25 = (bf16[2,224,256]{2,1,0:T(8,128)(2,1)S(1)}, bf16[2,224,256]{2,1,0:T(8,128)(2,1)S(1)}, u32[]{:S(2)}, u32[]{:S(2)}) collective-permute-start(bf16[2,224,256]{2,1,0:T(8,128)(2,1)S(1)} %get-tuple-element.127), channel_id=1, source_target_pairs={{0,6},{64,70},{1,7},{65,71},{2,4},{66,68},{3,5},{67,69},{4,2},{68,... | collective-permute-start | bytes 688136 | tf_op jit(solution)/shard_map/ppermute | solution.py:38
  111.5 5.2 %collective-permute-start.28 = (bf16[2,224,256]{2,1,0:T(8,128)(2,1)S(1)}, bf16[2,224,256]{2,1,0:T(8,128)(2,1)S(1)}, u32[]{:S(2)}, u32[]{:S(2)}) collective-permute-start(bf16[2,224,256]{2,1,0:T(8,128)(2,1)S(1)} %fusion.25), channel_id=1, source_target_pairs={{0,65},{64,1},{1,64},{65,0},{2,67},{66,3},{3,66},{67,2},{4,69},{68... | collective-permute-start | bytes 688136 | tf_op jit(solution)/shard_map/ppermute | solution.py:38
  117.2 13.4 %collective-permute-start.32 = (bf16[224,256]{1,0:T(8,128)(2,1)S(1)}, bf16[224,256]{1,0:T(8,128)(2,1)S(1)}, u32[]{:S(2)}, u32[]{:S(2)}) collective-permute-start(bf16[224,256]{1,0:T(8,128)(2,1)S(1)} %slice_bitcast_fusion.12), channel_id=1, source_target_pairs={{0,32},{64,96},{1,33},{65,97},{2,34},{66,98},{3,35},{67,99},{4,36}... | collective-permute-start | bytes 344072 | tf_op jit(solution)/shard_map/ppermute | solution.py:38
  127.9 5.2 %collective-permute-start.29 = (bf16[2,224,256]{2,1,0:T(8,128)(2,1)S(1)}, bf16[2,224,256]{2,1,0:T(8,128)(2,1)S(1)}, u32[]{:S(2)}, u32[]{:S(2)}) collective-permute-start(bf16[2,224,256]{2,1,0:T(8,128)(2,1)S(1)} %get-tuple-element.97), channel_id=1, source_target_pairs={{0,6},{64,70},{1,7},{65,71},{2,4},{66,68},{3,5},{67,69},{4,2},{68,... | collective-permute-start | bytes 688136 | tf_op jit(solution)/shard_map/ppermute | solution.py:38
  128.0 7.6 %collective-permute-start.30 = (bf16[2,224,256]{2,1,0:T(8,128)(2,1)S(1)}, bf16[2,224,256]{2,1,0:T(8,128)(2,1)S(1)}, u32[]{:S(2)}, u32[]{:S(2)}) collective-permute-start(bf16[2,224,256]{2,1,0:T(8,128)(2,1)S(1)} %get-tuple-element.97), channel_id=1, source_target_pairs={{0,24},{64,88},{1,25},{65,89},{2,26},{66,90},{3,27},{67,91},{4,28}... | collective-permute-start | bytes 688136 | tf_op jit(solution)/shard_map/ppermute | solution.py:38
  128.4 7.2 %collective-permute-start.31 = (bf16[2,224,256]{2,1,0:T(8,128)(2,1)S(1)}, bf16[2,224,256]{2,1,0:T(8,128)(2,1)S(1)}, u32[]{:S(2)}, u32[]{:S(2)}) collective-permute-start(bf16[2,224,256]{2,1,0:T(8,128)(2,1)S(1)} %get-tuple-element.97), channel_id=1, source_target_pairs={{0,30},{64,94},{1,31},{65,95},{2,28},{66,92},{3,29},{67,93},{4,26}... | collective-permute-start | bytes 688136 | tf_op jit(solution)/shard_map/ppermute | solution.py:38
  135.6 6.2 %collective-permute-start.36 = (bf16[224,512]{1,0:T(8,128)(2,1)S(1)}, bf16[224,512]{1,0:T(8,128)(2,1)S(1)}, u32[]{:S(2)}, u32[]{:S(2)}) collective-permute-start(bf16[224,512]{1,0:T(8,128)(2,1)S(1)} %maximum_select_fusion.1), channel_id=1, source_target_pairs={{0,64},{64,0},{1,65},{65,1},{2,66},{66,2},{3,67},{67,3},{4,68},{68... | collective-permute-start | bytes 688136 | tf_op jit(solution)/shard_map/ppermute | solution.py:38
  136.4 9.9 %collective-permute-start.33 = (bf16[3,224,256]{2,1,0:T(8,128)(2,1)S(1)}, bf16[3,224,256]{2,1,0:T(8,128)(2,1)S(1)}, u32[]{:S(2)}, u32[]{:S(2)}) collective-permute-start(bf16[3,224,256]{2,1,0:T(8,128)(2,1)S(1)} %get-tuple-element.102), channel_id=1, source_target_pairs={{0,64},{64,0},{1,65},{65,1},{2,66},{66,2},{3,67},{67,3},{4,68},{68... | collective-permute-start | bytes 1032200 | tf_op jit(solution)/shard_map/ppermute | solution.py:38
  138.9 7.5 %collective-permute-start.34 = (bf16[3,224,256]{2,1,0:T(8,128)(2,1)S(1)}, bf16[3,224,256]{2,1,0:T(8,128)(2,1)S(1)}, u32[]{:S(2)}, u32[]{:S(2)}) collective-permute-start(bf16[3,224,256]{2,1,0:T(8,128)(2,1)S(1)} %get-tuple-element.104), channel_id=1, source_target_pairs={{0,2},{64,66},{1,3},{65,67},{2,0},{66,64},{3,1},{67,65},{4,6},{68,... | collective-permute-start | bytes 1032200 | tf_op jit(solution)/shard_map/ppermute | solution.py:38
  140.3 6.1 %collective-permute-start.35 = (bf16[2,224,256]{2,1,0:T(8,128)(2,1)S(1)}, bf16[2,224,256]{2,1,0:T(8,128)(2,1)S(1)}, u32[]{:S(2)}, u32[]{:S(2)}) collective-permute-start(bf16[2,224,256]{2,1,0:T(8,128)(2,1)S(1)} %collective-permute-done.31), channel_id=1, source_target_pairs={{0,8},{64,72},{1,9},{65,73},{2,10},{66,74},{3,11},{67,75},{4,12},{... | collective-permute-start | bytes 688136 | tf_op jit(solution)/shard_map/ppermute | solution.py:38
  146.5 11.1 %collective-permute-start.37 = (bf16[2,3,224,256]{3,2,1,0:T(8,128)(2,1)S(1)}, bf16[2,3,224,256]{3,2,1,0:T(8,128)(2,1)S(1)}, u32[]{:S(2)}, u32[]{:S(2)}) collective-permute-start(bf16[2,3,224,256]{3,2,1,0:T(8,128)(2,1)S(1)} %pad_maximum_fusion.6), channel_id=1, source_target_pairs={{0,8},{64,72},{1,9},{65,73},{2,10},{66,74},{3,11},{67,75},{4,12},{... | collective-permute-start | bytes 2064392 | tf_op jit(solution)/shard_map/ppermute | solution.py:38
  148.2 11.1 %collective-permute-start.38 = (bf16[2,3,224,256]{3,2,1,0:T(8,128)(2,1)S(1)}, bf16[2,3,224,256]{3,2,1,0:T(8,128)(2,1)S(1)}, u32[]{:S(2)}, u32[]{:S(2)}) collective-permute-start(bf16[2,3,224,256]{3,2,1,0:T(8,128)(2,1)S(1)} %pad_maximum_fusion.7), channel_id=1, source_target_pairs={{0,64},{64,0},{1,65},{65,1},{2,66},{66,2},{3,67},{67,3},{4,68},{68... | collective-permute-start | bytes 2064392 | tf_op jit(solution)/shard_map/ppermute | solution.py:38
  148.4 8.6 %collective-permute-start.39 = (bf16[2,2,224,256]{3,2,1,0:T(8,128)(2,1)S(1)}, bf16[2,2,224,256]{3,2,1,0:T(8,128)(2,1)S(1)}, u32[]{:S(2)}, u32[]{:S(2)}) collective-permute-start(bf16[2,2,224,256]{3,2,1,0:T(8,128)(2,1)S(1)} %pad_maximum_fusion.11), channel_id=1, source_target_pairs={{0,2},{64,66},{1,3},{65,67},{2,0},{66,64},{3,1},{67,65},{4,6},{68,... | collective-permute-start | bytes 1376264 | tf_op jit(solution)/shard_map/ppermute | solution.py:38
  159.4 19.1 %collective-permute-start.40 = (bf16[2,2,3,224,256]{4,3,2,1,0:T(8,128)(2,1)S(1)}, bf16[2,2,3,224,256]{4,3,2,1,0:T(8,128)(2,1)S(1)}, u32[]{:S(2)}, u32[]{:S(2)}) collective-permute-start(bf16[2,2,3,224,256]{4,3,2,1,0:T(8,128)(2,1)S(1)} %pad_maximum_fusion.refs_0_), channel_id=1, source_target_pairs={{0,2},{64,66},{1,3},{65,67},{2,0},{66,64},{3,1},{67,65},{4,6},{68,... | collective-permute-start | bytes 4128776 | tf_op jit(solution)/shard_map/ppermute | solution.py:38
  161.1 19.4 %collective-permute-start.41 = (bf16[2,2,3,224,256]{4,3,2,1,0:T(8,128)(2,1)S(1)}, bf16[2,2,3,224,256]{4,3,2,1,0:T(8,128)(2,1)S(1)}, u32[]{:S(2)}, u32[]{:S(2)}) collective-permute-start(bf16[2,2,3,224,256]{4,3,2,1,0:T(8,128)(2,1)S(1)} %pad_maximum_fusion.1.refs_1_), channel_id=1, source_target_pairs={{0,8},{64,72},{1,9},{65,73},{2,10},{66,74},{3,11},{67,75},{4,12},{... | collective-permute-start | bytes 4128776 | tf_op jit(solution)/shard_map/ppermute | solution.py:38
  162.1 13.5 %collective-permute-start.42 = (bf16[2,2,2,224,256]{4,3,2,1,0:T(8,128)(2,1)S(1)}, bf16[2,2,2,224,256]{4,3,2,1,0:T(8,128)(2,1)S(1)}, u32[]{:S(2)}, u32[]{:S(2)}) collective-permute-start(bf16[2,2,2,224,256]{4,3,2,1,0:T(8,128)(2,1)S(1)} %pad_maximum_fusion.3.refs_2_), channel_id=1, source_target_pairs={{0,64},{64,0},{1,65},{65,1},{2,66},{66,2},{3,67},{67,3},{4,68},{68... | collective-permute-start | bytes 2752520 | tf_op jit(solution)/shard_map/ppermute | solution.py:38
  163.4 17.9 %collective-permute-start.48 = (bf16[2,2,2,224,256]{4,3,2,1,0:T(8,128)(2,1)S(1)}, bf16[2,2,2,224,256]{4,3,2,1,0:T(8,128)(2,1)S(1)}, u32[]{:S(2)}, u32[]{:S(2)}) collective-permute-start(bf16[2,2,2,224,256]{4,3,2,1,0:T(8,128)(2,1)S(1)} %pad_maximum_fusion.3.refs_2_), channel_id=1, source_target_pairs={{0,32},{64,96},{1,33},{65,97},{2,34},{66,98},{3,35},{67,99},{4,36}... | collective-permute-start | bytes 2752520 | tf_op jit(solution)/shard_map/ppermute | solution.py:38
  166.1 17.6 %collective-permute-start.46 = (bf16[2,2,3,224,256]{4,3,2,1,0:T(8,128)(2,1)S(1)}, bf16[2,2,3,224,256]{4,3,2,1,0:T(8,128)(2,1)S(1)}, u32[]{:S(2)}, u32[]{:S(2)}) collective-permute-start(bf16[2,2,3,224,256]{4,3,2,1,0:T(8,128)(2,1)S(1)} %pad_maximum_fusion.refs_0_), channel_id=1, source_target_pairs={{0,32},{64,96},{1,33},{65,97},{2,34},{66,98},{3,35},{67,99},{4,36}... | collective-permute-start | bytes 4128776 | tf_op jit(solution)/shard_map/ppermute | solution.py:38
  175.7 8.0 %collective-permute-start.47 = (bf16[2,2,3,224,256]{4,3,2,1,0:T(8,128)(2,1)S(1)}, bf16[2,2,3,224,256]{4,3,2,1,0:T(8,128)(2,1)S(1)}, u32[]{:S(2)}, u32[]{:S(2)}) collective-permute-start(bf16[2,2,3,224,256]{4,3,2,1,0:T(8,128)(2,1)S(1)} %pad_maximum_fusion.1.refs_1_), channel_id=1, source_target_pairs={{0,32},{64,96},{1,33},{65,97},{2,34},{66,98},{3,35},{67,99},{4,36}... | collective-permute-start | bytes 4128776 | tf_op jit(solution)/shard_map/ppermute | solution.py:38
  178.5 8.0 %collective-permute-start.43 = (bf16[2,2,3,224,256]{4,3,2,1,0:T(8,128)(2,1)S(1)}, bf16[2,2,3,224,256]{4,3,2,1,0:T(8,128)(2,1)S(1)}, u32[]{:S(2)}, u32[]{:S(2)}) collective-permute-start(bf16[2,2,3,224,256]{4,3,2,1,0:T(8,128)(2,1)S(1)} %collective-permute-done.40.refs_0_), channel_id=1, source_target_pairs={{0,32},{64,96},{1,33},{65,97},{2,34},{66,98},{3,35},{67,99},{4,36}... | collective-permute-start | bytes 4128776 | tf_op jit(solution)/shard_map/ppermute | solution.py:38
  180.5 6.0 %collective-permute-start.44 = (bf16[2,2,3,224,256]{4,3,2,1,0:T(8,128)(2,1)S(1)}, bf16[2,2,3,224,256]{4,3,2,1,0:T(8,128)(2,1)S(1)}, u32[]{:S(2)}, u32[]{:S(2)}) collective-permute-start(bf16[2,2,3,224,256]{4,3,2,1,0:T(8,128)(2,1)S(1)} %collective-permute-done.41.refs_1_), channel_id=1, source_target_pairs={{0,32},{64,96},{1,33},{65,97},{2,34},{66,98},{3,35},{67,99},{4,36}... | collective-permute-start | bytes 4128776 | tf_op jit(solution)/shard_map/ppermute | solution.py:38
  181.2 5.3 %collective-permute-start.45 = (bf16[2,2,2,224,256]{4,3,2,1,0:T(8,128)(2,1)S(1)}, bf16[2,2,2,224,256]{4,3,2,1,0:T(8,128)(2,1)S(1)}, u32[]{:S(2)}, u32[]{:S(2)}) collective-permute-start(bf16[2,2,2,224,256]{4,3,2,1,0:T(8,128)(2,1)S(1)} %collective-permute-done.42.refs_2_), channel_id=1, source_target_pairs={{0,32},{64,96},{1,33},{65,97},{2,34},{66,98},{3,35},{67,99},{4,36}... | collective-permute-start | bytes 2752520 | tf_op jit(solution)/shard_map/ppermute | solution.py:38
  (10 other events, 82.6 us)

commit v5 on v4

--- a/solution.py
+++ b/solution.py
@@ -297,8 +297,8 @@
         lax.dynamic_slice(basis, (zl * brows, core * half), (brows, half)), swapped
     )
     whole = place(place(None, near, 0, pos, mine), far, 1, pos, mine)
-    near_acts = load(activations, act_other)
-    projected = project(*near_acts, whole)
+    act_other, g_other = load(act_other, g_other)
+    projected = project(activations, act_other, whole)
     sums = partials(out_grads, g_other, *projected, pos)
     keeps, sends = sums[0::2], sums[1::2]
 
@@ -307,7 +307,7 @@
     for stage in range(3):
         gots = [swap(send, order[stage]) for order, send in zip(ORDERS, sends)]
         if stage == 1:
-            *gots, theirs_moments = lax.optimization_barrier((*gots, swap(moments, "z", late=1)))
+            gots[2], theirs_moments = lax.optimization_barrier((gots[2], swap(moments, "z", late=1)))
         if stage < 2:
             sends = [add(keep[1], got[1]) for keep, got in zip(keeps, gots)]
             keeps = [add(keep[0], got[0]) for keep, got in zip(keeps, gots)]

time: 193 us -> 188 us (0.974)
  waiting for transfers between devices: 86.4 us -> 78.9 us
  starting transfers between devices: 71 us -> 75.4 us
    ppermute x49, waiting for transfers between devices: 86.4 us -> 78.9 us  [permute(): return lax.ppermute(arr, AXES, pairs)]
    ppermute x49, starting transfers between devices: 71 us -> 75.4 us  [permute(): return lax.ppermute(arr, AXES, pairs)]
    pallas_call x1, Pallas kernels: 7.95 us -> 5.35 us  [partials(): pl.pallas_call(kernel, out_shape=[jax.ShapeDtypeStruct(s, BF) for s in sh...]
  transfers between devices with their start and end apart: 49 -> 49, of which waited for: 27 -> 30; matrix products, arithmetic and copies ran while one was open for 3% -> 4% of each run, Pallas kernels for 3% -> 4%
where the time goes in v5:
time: 188 us
  waiting for transfers between devices  78.9 us (42%)
  starting transfers between devices  75.4 us (40%)
  Pallas kernels  23 us (12%)
  other arithmetic  5.96 us (3%)
  local copies, waits for them, and re-layouts  3.67 us (2%)
    ppermute x49, waiting for transfers between devices, permute(): return lax.ppermute(arr, AXES, pairs)  78.9 us
    ppermute x49, starting transfers between devices, permute(): return lax.ppermute(arr, AXES, pairs)  75.4 us
    pallas_call x1, Pallas kernels, updates(): pl.pallas_call(kernel, out_shape=jax.ShapeDtypeStruct((rows, ffw), BF), i...  5.57 us
    pallas_call x1, Pallas kernels, partials(): pl.pallas_call(kernel, out_shape=[jax.ShapeDtypeStruct(s, BF) for s in sh...  5.35 us
    pallas_call x6, Pallas kernels, place(): pl.pallas_call(kernel, out_shape=jax.ShapeDtypeStruct((64, rows, cols), B...  5.3 us
    pallas_call x1, Pallas kernels, load(): pl.pallas_call(kernel, out_shape=[jax.ShapeDtypeStruct(a.shape, a.dtype)...  4.43 us
  transfers between devices with their start and end apart: 49, of which 30 were waited for; matrix products, arithmetic and copies ran while one was open for 4% of the time, Pallas kernels for 4%

profile of v5, /device:TPU:1, one launch (start us, length us, event | category | flops | bytes accessed | tf_op | source)
XLA Modules:
  0.0 188.1 jit_solution(17180392697779143630)
XLA Ops:
  0.6 1.5 collective-permute-start.11
  3.1 1.7 collective-permute-start
  4.8 1.7 collective-permute-done
  10.4 2.0 %collective-permute-done.2 = bf16[2,128,256]{2,1,0:T(8,128)(2,1)S(1)} collective-permute-done((bf16[2,128,256]{2,1,0:T(8,128)(2,1)S(1)}, bf16[2,128,256]{2,1,0:T(8,128)(2,1)S(1)}, u32[]{:S(2)}, u32[]{:S(2)}) %collective-permute-start.2) | collective-permute-done | bytes 131104 | tf_op jit(solution)/shard_map/ppermute | solution.py:38
  12.4 1.4 collective-permute-done.3
  13.8 4.0 %collective-permute-start.4 = (bf16[3,128,256]{2,1,0:T(8,128)(2,1)S(1)}, bf16[3,128,256]{2,1,0:T(8,128)(2,1)S(1)}, u32[]{:S(2)}, u32[]{:S(2)}) collective-permute-start(bf16[3,128,256]{2,1,0:T(8,128)(2,1)S(1)} %get-tuple-element.65), channel_id=1, source_target_pairs={{0,64},{64,0},{1,65},{65,1},{2,66},{66,2},{3,67},{67,3},{4,68},{68... | collective-permute-start | bytes 589832 | tf_op jit(solution)/shard_map/ppermute | solution.py:38
  17.8 1.5 collective-permute-start.5
  19.3 1.9 %collective-permute-start.6 = (bf16[2,128,256]{2,1,0:T(8,128)(2,1)S(1)}, bf16[2,128,256]{2,1,0:T(8,128)(2,1)S(1)}, u32[]{:S(2)}, u32[]{:S(2)}) collective-permute-start(bf16[2,128,256]{2,1,0:T(8,128)(2,1)S(1)} %collective-permute-done.3), channel_id=1, source_target_pairs={{0,8},{64,72},{1,9},{65,73},{2,10},{66,74},{3,11},{67,75},{4,12},{... | collective-permute-start | bytes 393224 | tf_op jit(solution)/shard_map/ppermute | solution.py:38
  21.2 3.6 %collective-permute-done.6 = bf16[2,128,256]{2,1,0:T(8,128)(2,1)S(1)} collective-permute-done((bf16[2,128,256]{2,1,0:T(8,128)(2,1)S(1)}, bf16[2,128,256]{2,1,0:T(8,128)(2,1)S(1)}, u32[]{:S(2)}, u32[]{:S(2)}) %collective-permute-start.6) | collective-permute-done | bytes 131104 | tf_op jit(solution)/shard_map/ppermute | solution.py:38
  24.9 1.5 collective-permute-start.7
  26.4 1.5 collective-permute-start.8
  30.7 3.8 %collective-permute-done.9 = bf16[2,2,128,256]{3,2,1,0:T(8,128)(2,1)S(1)} collective-permute-done((bf16[2,2,128,256]{3,2,1,0:T(8,128)(2,1)S(1)}, bf16[2,2,128,256]{3,2,1,0:T(8,128)(2,1)S(1)}, u32[]{:S(2)}, u32[]{:S(2)}) %collective-permute-start.9) | collective-permute-done | bytes 262176 | tf_op jit(solution)/shard_map/ppermute | solution.py:38
  37.0 1.8 collective-permute-start.14
  39.6 4.4 %shard_map.76 = (bf16[256,8192]{1,0:T(8,128)(2,1)S(1)}, bf16[256,14336]{1,0:T(8,128)(2,1)S(1)}) custom-call(bf16[256,8192]{1,0:T(8,128)(2,1)} %collective-permute-done.10.refs_0_, bf16[256,14336]{1,0:T(8,128)(2,1)} %collective-permute-done.11.refs_1_), custom_call_target="tpu_custom_call" | custom-call | bytes 11534336 | tf_op jit(solution)/shard_map/pallas_call | solution.py:166
  44.0 2.3 %collective-permute-done.14.refs_2_ = bf16[2,2,2,128,256]{4,3,2,1,0:T(8,128)(2,1)S(1)} collective-permute-done((bf16[2,2,2,128,256]{4,3,2,1,0:T(8,128)(2,1)S(1)}, bf16[2,2,2,128,256]{4,3,2,1,0:T(8,128)(2,1)S(1)}, u32[]{:S(2)}, u32[]{:S(2)}) %collective-permute-start.14) | collective-permute-done | bytes 524320 | tf_op jit(solution)/shard_map/ppermute | solution.py:38
  48.4 1.4 shard_map.78.b_ref
  50.9 2.4 %shard_map.79 = (bf16[256,256]{1,0:T(8,128)(2,1)S(1)}, bf16[256,256]{1,0:T(8,128)(2,1)S(1)}) custom-call(bf16[256,8192]{1,0:T(8,128)(2,1)S(1)} %copy-done, bf16[256,8192]{1,0:T(8,128)(2,1)S(1)} %get-tuple-element.74.a1_ref, bf16[64,128,256]{2,1,0:T(8,128)(2,1)S(1)} %shard_map.78.b_ref), custom_call_target="tpu_custom_call" | custom-call | flops 2147483648 | bytes 12582912 | tf_op jit(solution)/shard_map/pallas_call | solution.py:187
  53.3 5.3 %shard_map.80 = (bf16[2,2,3,224,256]{4,3,2,1,0:T(8,128)(2,1)S(1)}, bf16[2,2,3,224,256]{4,3,2,1,0:T(8,128)(2,1)S(1)}, bf16[2,2,3,224,256]{4,3,2,1,0:T(8,128)(2,1)...) custom-call(s32[4]{0:T(128)S(1)} %pad_add_fusion.pos_ref, ...), custom_call_target="tpu_custom_call" | custom-call | flops 3758096384 | bytes 22020096 | tf_op jit(solution)/shard_map/pallas_call | solution.py:225
  59.4 1.7 collective-permute-start.15
  61.1 2.1 %collective-permute-start.18 = (bf16[2,2,3,224,256]{4,3,2,1,0:T(8,128)(2,1)S(1)}, bf16[2,2,3,224,256]{4,3,2,1,0:T(8,128)(2,1)S(1)}, u32[]{:S(2)}, u32[]{:S(2)}) collective-permute-start(bf16[2,2,3,224,256]{4,3,2,1,0:T(8,128)(2,1)S(1)} %get-tuple-element.89), channel_id=1, source_target_pairs={{0,2},{64,66},{1,3},{65,67},{2,0},{66,64},{3,1},{67,65},{4,6},{68,... | collective-permute-start | bytes 4128776 | tf_op jit(solution)/shard_map/ppermute | solution.py:38
  63.2 11.4 %collective-permute-done.15 = bf16[2,2,2,224,256]{4,3,2,1,0:T(8,128)(2,1)S(1)} collective-permute-done((bf16[2,2,2,224,256]{4,3,2,1,0:T(8,128)(2,1)S(1)}, bf16[2,2,2,224,256]{4,3,2,1,0:T(8,128)(2,1)S(1)}, u32[]{:S(2)}, u32[]{:S(2)}) %collective-permute-start.15) | collective-permute-done | bytes 917536 | tf_op jit(solution)/shard_map/ppermute | solution.py:38
  74.9 2.5 %collective-permute-start.16 = (bf16[2,2,224,256]{3,2,1,0:T(8,128)(2,1)S(1)}, bf16[2,2,224,256]{3,2,1,0:T(8,128)(2,1)S(1)}, u32[]{:S(2)}, u32[]{:S(2)}) collective-permute-start(bf16[2,2,224,256]{3,2,1,0:T(8,128)(2,1)S(1)} %get-tuple-element.122), channel_id=1, source_target_pairs={{0,2},{64,66},{1,3},{65,67},{2,0},{66,64},{3,1},{67,65},{4,6},{68,... | collective-permute-start | bytes 1376264 | tf_op jit(solution)/shard_map/ppermute | solution.py:38
  79.9 3.4 %collective-permute-start.19 = (bf16[2,3,224,256]{3,2,1,0:T(8,128)(2,1)S(1)}, bf16[2,3,224,256]{3,2,1,0:T(8,128)(2,1)S(1)}, u32[]{:S(2)}, u32[]{:S(2)}) collective-permute-start(bf16[2,3,224,256]{3,2,1,0:T(8,128)(2,1)S(1)} %get-tuple-element.118), channel_id=1, source_target_pairs={{0,8},{64,72},{1,9},{65,73},{2,10},{66,74},{3,11},{67,75},{4,12},{... | collective-permute-start | bytes 2064392 | tf_op jit(solution)/shard_map/ppermute | solution.py:38
  84.4 3.8 %collective-permute-start.24 = (bf16[2,224,256]{2,1,0:T(8,128)(2,1)S(1)}, bf16[2,224,256]{2,1,0:T(8,128)(2,1)S(1)}, u32[]{:S(2)}, u32[]{:S(2)}) collective-permute-start(bf16[2,224,256]{2,1,0:T(8,128)(2,1)S(1)} %fusion.35), channel_id=1, source_target_pairs={{0,8},{64,72},{1,9},{65,73},{2,10},{66,74},{3,11},{67,75},{4,12},{... | collective-permute-start | bytes 688136 | tf_op jit(solution)/shard_map/ppermute | solution.py:38
  89.0 2.0 %collective-permute-start.23 = (bf16[3,224,256]{2,1,0:T(8,128)(2,1)S(1)}, bf16[3,224,256]{2,1,0:T(8,128)(2,1)S(1)}, u32[]{:S(2)}, u32[]{:S(2)}) collective-permute-start(bf16[3,224,256]{2,1,0:T(8,128)(2,1)S(1)} %fusion.33), channel_id=1, source_target_pairs={{0,2},{64,66},{1,3},{65,67},{2,0},{66,64},{3,1},{67,65},{4,6},{68,... | collective-permute-start | bytes 1032200 | tf_op jit(solution)/shard_map/ppermute | solution.py:38
  91.7 2.7 %collective-permute-start.20 = (bf16[3,224,256]{2,1,0:T(8,128)(2,1)S(1)}, bf16[3,224,256]{2,1,0:T(8,128)(2,1)S(1)}, u32[]{:S(2)}, u32[]{:S(2)}) collective-permute-start(bf16[3,224,256]{2,1,0:T(8,128)(2,1)S(1)} %fusion.31), channel_id=1, source_target_pairs={{0,64},{64,0},{1,65},{65,1},{2,66},{66,2},{3,67},{67,3},{4,68},{68... | collective-permute-start | bytes 1032200 | tf_op jit(solution)/shard_map/ppermute | solution.py:38
  94.5 1.9 %collective-permute-done.23 = bf16[3,224,256]{2,1,0:T(8,128)(2,1)S(1)} collective-permute-done((bf16[3,224,256]{2,1,0:T(8,128)(2,1)S(1)}, bf16[3,224,256]{2,1,0:T(8,128)(2,1)S(1)}, u32[]{:S(2)}, u32[]{:S(2)}) %collective-permute-start.23) | collective-permute-done | bytes 344096 | tf_op jit(solution)/shard_map/ppermute | solution.py:38
  96.6 2.5 %collective-permute-done.20 = bf16[3,224,256]{2,1,0:T(8,128)(2,1)S(1)} collective-permute-done((bf16[3,224,256]{2,1,0:T(8,128)(2,1)S(1)}, bf16[3,224,256]{2,1,0:T(8,128)(2,1)S(1)}, u32[]{:S(2)}, u32[]{:S(2)}) %collective-permute-start.20) | collective-permute-done | bytes 344096 | tf_op jit(solution)/shard_map/ppermute | solution.py:38
  99.6 2.5 %collective-permute-start.25 = (bf16[2,224,256]{2,1,0:T(8,128)(2,1)S(1)}, bf16[2,224,256]{2,1,0:T(8,128)(2,1)S(1)}, u32[]{:S(2)}, u32[]{:S(2)}) collective-permute-start(bf16[2,224,256]{2,1,0:T(8,128)(2,1)S(1)} %get-tuple-element.123), channel_id=1, source_target_pairs={{0,6},{64,70},{1,7},{65,71},{2,4},{66,68},{3,5},{67,69},{4,2},{68,... | collective-permute-start | bytes 688136 | tf_op jit(solution)/shard_map/ppermute | solution.py:38
  102.1 3.2 %collective-permute-done.27 = bf16[2,224,256]{2,1,0:T(8,128)(2,1)S(1)} collective-permute-done((bf16[2,224,256]{2,1,0:T(8,128)(2,1)S(1)}, bf16[2,224,256]{2,1,0:T(8,128)(2,1)S(1)}, u32[]{:S(2)}, u32[]{:S(2)}) %collective-permute-start.27) | collective-permute-done | bytes 229408 | tf_op jit(solution)/shard_map/ppermute | solution.py:38
  105.3 1.5 collective-permute-done.26
  107.1 5.2 %collective-permute-done.28 = bf16[2,224,256]{2,1,0:T(8,128)(2,1)S(1)} collective-permute-done((bf16[2,224,256]{2,1,0:T(8,128)(2,1)S(1)}, bf16[2,224,256]{2,1,0:T(8,128)(2,1)S(1)}, u32[]{:S(2)}, u32[]{:S(2)}) %collective-permute-start.28) | collective-permute-done | bytes 229408 | tf_op jit(solution)/shard_map/ppermute | solution.py:38
  112.7 10.8 %collective-permute-start.32 = (bf16[224,256]{1,0:T(8,128)(2,1)S(1)}, bf16[224,256]{1,0:T(8,128)(2,1)S(1)}, u32[]{:S(2)}, u32[]{:S(2)}) collective-permute-start(bf16[224,256]{1,0:T(8,128)(2,1)S(1)} %slice_bitcast_fusion.12), channel_id=1, source_target_pairs={{0,32},{64,96},{1,33},{65,97},{2,34},{66,98},{3,35},{67,99},{4,36}... | collective-permute-start | bytes 344072 | tf_op jit(solution)/shard_map/ppermute | solution.py:38
  124.5 1.7 collective-permute-start.31
  126.2 2.4 %collective-permute-done.29 = bf16[2,224,256]{2,1,0:T(8,128)(2,1)S(1)} collective-permute-done((bf16[2,224,256]{2,1,0:T(8,128)(2,1)S(1)}, bf16[2,224,256]{2,1,0:T(8,128)(2,1)S(1)}, u32[]{:S(2)}, u32[]{:S(2)}) %collective-permute-start.29) | collective-permute-done | bytes 229408 | tf_op jit(solution)/shard_map/ppermute | solution.py:38
  129.2 2.6 %collective-permute-done.31 = bf16[2,224,256]{2,1,0:T(8,128)(2,1)S(1)} collective-permute-done((bf16[2,224,256]{2,1,0:T(8,128)(2,1)S(1)}, bf16[2,224,256]{2,1,0:T(8,128)(2,1)S(1)}, u32[]{:S(2)}, u32[]{:S(2)}) %collective-permute-start.31) | collective-permute-done | bytes 229408 | tf_op jit(solution)/shard_map/ppermute | solution.py:38
  133.0 2.4 %collective-permute-start.33 = (bf16[3,224,256]{2,1,0:T(8,128)(2,1)S(1)}, bf16[3,224,256]{2,1,0:T(8,128)(2,1)S(1)}, u32[]{:S(2)}, u32[]{:S(2)}) collective-permute-start(bf16[3,224,256]{2,1,0:T(8,128)(2,1)S(1)} %get-tuple-element.98), channel_id=1, source_target_pairs={{0,64},{64,0},{1,65},{65,1},{2,66},{66,2},{3,67},{67,3},{4,68},{68... | collective-permute-start | bytes 1032200 | tf_op jit(solution)/shard_map/ppermute | solution.py:38
  135.4 1.7 collective-permute-start.34
  138.2 5.0 %collective-permute-done.35 = bf16[2,224,256]{2,1,0:T(8,128)(2,1)S(1)} collective-permute-done((bf16[2,224,256]{2,1,0:T(8,128)(2,1)S(1)}, bf16[2,224,256]{2,1,0:T(8,128)(2,1)S(1)}, u32[]{:S(2)}, u32[]{:S(2)}) %collective-permute-start.35) | collective-permute-done | bytes 229408 | tf_op jit(solution)/shard_map/ppermute | solution.py:38
  145.0 1.5 collective-permute-start.39
  146.5 7.1 %collective-permute-done.39 = bf16[2,2,224,256]{3,2,1,0:T(8,128)(2,1)S(1)} collective-permute-done((bf16[2,2,224,256]{3,2,1,0:T(8,128)(2,1)S(1)}, bf16[2,2,224,256]{3,2,1,0:T(8,128)(2,1)S(1)}, u32[]{:S(2)}, u32[]{:S(2)}) %collective-permute-start.39) | collective-permute-done | bytes 458784 | tf_op jit(solution)/shard_map/ppermute | solution.py:38
  155.8 1.5 collective-permute-start.40
  157.4 1.4 collective-permute-start.41
  160.2 2.3 %collective-permute-start.48 = (bf16[2,2,2,224,256]{4,3,2,1,0:T(8,128)(2,1)S(1)}, bf16[2,2,2,224,256]{4,3,2,1,0:T(8,128)(2,1)S(1)}, u32[]{:S(2)}, u32[]{:S(2)}) collective-permute-start(bf16[2,2,2,224,256]{4,3,2,1,0:T(8,128)(2,1)S(1)} %pad_maximum_fusion.3.refs_2_), channel_id=1, source_target_pairs={{0,32},{64,96},{1,33},{65,97},{2,34},{66,98},{3,35},{67,99},{4,36}... | collective-permute-start | bytes 2752520 | tf_op jit(solution)/shard_map/ppermute | solution.py:38
  162.5 9.9 %collective-permute-done.42.refs_2_ = bf16[2,2,2,224,256]{4,3,2,1,0:T(8,128)(2,1)S(1)} collective-permute-done((bf16[2,2,2,224,256]{4,3,2,1,0:T(8,128)(2,1)S(1)}, bf16[2,2,2,224,256]{4,3,2,1,0:T(8,128)(2,1)S(1)}, u32[]{:S(2)}, u32[]{:S(2)}) %collective-permute-start.42) | collective-permute-done | bytes 917536 | tf_op jit(solution)/shard_map/ppermute | solution.py:38
  176.5 1.5 fusion.1
  179.6 2.0 %collective-permute-done.45.refs_2_ = bf16[2,2,2,224,256]{4,3,2,1,0:T(8,128)(2,1)S(1)} collective-permute-done((bf16[2,2,2,224,256]{4,3,2,1,0:T(8,128)(2,1)S(1)}, bf16[2,2,2,224,256]{4,3,2,1,0:T(8,128)(2,1)S(1)}, u32[]{:S(2)}, u32[]{:S(2)}) %collective-permute-start.45) | collective-permute-done | bytes 917536 | tf_op jit(solution)/shard_map/ppermute | solution.py:38
  182.4 5.6 %shard_map.85 = bf16[256,14336]{1,0:T(8,128)(2,1)} custom-call(s32[1]{0:T(128)} %bitcast.core_ref, bf16[64,224,256]{2,1,0:T(8,128)(2,1)S(1)} %shard_map.82.own_ref, bf16[64,224,256]{2,1,0:T(8,128)(2,1)S(1)} %shard_map.84.other_ref, bf16[2,256,256]{2,1,0:T(8,128)(2,1)S(1)} %pad_maximum_fusion.17.b_ref), custom_call_target="tpu_custom_call" | custom-call | flops 3758096384 | bytes 22020096 | tf_op jit(solution)/shard_map/pallas_call | solution.py:262
  (117 shorter events, 37.2 us)
Async XLA Ops:
  0.6 33.9 %collective-permute-start.11 = (bf16[256,14336]{1,0:T(8,128)(2,1)}, bf16[256,14336]{1,0:T(8,128)(2,1)}, u32[]{:S(2)}, u32[]{:S(2)}) collective-permute-start(bf16[256,14336]{1,0:T(8,128)(2,1)} %g0_ref.1), channel_id=1, source_target_pairs={{0,32},{64,96},{1,33},{65,97},{2,34},{66,98},{3,35},{67,99},{4,36}... | collective-permute-start | bytes 22020104 | tf_op jit(solution)/shard_map/ppermute | solution.py:38
  2.1 32.4 %collective-permute-start.10 = (bf16[256,8192]{1,0:T(8,128)(2,1)}, bf16[256,8192]{1,0:T(8,128)(2,1)}, u32[]{:S(2)}, u32[]{:S(2)}) collective-permute-start(bf16[256,8192]{1,0:T(8,128)(2,1)} %a0_ref.1), channel_id=1, source_target_pairs={{0,32},{64,96},{1,33},{65,97},{2,34},{66,98},{3,35},{67,99},{4,36}... | collective-permute-start | bytes 12582920 | tf_op jit(solution)/shard_map/ppermute | solution.py:38
  6.5 3.9 %collective-permute-start.1 = (bf16[2,128,256]{2,1,0:T(8,128)(2,1)S(1)}, bf16[2,128,256]{2,1,0:T(8,128)(2,1)S(1)}, u32[]{:S(2)}, u32[]{:S(2)}) collective-permute-start(bf16[2,128,256]{2,1,0:T(8,128)(2,1)S(1)} %pad_maximum_fusion.20), channel_id=1, source_target_pairs={{0,6},{64,70},{1,7},{65,71},{2,4},{66,68},{3,5},{67,69},{4,2},{68,... | collective-permute-start | bytes 393224 | tf_op jit(solution)/shard_map/ppermute | solution.py:38
  7.8 4.6 %collective-permute-start.2 = (bf16[2,128,256]{2,1,0:T(8,128)(2,1)S(1)}, bf16[2,128,256]{2,1,0:T(8,128)(2,1)S(1)}, u32[]{:S(2)}, u32[]{:S(2)}) collective-permute-start(bf16[2,128,256]{2,1,0:T(8,128)(2,1)S(1)} %pad_maximum_fusion.20), channel_id=1, source_target_pairs={{0,24},{64,88},{1,25},{65,89},{2,26},{66,90},{3,27},{67,91},{4,28}... | collective-permute-start | bytes 393224 | tf_op jit(solution)/shard_map/ppermute | solution.py:38
  9.1 4.7 %collective-permute-start.3 = (bf16[2,128,256]{2,1,0:T(8,128)(2,1)S(1)}, bf16[2,128,256]{2,1,0:T(8,128)(2,1)S(1)}, u32[]{:S(2)}, u32[]{:S(2)}) collective-permute-start(bf16[2,128,256]{2,1,0:T(8,128)(2,1)S(1)} %pad_maximum_fusion.20), channel_id=1, source_target_pairs={{0,30},{64,94},{1,31},{65,95},{2,28},{66,92},{3,29},{67,93},{4,26}... | collective-permute-start | bytes 393224 | tf_op jit(solution)/shard_map/ppermute | solution.py:38
  13.8 11.0 %collective-permute-start.4 = (bf16[3,128,256]{2,1,0:T(8,128)(2,1)S(1)}, bf16[3,128,256]{2,1,0:T(8,128)(2,1)S(1)}, u32[]{:S(2)}, u32[]{:S(2)}) collective-permute-start(bf16[3,128,256]{2,1,0:T(8,128)(2,1)S(1)} %get-tuple-element.65), channel_id=1, source_target_pairs={{0,64},{64,0},{1,65},{65,1},{2,66},{66,2},{3,67},{67,3},{4,68},{68... | collective-permute-start | bytes 589832 | tf_op jit(solution)/shard_map/ppermute | solution.py:38
  17.8 7.0 %collective-permute-start.5 = (bf16[3,128,256]{2,1,0:T(8,128)(2,1)S(1)}, bf16[3,128,256]{2,1,0:T(8,128)(2,1)S(1)}, u32[]{:S(2)}, u32[]{:S(2)}) collective-permute-start(bf16[3,128,256]{2,1,0:T(8,128)(2,1)S(1)} %get-tuple-element.67), channel_id=1, source_target_pairs={{0,2},{64,66},{1,3},{65,67},{2,0},{66,64},{3,1},{67,65},{4,6},{68,... | collective-permute-start | bytes 589832 | tf_op jit(solution)/shard_map/ppermute | solution.py:38
  19.3 5.5 %collective-permute-start.6 = (bf16[2,128,256]{2,1,0:T(8,128)(2,1)S(1)}, bf16[2,128,256]{2,1,0:T(8,128)(2,1)S(1)}, u32[]{:S(2)}, u32[]{:S(2)}) collective-permute-start(bf16[2,128,256]{2,1,0:T(8,128)(2,1)S(1)} %collective-permute-done.3), channel_id=1, source_target_pairs={{0,8},{64,72},{1,9},{65,73},{2,10},{66,74},{3,11},{67,75},{4,12},{... | collective-permute-start | bytes 393224 | tf_op jit(solution)/shard_map/ppermute | solution.py:38
  24.9 9.6 %collective-permute-start.7 = (bf16[2,3,128,256]{3,2,1,0:T(8,128)(2,1)S(1)}, bf16[2,3,128,256]{3,2,1,0:T(8,128)(2,1)S(1)}, u32[]{:S(2)}, u32[]{:S(2)}) collective-permute-start(bf16[2,3,128,256]{3,2,1,0:T(8,128)(2,1)S(1)} %pad_maximum_fusion.12), channel_id=1, source_target_pairs={{0,8},{64,72},{1,9},{65,73},{2,10},{66,74},{3,11},{67,75},{4,12},{... | collective-permute-start | bytes 1179656 | tf_op jit(solution)/shard_map/ppermute | solution.py:38
  26.4 8.1 %collective-permute-start.8 = (bf16[2,3,128,256]{3,2,1,0:T(8,128)(2,1)S(1)}, bf16[2,3,128,256]{3,2,1,0:T(8,128)(2,1)S(1)}, u32[]{:S(2)}, u32[]{:S(2)}) collective-permute-start(bf16[2,3,128,256]{3,2,1,0:T(8,128)(2,1)S(1)} %pad_maximum_fusion.13), channel_id=1, source_target_pairs={{0,64},{64,0},{1,65},{65,1},{2,66},{66,2},{3,67},{67,3},{4,68},{68... | collective-permute-start | bytes 1179656 | tf_op jit(solution)/shard_map/ppermute | solution.py:38
  28.0 6.5 %collective-permute-start.9 = (bf16[2,2,128,256]{3,2,1,0:T(8,128)(2,1)S(1)}, bf16[2,2,128,256]{3,2,1,0:T(8,128)(2,1)S(1)}, u32[]{:S(2)}, u32[]{:S(2)}) collective-permute-start(bf16[2,2,128,256]{3,2,1,0:T(8,128)(2,1)S(1)} %pad_maximum_fusion.16), channel_id=1, source_target_pairs={{0,2},{64,66},{1,3},{65,67},{2,0},{66,64},{3,1},{67,65},{4,6},{68,... | collective-permute-start | bytes 786440 | tf_op jit(solution)/shard_map/ppermute | solution.py:38
  35.3 12.1 %collective-permute-start.12 = (bf16[2,2,3,128,256]{4,3,2,1,0:T(8,128)(2,1)S(1)}, bf16[2,2,3,128,256]{4,3,2,1,0:T(8,128)(2,1)S(1)}, u32[]{:S(2)}, u32[]{:S(2)}) collective-permute-start(bf16[2,2,3,128,256]{4,3,2,1,0:T(8,128)(2,1)S(1)} %pad_maximum_fusion.4.refs_0_), channel_id=1, source_target_pairs={{0,2},{64,66},{1,3},{65,67},{2,0},{66,64},{3,1},{67,65},{4,6},{68,... | collective-permute-start | bytes 2359304 | tf_op jit(solution)/shard_map/ppermute | solution.py:38
  36.2 12.2 %collective-permute-start.13 = (bf16[2,2,3,128,256]{4,3,2,1,0:T(8,128)(2,1)S(1)}, bf16[2,2,3,128,256]{4,3,2,1,0:T(8,128)(2,1)}, u32[]{:S(2)}, u32[]{:S(2)}) collective-permute-start(bf16[2,2,3,128,256]{4,3,2,1,0:T(8,128)(2,1)S(1)} %pad_maximum_fusion.5.refs_1_), channel_id=1, source_target_pairs={{0,8},{64,72},{1,9},{65,73},{2,10},{66,74},{3,11},{67,75},{4,12},{... | collective-permute-start | bytes 2359304 | tf_op jit(solution)/shard_map/ppermute | solution.py:38
  37.0 9.3 %collective-permute-start.14 = (bf16[2,2,2,128,256]{4,3,2,1,0:T(8,128)(2,1)S(1)}, bf16[2,2,2,128,256]{4,3,2,1,0:T(8,128)(2,1)S(1)}, u32[]{:S(2)}, u32[]{:S(2)}) collective-permute-start(bf16[2,2,2,128,256]{4,3,2,1,0:T(8,128)(2,1)S(1)} %pad_maximum_fusion.8.refs_2_), channel_id=1, source_target_pairs={{0,64},{64,0},{1,65},{65,1},{2,66},{66,2},{3,67},{67,3},{4,68},{68... | collective-permute-start | bytes 1572872 | tf_op jit(solution)/shard_map/ppermute | solution.py:38
  58.6 18.8 %collective-permute-start.21 = (bf16[2,2,3,224,256]{4,3,2,1,0:T(8,128)(2,1)S(1)}, bf16[2,2,3,224,256]{4,3,2,1,0:T(8,128)(2,1)S(1)}, u32[]{:S(2)}, u32[]{:S(2)}) collective-permute-start(bf16[2,2,3,224,256]{4,3,2,1,0:T(8,128)(2,1)S(1)} %get-tuple-element.91), channel_id=1, source_target_pairs={{0,8},{64,72},{1,9},{65,73},{2,10},{66,74},{3,11},{67,75},{4,12},{... | collective-permute-start | bytes 4128776 | tf_op jit(solution)/shard_map/ppermute | solution.py:38
  59.4 15.2 %collective-permute-start.15 = (bf16[2,2,2,224,256]{4,3,2,1,0:T(8,128)(2,1)S(1)}, bf16[2,2,2,224,256]{4,3,2,1,0:T(8,128)(2,1)S(1)}, u32[]{:S(2)}, u32[]{:S(2)}) collective-permute-start(bf16[2,2,2,224,256]{4,3,2,1,0:T(8,128)(2,1)S(1)} %get-tuple-element.86), channel_id=1, source_target_pairs={{0,64},{64,0},{1,65},{65,1},{2,66},{66,2},{3,67},{67,3},{4,68},{68... | collective-permute-start | bytes 2752520 | tf_op jit(solution)/shard_map/ppermute | solution.py:38
  61.1 18.4 %collective-permute-start.18 = (bf16[2,2,3,224,256]{4,3,2,1,0:T(8,128)(2,1)S(1)}, bf16[2,2,3,224,256]{4,3,2,1,0:T(8,128)(2,1)S(1)}, u32[]{:S(2)}, u32[]{:S(2)}) collective-permute-start(bf16[2,2,3,224,256]{4,3,2,1,0:T(8,128)(2,1)S(1)} %get-tuple-element.89), channel_id=1, source_target_pairs={{0,2},{64,66},{1,3},{65,67},{2,0},{66,64},{3,1},{67,65},{4,6},{68,... | collective-permute-start | bytes 4128776 | tf_op jit(solution)/shard_map/ppermute | solution.py:38
  63.2 20.1 %collective-permute-start.17 = (f32[2,224,256]{2,1,0:T(8,128)S(1)}, f32[2,224,256]{2,1,0:T(8,128)S(1)}, u32[]{:S(2)}, u32[]{:S(2)}) collective-permute-start(f32[2,224,256]{2,1,0:T(8,128)S(1)} %copy-done.1), channel_id=1, source_target_pairs={{0,65},{64,1},{1,64},{65,0},{2,67},{66,3},{3,66},{67,2},{4,69},{68... | collective-permute-start | bytes 1376264 | tf_op jit(solution)/shard_map/ppermute | solution.py:38
  74.9 9.5 %collective-permute-start.16 = (bf16[2,2,224,256]{3,2,1,0:T(8,128)(2,1)S(1)}, bf16[2,2,224,256]{3,2,1,0:T(8,128)(2,1)S(1)}, u32[]{:S(2)}, u32[]{:S(2)}) collective-permute-start(bf16[2,2,224,256]{3,2,1,0:T(8,128)(2,1)S(1)} %get-tuple-element.122), channel_id=1, source_target_pairs={{0,2},{64,66},{1,3},{65,67},{2,0},{66,64},{3,1},{67,65},{4,6},{68,... | collective-permute-start | bytes 1376264 | tf_op jit(solution)/shard_map/ppermute | solution.py:38
  77.9 11.1 %collective-permute-start.22 = (bf16[2,3,224,256]{3,2,1,0:T(8,128)(2,1)S(1)}, bf16[2,3,224,256]{3,2,1,0:T(8,128)(2,1)S(1)}, u32[]{:S(2)}, u32[]{:S(2)}) collective-permute-start(bf16[2,3,224,256]{3,2,1,0:T(8,128)(2,1)S(1)} %get-tuple-element.120), channel_id=1, source_target_pairs={{0,64},{64,0},{1,65},{65,1},{2,66},{66,2},{3,67},{67,3},{4,68},{68... | collective-permute-start | bytes 2064392 | tf_op jit(solution)/shard_map/ppermute | solution.py:38
  79.9 11.7 %collective-permute-start.19 = (bf16[2,3,224,256]{3,2,1,0:T(8,128)(2,1)S(1)}, bf16[2,3,224,256]{3,2,1,0:T(8,128)(2,1)S(1)}, u32[]{:S(2)}, u32[]{:S(2)}) collective-permute-start(bf16[2,3,224,256]{3,2,1,0:T(8,128)(2,1)S(1)} %get-tuple-element.118), channel_id=1, source_target_pairs={{0,8},{64,72},{1,9},{65,73},{2,10},{66,74},{3,11},{67,75},{4,12},{... | collective-permute-start | bytes 2064392 | tf_op jit(solution)/shard_map/ppermute | solution.py:38
  84.4 10.0 %collective-permute-start.24 = (bf16[2,224,256]{2,1,0:T(8,128)(2,1)S(1)}, bf16[2,224,256]{2,1,0:T(8,128)(2,1)S(1)}, u32[]{:S(2)}, u32[]{:S(2)}) collective-permute-start(bf16[2,224,256]{2,1,0:T(8,128)(2,1)S(1)} %fusion.35), channel_id=1, source_target_pairs={{0,8},{64,72},{1,9},{65,73},{2,10},{66,74},{3,11},{67,75},{4,12},{... | collective-permute-start | bytes 688136 | tf_op jit(solution)/shard_map/ppermute | solution.py:38
  89.0 7.4 %collective-permute-start.23 = (bf16[3,224,256]{2,1,0:T(8,128)(2,1)S(1)}, bf16[3,224,256]{2,1,0:T(8,128)(2,1)S(1)}, u32[]{:S(2)}, u32[]{:S(2)}) collective-permute-start(bf16[3,224,256]{2,1,0:T(8,128)(2,1)S(1)} %fusion.33), channel_id=1, source_target_pairs={{0,2},{64,66},{1,3},{65,67},{2,0},{66,64},{3,1},{67,65},{4,6},{68,... | collective-permute-start | bytes 1032200 | tf_op jit(solution)/shard_map/ppermute | solution.py:38
  91.7 7.4 %collective-permute-start.20 = (bf16[3,224,256]{2,1,0:T(8,128)(2,1)S(1)}, bf16[3,224,256]{2,1,0:T(8,128)(2,1)S(1)}, u32[]{:S(2)}, u32[]{:S(2)}) collective-permute-start(bf16[3,224,256]{2,1,0:T(8,128)(2,1)S(1)} %fusion.31), channel_id=1, source_target_pairs={{0,64},{64,0},{1,65},{65,1},{2,66},{66,2},{3,67},{67,3},{4,68},{68... | collective-permute-start | bytes 1032200 | tf_op jit(solution)/shard_map/ppermute | solution.py:38
  99.4 6.0 %collective-permute-start.27 = (bf16[2,224,256]{2,1,0:T(8,128)(2,1)S(1)}, bf16[2,224,256]{2,1,0:T(8,128)(2,1)S(1)}, u32[]{:S(2)}, u32[]{:S(2)}) collective-permute-start(bf16[2,224,256]{2,1,0:T(8,128)(2,1)S(1)} %get-tuple-element.124), channel_id=1, source_target_pairs={{0,30},{64,94},{1,31},{65,95},{2,28},{66,92},{3,29},{67,93},{4,26}... | collective-permute-start | bytes 688136 | tf_op jit(solution)/shard_map/ppermute | solution.py:38
  99.5 7.4 %collective-permute-start.26 = (bf16[2,224,256]{2,1,0:T(8,128)(2,1)S(1)}, bf16[2,224,256]{2,1,0:T(8,128)(2,1)S(1)}, u32[]{:S(2)}, u32[]{:S(2)}) collective-permute-start(bf16[2,224,256]{2,1,0:T(8,128)(2,1)S(1)} %get-tuple-element.125), channel_id=1, source_target_pairs={{0,24},{64,88},{1,25},{65,89},{2,26},{66,90},{3,27},{67,91},{4,28}... | collective-permute-start | bytes 688136 | tf_op jit(solution)/shard_map/ppermute | solution.py:38
  99.6 7.3 %collective-permute-start.25 = (bf16[2,224,256]{2,1,0:T(8,128)(2,1)S(1)}, bf16[2,224,256]{2,1,0:T(8,128)(2,1)S(1)}, u32[]{:S(2)}, u32[]{:S(2)}) collective-permute-start(bf16[2,224,256]{2,1,0:T(8,128)(2,1)S(1)} %get-tuple-element.123), channel_id=1, source_target_pairs={{0,6},{64,70},{1,7},{65,71},{2,4},{66,68},{3,5},{67,69},{4,2},{68,... | collective-permute-start | bytes 688136 | tf_op jit(solution)/shard_map/ppermute | solution.py:38
  107.0 5.2 %collective-permute-start.28 = (bf16[2,224,256]{2,1,0:T(8,128)(2,1)S(1)}, bf16[2,224,256]{2,1,0:T(8,128)(2,1)S(1)}, u32[]{:S(2)}, u32[]{:S(2)}) collective-permute-start(bf16[2,224,256]{2,1,0:T(8,128)(2,1)S(1)} %fusion.25), channel_id=1, source_target_pairs={{0,65},{64,1},{1,64},{65,0},{2,67},{66,3},{3,66},{67,2},{4,69},{68... | collective-permute-start | bytes 688136 | tf_op jit(solution)/shard_map/ppermute | solution.py:38
  112.7 13.5 %collective-permute-start.32 = (bf16[224,256]{1,0:T(8,128)(2,1)S(1)}, bf16[224,256]{1,0:T(8,128)(2,1)S(1)}, u32[]{:S(2)}, u32[]{:S(2)}) collective-permute-start(bf16[224,256]{1,0:T(8,128)(2,1)S(1)} %slice_bitcast_fusion.12), channel_id=1, source_target_pairs={{0,32},{64,96},{1,33},{65,97},{2,34},{66,98},{3,35},{67,99},{4,36}... | collective-permute-start | bytes 344072 | tf_op jit(solution)/shard_map/ppermute | solution.py:38
  123.5 5.2 %collective-permute-start.29 = (bf16[2,224,256]{2,1,0:T(8,128)(2,1)S(1)}, bf16[2,224,256]{2,1,0:T(8,128)(2,1)S(1)}, u32[]{:S(2)}, u32[]{:S(2)}) collective-permute-start(bf16[2,224,256]{2,1,0:T(8,128)(2,1)S(1)} %get-tuple-element.93), channel_id=1, source_target_pairs={{0,6},{64,70},{1,7},{65,71},{2,4},{66,68},{3,5},{67,69},{4,2},{68,... | collective-permute-start | bytes 688136 | tf_op jit(solution)/shard_map/ppermute | solution.py:38
  124.1 5.2 %collective-permute-start.30 = (bf16[2,224,256]{2,1,0:T(8,128)(2,1)S(1)}, bf16[2,224,256]{2,1,0:T(8,128)(2,1)S(1)}, u32[]{:S(2)}, u32[]{:S(2)}) collective-permute-start(bf16[2,224,256]{2,1,0:T(8,128)(2,1)S(1)} %get-tuple-element.93), channel_id=1, source_target_pairs={{0,24},{64,88},{1,25},{65,89},{2,26},{66,90},{3,27},{67,91},{4,28}... | collective-permute-start | bytes 688136 | tf_op jit(solution)/shard_map/ppermute | solution.py:38
  124.5 7.3 %collective-permute-start.31 = (bf16[2,224,256]{2,1,0:T(8,128)(2,1)S(1)}, bf16[2,224,256]{2,1,0:T(8,128)(2,1)S(1)}, u32[]{:S(2)}, u32[]{:S(2)}) collective-permute-start(bf16[2,224,256]{2,1,0:T(8,128)(2,1)S(1)} %get-tuple-element.93), channel_id=1, source_target_pairs={{0,30},{64,94},{1,31},{65,95},{2,28},{66,92},{3,29},{67,93},{4,26}... | collective-permute-start | bytes 688136 | tf_op jit(solution)/shard_map/ppermute | solution.py:38
  131.8 6.2 %collective-permute-start.36 = (bf16[224,512]{1,0:T(8,128)(2,1)S(1)}, bf16[224,512]{1,0:T(8,128)(2,1)S(1)}, u32[]{:S(2)}, u32[]{:S(2)}) collective-permute-start(bf16[224,512]{1,0:T(8,128)(2,1)S(1)} %maximum_select_fusion.1), channel_id=1, source_target_pairs={{0,64},{64,0},{1,65},{65,1},{2,66},{66,2},{3,67},{67,3},{4,68},{68... | collective-permute-start | bytes 688136 | tf_op jit(solution)/shard_map/ppermute | solution.py:38
  133.0 10.2 %collective-permute-start.33 = (bf16[3,224,256]{2,1,0:T(8,128)(2,1)S(1)}, bf16[3,224,256]{2,1,0:T(8,128)(2,1)S(1)}, u32[]{:S(2)}, u32[]{:S(2)}) collective-permute-start(bf16[3,224,256]{2,1,0:T(8,128)(2,1)S(1)} %get-tuple-element.98), channel_id=1, source_target_pairs={{0,64},{64,0},{1,65},{65,1},{2,66},{66,2},{3,67},{67,3},{4,68},{68... | collective-permute-start | bytes 1032200 | tf_op jit(solution)/shard_map/ppermute | solution.py:38
  135.4 7.8 %collective-permute-start.34 = (bf16[3,224,256]{2,1,0:T(8,128)(2,1)S(1)}, bf16[3,224,256]{2,1,0:T(8,128)(2,1)S(1)}, u32[]{:S(2)}, u32[]{:S(2)}) collective-permute-start(bf16[3,224,256]{2,1,0:T(8,128)(2,1)S(1)} %get-tuple-element.100), channel_id=1, source_target_pairs={{0,2},{64,66},{1,3},{65,67},{2,0},{66,64},{3,1},{67,65},{4,6},{68,... | collective-permute-start | bytes 1032200 | tf_op jit(solution)/shard_map/ppermute | solution.py:38
  137.1 6.1 %collective-permute-start.35 = (bf16[2,224,256]{2,1,0:T(8,128)(2,1)S(1)}, bf16[2,224,256]{2,1,0:T(8,128)(2,1)S(1)}, u32[]{:S(2)}, u32[]{:S(2)}) collective-permute-start(bf16[2,224,256]{2,1,0:T(8,128)(2,1)S(1)} %collective-permute-done.31), channel_id=1, source_target_pairs={{0,8},{64,72},{1,9},{65,73},{2,10},{66,74},{3,11},{67,75},{4,12},{... | collective-permute-start | bytes 688136 | tf_op jit(solution)/shard_map/ppermute | solution.py:38
  143.3 11.1 %collective-permute-start.37 = (bf16[2,3,224,256]{3,2,1,0:T(8,128)(2,1)S(1)}, bf16[2,3,224,256]{3,2,1,0:T(8,128)(2,1)S(1)}, u32[]{:S(2)}, u32[]{:S(2)}) collective-permute-start(bf16[2,3,224,256]{3,2,1,0:T(8,128)(2,1)S(1)} %pad_maximum_fusion.6), channel_id=1, source_target_pairs={{0,8},{64,72},{1,9},{65,73},{2,10},{66,74},{3,11},{67,75},{4,12},{... | collective-permute-start | bytes 2064392 | tf_op jit(solution)/shard_map/ppermute | solution.py:38
  144.6 11.1 %collective-permute-start.38 = (bf16[2,3,224,256]{3,2,1,0:T(8,128)(2,1)S(1)}, bf16[2,3,224,256]{3,2,1,0:T(8,128)(2,1)S(1)}, u32[]{:S(2)}, u32[]{:S(2)}) collective-permute-start(bf16[2,3,224,256]{3,2,1,0:T(8,128)(2,1)S(1)} %pad_maximum_fusion.7), channel_id=1, source_target_pairs={{0,64},{64,0},{1,65},{65,1},{2,66},{66,2},{3,67},{67,3},{4,68},{68... | collective-permute-start | bytes 2064392 | tf_op jit(solution)/shard_map/ppermute | solution.py:38
  145.0 8.6 %collective-permute-start.39 = (bf16[2,2,224,256]{3,2,1,0:T(8,128)(2,1)S(1)}, bf16[2,2,224,256]{3,2,1,0:T(8,128)(2,1)S(1)}, u32[]{:S(2)}, u32[]{:S(2)}) collective-permute-start(bf16[2,2,224,256]{3,2,1,0:T(8,128)(2,1)S(1)} %pad_maximum_fusion.11), channel_id=1, source_target_pairs={{0,2},{64,66},{1,3},{65,67},{2,0},{66,64},{3,1},{67,65},{4,6},{68,... | collective-permute-start | bytes 1376264 | tf_op jit(solution)/shard_map/ppermute | solution.py:38
  155.8 18.5 %collective-permute-start.40 = (bf16[2,2,3,224,256]{4,3,2,1,0:T(8,128)(2,1)S(1)}, bf16[2,2,3,224,256]{4,3,2,1,0:T(8,128)(2,1)S(1)}, u32[]{:S(2)}, u32[]{:S(2)}) collective-permute-start(bf16[2,2,3,224,256]{4,3,2,1,0:T(8,128)(2,1)S(1)} %pad_maximum_fusion.refs_0_), channel_id=1, source_target_pairs={{0,2},{64,66},{1,3},{65,67},{2,0},{66,64},{3,1},{67,65},{4,6},{68,... | collective-permute-start | bytes 4128776 | tf_op jit(solution)/shard_map/ppermute | solution.py:38
  157.4 18.5 %collective-permute-start.41 = (bf16[2,2,3,224,256]{4,3,2,1,0:T(8,128)(2,1)S(1)}, bf16[2,2,3,224,256]{4,3,2,1,0:T(8,128)(2,1)S(1)}, u32[]{:S(2)}, u32[]{:S(2)}) collective-permute-start(bf16[2,2,3,224,256]{4,3,2,1,0:T(8,128)(2,1)S(1)} %pad_maximum_fusion.1.refs_1_), channel_id=1, source_target_pairs={{0,8},{64,72},{1,9},{65,73},{2,10},{66,74},{3,11},{67,75},{4,12},{... | collective-permute-start | bytes 4128776 | tf_op jit(solution)/shard_map/ppermute | solution.py:38
  158.9 13.5 %collective-permute-start.42 = (bf16[2,2,2,224,256]{4,3,2,1,0:T(8,128)(2,1)S(1)}, bf16[2,2,2,224,256]{4,3,2,1,0:T(8,128)(2,1)S(1)}, u32[]{:S(2)}, u32[]{:S(2)}) collective-permute-start(bf16[2,2,2,224,256]{4,3,2,1,0:T(8,128)(2,1)S(1)} %pad_maximum_fusion.3.refs_2_), channel_id=1, source_target_pairs={{0,64},{64,0},{1,65},{65,1},{2,66},{66,2},{3,67},{67,3},{4,68},{68... | collective-permute-start | bytes 2752520 | tf_op jit(solution)/shard_map/ppermute | solution.py:38
  160.2 16.1 %collective-permute-start.48 = (bf16[2,2,2,224,256]{4,3,2,1,0:T(8,128)(2,1)S(1)}, bf16[2,2,2,224,256]{4,3,2,1,0:T(8,128)(2,1)S(1)}, u32[]{:S(2)}, u32[]{:S(2)}) collective-permute-start(bf16[2,2,2,224,256]{4,3,2,1,0:T(8,128)(2,1)S(1)} %pad_maximum_fusion.3.refs_2_), channel_id=1, source_target_pairs={{0,32},{64,96},{1,33},{65,97},{2,34},{66,98},{3,35},{67,99},{4,36}... | collective-permute-start | bytes 2752520 | tf_op jit(solution)/shard_map/ppermute | solution.py:38
  162.5 16.4 %collective-permute-start.46 = (bf16[2,2,3,224,256]{4,3,2,1,0:T(8,128)(2,1)S(1)}, bf16[2,2,3,224,256]{4,3,2,1,0:T(8,128)(2,1)S(1)}, u32[]{:S(2)}, u32[]{:S(2)}) collective-permute-start(bf16[2,2,3,224,256]{4,3,2,1,0:T(8,128)(2,1)S(1)} %pad_maximum_fusion.refs_0_), channel_id=1, source_target_pairs={{0,32},{64,96},{1,33},{65,97},{2,34},{66,98},{3,35},{67,99},{4,36}... | collective-permute-start | bytes 4128776 | tf_op jit(solution)/shard_map/ppermute | solution.py:38
  172.5 6.4 %collective-permute-start.47 = (bf16[2,2,3,224,256]{4,3,2,1,0:T(8,128)(2,1)S(1)}, bf16[2,2,3,224,256]{4,3,2,1,0:T(8,128)(2,1)S(1)}, u32[]{:S(2)}, u32[]{:S(2)}) collective-permute-start(bf16[2,2,3,224,256]{4,3,2,1,0:T(8,128)(2,1)S(1)} %pad_maximum_fusion.1.refs_1_), channel_id=1, source_target_pairs={{0,32},{64,96},{1,33},{65,97},{2,34},{66,98},{3,35},{67,99},{4,36}... | collective-permute-start | bytes 4128776 | tf_op jit(solution)/shard_map/ppermute | solution.py:38
  174.2 7.4 %collective-permute-start.43 = (bf16[2,2,3,224,256]{4,3,2,1,0:T(8,128)(2,1)S(1)}, bf16[2,2,3,224,256]{4,3,2,1,0:T(8,128)(2,1)S(1)}, u32[]{:S(2)}, u32[]{:S(2)}) collective-permute-start(bf16[2,2,3,224,256]{4,3,2,1,0:T(8,128)(2,1)S(1)} %collective-permute-done.40.refs_0_), channel_id=1, source_target_pairs={{0,32},{64,96},{1,33},{65,97},{2,34},{66,98},{3,35},{67,99},{4,36}... | collective-permute-start | bytes 4128776 | tf_op jit(solution)/shard_map/ppermute | solution.py:38
  175.9 5.7 %collective-permute-start.44 = (bf16[2,2,3,224,256]{4,3,2,1,0:T(8,128)(2,1)S(1)}, bf16[2,2,3,224,256]{4,3,2,1,0:T(8,128)(2,1)S(1)}, u32[]{:S(2)}, u32[]{:S(2)}) collective-permute-start(bf16[2,2,3,224,256]{4,3,2,1,0:T(8,128)(2,1)S(1)} %collective-permute-done.41.refs_1_), channel_id=1, source_target_pairs={{0,32},{64,96},{1,33},{65,97},{2,34},{66,98},{3,35},{67,99},{4,36}... | collective-permute-start | bytes 4128776 | tf_op jit(solution)/shard_map/ppermute | solution.py:38
  176.3 5.3 %collective-permute-start.45 = (bf16[2,2,2,224,256]{4,3,2,1,0:T(8,128)(2,1)S(1)}, bf16[2,2,2,224,256]{4,3,2,1,0:T(8,128)(2,1)S(1)}, u32[]{:S(2)}, u32[]{:S(2)}) collective-permute-start(bf16[2,2,2,224,256]{4,3,2,1,0:T(8,128)(2,1)S(1)} %collective-permute-done.42.refs_2_), channel_id=1, source_target_pairs={{0,32},{64,96},{1,33},{65,97},{2,34},{66,98},{3,35},{67,99},{4,36}... | collective-permute-start | bytes 2752520 | tf_op jit(solution)/shard_map/ppermute | solution.py:38
  (10 other events, 76.2 us)

commit v6 on v5

--- a/solution.py
+++ b/solution.py
@@ -76,12 +76,12 @@
     tied = ()
     if piece.ndim == 2:
         ((piece,),) = join([piece], [swap(piece, "z", late=1)])
-    gots = [swap(piece, axes, late=1) for axes in ("x", "y", "xy")]
+    gots = [swap(piece, axes, late=1) for axes in ("xy", "x", "y")]
     if beside:
         tied = beside[0](*tied)
     blocks = lax.optimization_barrier((piece, *gots, *tied))
     tied, beside = blocks[4:], beside[1:]
-    piece = jnp.concatenate(blocks[:4])
+    piece = jnp.concatenate([blocks[0], blocks[2], blocks[3], blocks[1]])
     parts = [piece[begin:end] for begin, end in PARTS]
     for stage in (2, 1):
         gots = [swap(part, order[stage]) for order, part in zip(ORDERS, parts)]

time: 188 us -> 187 us (level)
  starting transfers between devices: 75.4 us -> 68.5 us
  waiting for transfers between devices: 78.9 us -> 85 us
    ppermute x49, starting transfers between devices: 75.4 us -> 68.5 us  [permute(): return lax.ppermute(arr, AXES, pairs)]
    ppermute x49, waiting for transfers between devices: 78.9 us -> 85 us  [permute(): return lax.ppermute(arr, AXES, pairs)]
  transfers between devices with their start and end apart: 49 -> 49, of which waited for: 30 -> 31; matrix products, arithmetic and copies ran while one was open for 4% -> 4% of each run, Pallas kernels for 4% -> 4%
where the time goes in v6:
time: 187 us
  waiting for transfers between devices  85 us (45%)
  starting transfers between devices  68.5 us (37%)
  Pallas kernels  23 us (12%)
  other arithmetic  5.96 us (3%)
  local copies, waits for them, and re-layouts  3.01 us (2%)
    ppermute x49, waiting for transfers between devices, permute(): return lax.ppermute(arr, AXES, pairs)  85 us
    ppermute x49, starting transfers between devices, permute(): return lax.ppermute(arr, AXES, pairs)  68.5 us
    pallas_call x1, Pallas kernels, updates(): pl.pallas_call(kernel, out_shape=jax.ShapeDtypeStruct((rows, ffw), BF), i...  5.56 us
    pallas_call x1, Pallas kernels, partials(): pl.pallas_call(kernel, out_shape=[jax.ShapeDtypeStruct(s, BF) for s in sh...  5.35 us
    pallas_call x6, Pallas kernels, place(): pl.pallas_call(kernel, out_shape=jax.ShapeDtypeStruct((64, rows, cols), B...  5.3 us
    pallas_call x1, Pallas kernels, load(): pl.pallas_call(kernel, out_shape=[jax.ShapeDtypeStruct(a.shape, a.dtype)...  4.43 us
  transfers between devices with their start and end apart: 49, of which 31 were waited for; matrix products, arithmetic and copies ran while one was open for 4% of the time, Pallas kernels for 4%

profile of v6, /device:TPU:1, one launch (start us, length us, event | category | flops | bytes accessed | tf_op | source)
XLA Modules:
  0.0 186.7 jit_solution(15016710792982454063)
XLA Ops:
  0.6 1.5 collective-permute-start.11
  3.1 1.7 collective-permute-start
  4.8 1.7 collective-permute-done
  6.5 2.3 %collective-permute-start.1 = (bf16[2,128,256]{2,1,0:T(8,128)(2,1)S(1)}, bf16[2,128,256]{2,1,0:T(8,128)(2,1)S(1)}, u32[]{:S(2)}, u32[]{:S(2)}) collective-permute-start(bf16[2,128,256]{2,1,0:T(8,128)(2,1)S(1)} %pad_maximum_fusion.20), channel_id=1, source_target_pairs={{0,30},{64,94},{1,31},{65,95},{2,28},{66,92},{3,29},{67,93},{4,26}... | collective-permute-start | bytes 393224 | tf_op jit(solution)/shard_map/ppermute | solution.py:38
  9.2 2.1 %collective-permute-done.1 = bf16[2,128,256]{2,1,0:T(8,128)(2,1)S(1)} collective-permute-done((bf16[2,128,256]{2,1,0:T(8,128)(2,1)S(1)}, bf16[2,128,256]{2,1,0:T(8,128)(2,1)S(1)}, u32[]{:S(2)}, u32[]{:S(2)}) %collective-permute-start.1) | collective-permute-done | bytes 131104 | tf_op jit(solution)/shard_map/ppermute | solution.py:38
  11.3 1.5 collective-permute-done.2
  12.9 3.7 %collective-permute-start.4 = (bf16[3,128,256]{2,1,0:T(8,128)(2,1)S(1)}, bf16[3,128,256]{2,1,0:T(8,128)(2,1)S(1)}, u32[]{:S(2)}, u32[]{:S(2)}) collective-permute-start(bf16[3,128,256]{2,1,0:T(8,128)(2,1)S(1)} %get-tuple-element.65), channel_id=1, source_target_pairs={{0,64},{64,0},{1,65},{65,1},{2,66},{66,2},{3,67},{67,3},{4,68},{68... | collective-permute-start | bytes 589832 | tf_op jit(solution)/shard_map/ppermute | solution.py:38
  16.6 2.5 %collective-permute-start.5 = (bf16[3,128,256]{2,1,0:T(8,128)(2,1)S(1)}, bf16[3,128,256]{2,1,0:T(8,128)(2,1)S(1)}, u32[]{:S(2)}, u32[]{:S(2)}) collective-permute-start(bf16[3,128,256]{2,1,0:T(8,128)(2,1)S(1)} %get-tuple-element.67), channel_id=1, source_target_pairs={{0,2},{64,66},{1,3},{65,67},{2,0},{66,64},{3,1},{67,65},{4,6},{68,... | collective-permute-start | bytes 589832 | tf_op jit(solution)/shard_map/ppermute | solution.py:38
  19.0 2.6 %collective-permute-start.6 = (bf16[2,128,256]{2,1,0:T(8,128)(2,1)S(1)}, bf16[2,128,256]{2,1,0:T(8,128)(2,1)S(1)}, u32[]{:S(2)}, u32[]{:S(2)}) collective-permute-start(bf16[2,128,256]{2,1,0:T(8,128)(2,1)S(1)} %collective-permute-done.1), channel_id=1, source_target_pairs={{0,8},{64,72},{1,9},{65,73},{2,10},{66,74},{3,11},{67,75},{4,12},{... | collective-permute-start | bytes 393224 | tf_op jit(solution)/shard_map/ppermute | solution.py:38
  21.6 2.5 %collective-permute-done.6 = bf16[2,128,256]{2,1,0:T(8,128)(2,1)S(1)} collective-permute-done((bf16[2,128,256]{2,1,0:T(8,128)(2,1)S(1)}, bf16[2,128,256]{2,1,0:T(8,128)(2,1)S(1)}, u32[]{:S(2)}, u32[]{:S(2)}) %collective-permute-start.6) | collective-permute-done | bytes 131104 | tf_op jit(solution)/shard_map/ppermute | solution.py:38
  24.1 2.6 %collective-permute-start.7 = (bf16[2,3,128,256]{3,2,1,0:T(8,128)(2,1)S(1)}, bf16[2,3,128,256]{3,2,1,0:T(8,128)(2,1)S(1)}, u32[]{:S(2)}, u32[]{:S(2)}) collective-permute-start(bf16[2,3,128,256]{3,2,1,0:T(8,128)(2,1)S(1)} %pad_maximum_fusion.12), channel_id=1, source_target_pairs={{0,8},{64,72},{1,9},{65,73},{2,10},{66,74},{3,11},{67,75},{4,12},{... | collective-permute-start | bytes 1179656 | tf_op jit(solution)/shard_map/ppermute | solution.py:38
  27.0 2.0 %collective-permute-start.9 = (bf16[2,2,128,256]{3,2,1,0:T(8,128)(2,1)S(1)}, bf16[2,2,128,256]{3,2,1,0:T(8,128)(2,1)S(1)}, u32[]{:S(2)}, u32[]{:S(2)}) collective-permute-start(bf16[2,2,128,256]{3,2,1,0:T(8,128)(2,1)S(1)} %pad_maximum_fusion.16), channel_id=1, source_target_pairs={{0,2},{64,66},{1,3},{65,67},{2,0},{66,64},{3,1},{67,65},{4,6},{68,... | collective-permute-start | bytes 786440 | tf_op jit(solution)/shard_map/ppermute | solution.py:38
  30.9 2.6 %collective-permute-done.9 = bf16[2,2,128,256]{3,2,1,0:T(8,128)(2,1)S(1)} collective-permute-done((bf16[2,2,128,256]{3,2,1,0:T(8,128)(2,1)S(1)}, bf16[2,2,128,256]{3,2,1,0:T(8,128)(2,1)S(1)}, u32[]{:S(2)}, u32[]{:S(2)}) %collective-permute-start.9) | collective-permute-done | bytes 262176 | tf_op jit(solution)/shard_map/ppermute | solution.py:38
  34.8 1.5 collective-permute-start.12
  39.1 4.4 %shard_map.76 = (bf16[256,8192]{1,0:T(8,128)(2,1)S(1)}, bf16[256,14336]{1,0:T(8,128)(2,1)S(1)}) custom-call(bf16[256,8192]{1,0:T(8,128)(2,1)} %collective-permute-done.10.refs_0_, bf16[256,14336]{1,0:T(8,128)(2,1)} %collective-permute-done.11.refs_1_), custom_call_target="tpu_custom_call" | custom-call | bytes 11534336 | tf_op jit(solution)/shard_map/pallas_call | solution.py:166
  43.5 3.4 %collective-permute-done.14.refs_2_ = bf16[2,2,2,128,256]{4,3,2,1,0:T(8,128)(2,1)S(1)} collective-permute-done((bf16[2,2,2,128,256]{4,3,2,1,0:T(8,128)(2,1)S(1)}, bf16[2,2,2,128,256]{4,3,2,1,0:T(8,128)(2,1)S(1)}, u32[]{:S(2)}, u32[]{:S(2)}) %collective-permute-start.14) | collective-permute-done | bytes 524320 | tf_op jit(solution)/shard_map/ppermute | solution.py:38
  46.9 1.6 collective-permute-done.13.refs_1_
  48.6 1.4 shard_map.78.b_ref
  51.0 2.4 %shard_map.79 = (bf16[256,256]{1,0:T(8,128)(2,1)S(1)}, bf16[256,256]{1,0:T(8,128)(2,1)S(1)}) custom-call(bf16[256,8192]{1,0:T(8,128)(2,1)S(1)} %copy-done, bf16[256,8192]{1,0:T(8,128)(2,1)S(1)} %get-tuple-element.74.a1_ref, bf16[64,128,256]{2,1,0:T(8,128)(2,1)S(1)} %shard_map.78.b_ref), custom_call_target="tpu_custom_call" | custom-call | flops 2147483648 | bytes 12582912 | tf_op jit(solution)/shard_map/pallas_call | solution.py:187
  53.4 5.3 %shard_map.80 = (bf16[2,2,3,224,256]{4,3,2,1,0:T(8,128)(2,1)S(1)}, bf16[2,2,3,224,256]{4,3,2,1,0:T(8,128)(2,1)S(1)}, bf16[2,2,3,224,256]{4,3,2,1,0:T(8,128)(2,1)...) custom-call(s32[4]{0:T(128)S(1)} %pad_add_fusion.pos_ref, ...), custom_call_target="tpu_custom_call" | custom-call | flops 3758096384 | bytes 22020096 | tf_op jit(solution)/shard_map/pallas_call | solution.py:225
  60.6 2.0 %collective-permute-start.18 = (bf16[2,2,3,224,256]{4,3,2,1,0:T(8,128)(2,1)S(1)}, bf16[2,2,3,224,256]{4,3,2,1,0:T(8,128)(2,1)S(1)}, u32[]{:S(2)}, u32[]{:S(2)}) collective-permute-start(bf16[2,2,3,224,256]{4,3,2,1,0:T(8,128)(2,1)S(1)} %get-tuple-element.89), channel_id=1, source_target_pairs={{0,2},{64,66},{1,3},{65,67},{2,0},{66,64},{3,1},{67,65},{4,6},{68,... | collective-permute-start | bytes 4128776 | tf_op jit(solution)/shard_map/ppermute | solution.py:38
  62.6 14.6 %collective-permute-done.15 = bf16[2,2,2,224,256]{4,3,2,1,0:T(8,128)(2,1)S(1)} collective-permute-done((bf16[2,2,2,224,256]{4,3,2,1,0:T(8,128)(2,1)S(1)}, bf16[2,2,2,224,256]{4,3,2,1,0:T(8,128)(2,1)S(1)}, u32[]{:S(2)}, u32[]{:S(2)}) %collective-permute-start.15) | collective-permute-done | bytes 917536 | tf_op jit(solution)/shard_map/ppermute | solution.py:38
  79.8 2.8 %collective-permute-start.19 = (bf16[2,3,224,256]{3,2,1,0:T(8,128)(2,1)S(1)}, bf16[2,3,224,256]{3,2,1,0:T(8,128)(2,1)S(1)}, u32[]{:S(2)}, u32[]{:S(2)}) collective-permute-start(bf16[2,3,224,256]{3,2,1,0:T(8,128)(2,1)S(1)} %get-tuple-element.118), channel_id=1, source_target_pairs={{0,8},{64,72},{1,9},{65,73},{2,10},{66,74},{3,11},{67,75},{4,12},{... | collective-permute-start | bytes 2064392 | tf_op jit(solution)/shard_map/ppermute | solution.py:38
  82.7 3.4 %collective-permute-done.16 = bf16[2,2,224,256]{3,2,1,0:T(8,128)(2,1)S(1)} collective-permute-done((bf16[2,2,224,256]{3,2,1,0:T(8,128)(2,1)S(1)}, bf16[2,2,224,256]{3,2,1,0:T(8,128)(2,1)S(1)}, u32[]{:S(2)}, u32[]{:S(2)}) %collective-permute-start.16) | collective-permute-done | bytes 458784 | tf_op jit(solution)/shard_map/ppermute | solution.py:38
  86.1 2.8 %collective-permute-start.24 = (bf16[2,224,256]{2,1,0:T(8,128)(2,1)S(1)}, bf16[2,224,256]{2,1,0:T(8,128)(2,1)S(1)}, u32[]{:S(2)}, u32[]{:S(2)}) collective-permute-start(bf16[2,224,256]{2,1,0:T(8,128)(2,1)S(1)} %fusion.35), channel_id=1, source_target_pairs={{0,8},{64,72},{1,9},{65,73},{2,10},{66,74},{3,11},{67,75},{4,12},{... | collective-permute-start | bytes 688136 | tf_op jit(solution)/shard_map/ppermute | solution.py:38
  90.0 1.8 collective-permute-start.23
  92.0 1.3 collective-permute-start.20
  93.6 3.9 %collective-permute-done.23 = bf16[3,224,256]{2,1,0:T(8,128)(2,1)S(1)} collective-permute-done((bf16[3,224,256]{2,1,0:T(8,128)(2,1)S(1)}, bf16[3,224,256]{2,1,0:T(8,128)(2,1)S(1)}, u32[]{:S(2)}, u32[]{:S(2)}) %collective-permute-start.23) | collective-permute-done | bytes 344096 | tf_op jit(solution)/shard_map/ppermute | solution.py:38
  97.6 1.8 collective-permute-done.20
  99.9 2.5 %collective-permute-start.25 = (bf16[2,224,256]{2,1,0:T(8,128)(2,1)S(1)}, bf16[2,224,256]{2,1,0:T(8,128)(2,1)S(1)}, u32[]{:S(2)}, u32[]{:S(2)}) collective-permute-start(bf16[2,224,256]{2,1,0:T(8,128)(2,1)S(1)} %get-tuple-element.123), channel_id=1, source_target_pairs={{0,6},{64,70},{1,7},{65,71},{2,4},{66,68},{3,5},{67,69},{4,2},{68,... | collective-permute-start | bytes 688136 | tf_op jit(solution)/shard_map/ppermute | solution.py:38
  102.4 3.2 %collective-permute-done.27 = bf16[2,224,256]{2,1,0:T(8,128)(2,1)S(1)} collective-permute-done((bf16[2,224,256]{2,1,0:T(8,128)(2,1)S(1)}, bf16[2,224,256]{2,1,0:T(8,128)(2,1)S(1)}, u32[]{:S(2)}, u32[]{:S(2)}) %collective-permute-start.27) | collective-permute-done | bytes 229408 | tf_op jit(solution)/shard_map/ppermute | solution.py:38
  105.6 1.5 collective-permute-done.26
  107.4 5.2 %collective-permute-done.28 = bf16[2,224,256]{2,1,0:T(8,128)(2,1)S(1)} collective-permute-done((bf16[2,224,256]{2,1,0:T(8,128)(2,1)S(1)}, bf16[2,224,256]{2,1,0:T(8,128)(2,1)S(1)}, u32[]{:S(2)}, u32[]{:S(2)}) %collective-permute-start.28) | collective-permute-done | bytes 229408 | tf_op jit(solution)/shard_map/ppermute | solution.py:38
  113.0 9.7 %collective-permute-start.32 = (bf16[224,256]{1,0:T(8,128)(2,1)S(1)}, bf16[224,256]{1,0:T(8,128)(2,1)S(1)}, u32[]{:S(2)}, u32[]{:S(2)}) collective-permute-start(bf16[224,256]{1,0:T(8,128)(2,1)S(1)} %slice_bitcast_fusion.12), channel_id=1, source_target_pairs={{0,32},{64,96},{1,33},{65,97},{2,34},{66,98},{3,35},{67,99},{4,36}... | collective-permute-start | bytes 344072 | tf_op jit(solution)/shard_map/ppermute | solution.py:38
  122.7 1.7 collective-permute-start.30
  125.5 3.1 %collective-permute-done.29 = bf16[2,224,256]{2,1,0:T(8,128)(2,1)S(1)} collective-permute-done((bf16[2,224,256]{2,1,0:T(8,128)(2,1)S(1)}, bf16[2,224,256]{2,1,0:T(8,128)(2,1)S(1)}, u32[]{:S(2)}, u32[]{:S(2)}) %collective-permute-start.29) | collective-permute-done | bytes 229408 | tf_op jit(solution)/shard_map/ppermute | solution.py:38
  128.6 1.9 %collective-permute-done.30 = bf16[2,224,256]{2,1,0:T(8,128)(2,1)S(1)} collective-permute-done((bf16[2,224,256]{2,1,0:T(8,128)(2,1)S(1)}, bf16[2,224,256]{2,1,0:T(8,128)(2,1)S(1)}, u32[]{:S(2)}, u32[]{:S(2)}) %collective-permute-start.30) | collective-permute-done | bytes 229408 | tf_op jit(solution)/shard_map/ppermute | solution.py:38
  132.3 2.4 %collective-permute-start.33 = (bf16[3,224,256]{2,1,0:T(8,128)(2,1)S(1)}, bf16[3,224,256]{2,1,0:T(8,128)(2,1)S(1)}, u32[]{:S(2)}, u32[]{:S(2)}) collective-permute-start(bf16[3,224,256]{2,1,0:T(8,128)(2,1)S(1)} %get-tuple-element.98), channel_id=1, source_target_pairs={{0,64},{64,0},{1,65},{65,1},{2,66},{66,2},{3,67},{67,3},{4,68},{68... | collective-permute-start | bytes 1032200 | tf_op jit(solution)/shard_map/ppermute | solution.py:38
  137.1 4.9 %collective-permute-done.35 = bf16[2,224,256]{2,1,0:T(8,128)(2,1)S(1)} collective-permute-done((bf16[2,224,256]{2,1,0:T(8,128)(2,1)S(1)}, bf16[2,224,256]{2,1,0:T(8,128)(2,1)S(1)}, u32[]{:S(2)}, u32[]{:S(2)}) %collective-permute-start.35) | collective-permute-done | bytes 229408 | tf_op jit(solution)/shard_map/ppermute | solution.py:38
  143.8 1.5 collective-permute-start.39
  145.3 7.1 %collective-permute-done.39 = bf16[2,2,224,256]{3,2,1,0:T(8,128)(2,1)S(1)} collective-permute-done((bf16[2,2,224,256]{3,2,1,0:T(8,128)(2,1)S(1)}, bf16[2,2,224,256]{3,2,1,0:T(8,128)(2,1)S(1)}, u32[]{:S(2)}, u32[]{:S(2)}) %collective-permute-start.39) | collective-permute-done | bytes 458784 | tf_op jit(solution)/shard_map/ppermute | solution.py:38
  154.5 1.5 collective-permute-start.40
  156.2 1.7 collective-permute-start.41
  159.3 1.6 collective-permute-start.48
  161.0 10.6 %collective-permute-done.42.refs_2_ = bf16[2,2,2,224,256]{4,3,2,1,0:T(8,128)(2,1)S(1)} collective-permute-done((bf16[2,2,2,224,256]{4,3,2,1,0:T(8,128)(2,1)S(1)}, bf16[2,2,2,224,256]{4,3,2,1,0:T(8,128)(2,1)S(1)}, u32[]{:S(2)}, u32[]{:S(2)}) %collective-permute-start.42) | collective-permute-done | bytes 917536 | tf_op jit(solution)/shard_map/ppermute | solution.py:38
  175.2 1.5 fusion.1
  178.4 1.7 collective-permute-done.45.refs_2_
  180.9 5.6 %shard_map.85 = bf16[256,14336]{1,0:T(8,128)(2,1)} custom-call(s32[1]{0:T(128)} %bitcast.core_ref, bf16[64,224,256]{2,1,0:T(8,128)(2,1)S(1)} %shard_map.82.own_ref, bf16[64,224,256]{2,1,0:T(8,128)(2,1)S(1)} %shard_map.84.other_ref, bf16[2,256,256]{2,1,0:T(8,128)(2,1)S(1)} %pad_maximum_fusion.17.b_ref), custom_call_target="tpu_custom_call" | custom-call | flops 3758096384 | bytes 22020096 | tf_op jit(solution)/shard_map/pallas_call | solution.py:262
  (117 shorter events, 32.7 us)
Async XLA Ops:
  0.6 34.1 %collective-permute-start.11 = (bf16[256,14336]{1,0:T(8,128)(2,1)}, bf16[256,14336]{1,0:T(8,128)(2,1)}, u32[]{:S(2)}, u32[]{:S(2)}) collective-permute-start(bf16[256,14336]{1,0:T(8,128)(2,1)} %g0_ref.1), channel_id=1, source_target_pairs={{0,32},{64,96},{1,33},{65,97},{2,34},{66,98},{3,35},{67,99},{4,36}... | collective-permute-start | bytes 22020104 | tf_op jit(solution)/shard_map/ppermute | solution.py:38
  2.1 32.6 %collective-permute-start.10 = (bf16[256,8192]{1,0:T(8,128)(2,1)}, bf16[256,8192]{1,0:T(8,128)(2,1)}, u32[]{:S(2)}, u32[]{:S(2)}) collective-permute-start(bf16[256,8192]{1,0:T(8,128)(2,1)} %a0_ref.1), channel_id=1, source_target_pairs={{0,32},{64,96},{1,33},{65,97},{2,34},{66,98},{3,35},{67,99},{4,36}... | collective-permute-start | bytes 12582920 | tf_op jit(solution)/shard_map/ppermute | solution.py:38
  6.5 4.8 %collective-permute-start.1 = (bf16[2,128,256]{2,1,0:T(8,128)(2,1)S(1)}, bf16[2,128,256]{2,1,0:T(8,128)(2,1)S(1)}, u32[]{:S(2)}, u32[]{:S(2)}) collective-permute-start(bf16[2,128,256]{2,1,0:T(8,128)(2,1)S(1)} %pad_maximum_fusion.20), channel_id=1, source_target_pairs={{0,30},{64,94},{1,31},{65,95},{2,28},{66,92},{3,29},{67,93},{4,26}... | collective-permute-start | bytes 393224 | tf_op jit(solution)/shard_map/ppermute | solution.py:38
  8.8 4.0 %collective-permute-start.2 = (bf16[2,128,256]{2,1,0:T(8,128)(2,1)S(1)}, bf16[2,128,256]{2,1,0:T(8,128)(2,1)S(1)}, u32[]{:S(2)}, u32[]{:S(2)}) collective-permute-start(bf16[2,128,256]{2,1,0:T(8,128)(2,1)S(1)} %pad_maximum_fusion.20), channel_id=1, source_target_pairs={{0,6},{64,70},{1,7},{65,71},{2,4},{66,68},{3,5},{67,69},{4,2},{68,... | collective-permute-start | bytes 393224 | tf_op jit(solution)/shard_map/ppermute | solution.py:38
  9.0 3.8 %collective-permute-start.3 = (bf16[2,128,256]{2,1,0:T(8,128)(2,1)S(1)}, bf16[2,128,256]{2,1,0:T(8,128)(2,1)S(1)}, u32[]{:S(2)}, u32[]{:S(2)}) collective-permute-start(bf16[2,128,256]{2,1,0:T(8,128)(2,1)S(1)} %pad_maximum_fusion.20), channel_id=1, source_target_pairs={{0,24},{64,88},{1,25},{65,89},{2,26},{66,90},{3,27},{67,91},{4,28}... | collective-permute-start | bytes 393224 | tf_op jit(solution)/shard_map/ppermute | solution.py:38
  12.9 11.2 %collective-permute-start.4 = (bf16[3,128,256]{2,1,0:T(8,128)(2,1)S(1)}, bf16[3,128,256]{2,1,0:T(8,128)(2,1)S(1)}, u32[]{:S(2)}, u32[]{:S(2)}) collective-permute-start(bf16[3,128,256]{2,1,0:T(8,128)(2,1)S(1)} %get-tuple-element.65), channel_id=1, source_target_pairs={{0,64},{64,0},{1,65},{65,1},{2,66},{66,2},{3,67},{67,3},{4,68},{68... | collective-permute-start | bytes 589832 | tf_op jit(solution)/shard_map/ppermute | solution.py:38
  16.6 7.5 %collective-permute-start.5 = (bf16[3,128,256]{2,1,0:T(8,128)(2,1)S(1)}, bf16[3,128,256]{2,1,0:T(8,128)(2,1)S(1)}, u32[]{:S(2)}, u32[]{:S(2)}) collective-permute-start(bf16[3,128,256]{2,1,0:T(8,128)(2,1)S(1)} %get-tuple-element.67), channel_id=1, source_target_pairs={{0,2},{64,66},{1,3},{65,67},{2,0},{66,64},{3,1},{67,65},{4,6},{68,... | collective-permute-start | bytes 589832 | tf_op jit(solution)/shard_map/ppermute | solution.py:38
  19.0 5.0 %collective-permute-start.6 = (bf16[2,128,256]{2,1,0:T(8,128)(2,1)S(1)}, bf16[2,128,256]{2,1,0:T(8,128)(2,1)S(1)}, u32[]{:S(2)}, u32[]{:S(2)}) collective-permute-start(bf16[2,128,256]{2,1,0:T(8,128)(2,1)S(1)} %collective-permute-done.1), channel_id=1, source_target_pairs={{0,8},{64,72},{1,9},{65,73},{2,10},{66,74},{3,11},{67,75},{4,12},{... | collective-permute-start | bytes 393224 | tf_op jit(solution)/shard_map/ppermute | solution.py:38
  24.1 9.4 %collective-permute-start.7 = (bf16[2,3,128,256]{3,2,1,0:T(8,128)(2,1)S(1)}, bf16[2,3,128,256]{3,2,1,0:T(8,128)(2,1)S(1)}, u32[]{:S(2)}, u32[]{:S(2)}) collective-permute-start(bf16[2,3,128,256]{3,2,1,0:T(8,128)(2,1)S(1)} %pad_maximum_fusion.12), channel_id=1, source_target_pairs={{0,8},{64,72},{1,9},{65,73},{2,10},{66,74},{3,11},{67,75},{4,12},{... | collective-permute-start | bytes 1179656 | tf_op jit(solution)/shard_map/ppermute | solution.py:38
  26.8 7.9 %collective-permute-start.8 = (bf16[2,3,128,256]{3,2,1,0:T(8,128)(2,1)S(1)}, bf16[2,3,128,256]{3,2,1,0:T(8,128)(2,1)S(1)}, u32[]{:S(2)}, u32[]{:S(2)}) collective-permute-start(bf16[2,3,128,256]{3,2,1,0:T(8,128)(2,1)S(1)} %pad_maximum_fusion.13), channel_id=1, source_target_pairs={{0,64},{64,0},{1,65},{65,1},{2,66},{66,2},{3,67},{67,3},{4,68},{68... | collective-permute-start | bytes 1179656 | tf_op jit(solution)/shard_map/ppermute | solution.py:38
  27.0 6.5 %collective-permute-start.9 = (bf16[2,2,128,256]{3,2,1,0:T(8,128)(2,1)S(1)}, bf16[2,2,128,256]{3,2,1,0:T(8,128)(2,1)S(1)}, u32[]{:S(2)}, u32[]{:S(2)}) collective-permute-start(bf16[2,2,128,256]{3,2,1,0:T(8,128)(2,1)S(1)} %pad_maximum_fusion.16), channel_id=1, source_target_pairs={{0,2},{64,66},{1,3},{65,67},{2,0},{66,64},{3,1},{67,65},{4,6},{68,... | collective-permute-start | bytes 786440 | tf_op jit(solution)/shard_map/ppermute | solution.py:38
  34.8 12.1 %collective-permute-start.12 = (bf16[2,2,3,128,256]{4,3,2,1,0:T(8,128)(2,1)S(1)}, bf16[2,2,3,128,256]{4,3,2,1,0:T(8,128)(2,1)S(1)}, u32[]{:S(2)}, u32[]{:S(2)}) collective-permute-start(bf16[2,2,3,128,256]{4,3,2,1,0:T(8,128)(2,1)S(1)} %pad_maximum_fusion.4.refs_0_), channel_id=1, source_target_pairs={{0,2},{64,66},{1,3},{65,67},{2,0},{66,64},{3,1},{67,65},{4,6},{68,... | collective-permute-start | bytes 2359304 | tf_op jit(solution)/shard_map/ppermute | solution.py:38
  36.4 12.2 %collective-permute-start.13 = (bf16[2,2,3,128,256]{4,3,2,1,0:T(8,128)(2,1)S(1)}, bf16[2,2,3,128,256]{4,3,2,1,0:T(8,128)(2,1)}, u32[]{:S(2)}, u32[]{:S(2)}) collective-permute-start(bf16[2,2,3,128,256]{4,3,2,1,0:T(8,128)(2,1)S(1)} %pad_maximum_fusion.5.refs_1_), channel_id=1, source_target_pairs={{0,8},{64,72},{1,9},{65,73},{2,10},{66,74},{3,11},{67,75},{4,12},{... | collective-permute-start | bytes 2359304 | tf_op jit(solution)/shard_map/ppermute | solution.py:38
  37.6 9.3 %collective-permute-start.14 = (bf16[2,2,2,128,256]{4,3,2,1,0:T(8,128)(2,1)S(1)}, bf16[2,2,2,128,256]{4,3,2,1,0:T(8,128)(2,1)S(1)}, u32[]{:S(2)}, u32[]{:S(2)}) collective-permute-start(bf16[2,2,2,128,256]{4,3,2,1,0:T(8,128)(2,1)S(1)} %pad_maximum_fusion.8.refs_2_), channel_id=1, source_target_pairs={{0,64},{64,0},{1,65},{65,1},{2,66},{66,2},{3,67},{67,3},{4,68},{68... | collective-permute-start | bytes 1572872 | tf_op jit(solution)/shard_map/ppermute | solution.py:38
  58.8 19.6 %collective-permute-start.21 = (bf16[2,2,3,224,256]{4,3,2,1,0:T(8,128)(2,1)S(1)}, bf16[2,2,3,224,256]{4,3,2,1,0:T(8,128)(2,1)S(1)}, u32[]{:S(2)}, u32[]{:S(2)}) collective-permute-start(bf16[2,2,3,224,256]{4,3,2,1,0:T(8,128)(2,1)S(1)} %get-tuple-element.91), channel_id=1, source_target_pairs={{0,8},{64,72},{1,9},{65,73},{2,10},{66,74},{3,11},{67,75},{4,12},{... | collective-permute-start | bytes 4128776 | tf_op jit(solution)/shard_map/ppermute | solution.py:38
  59.9 17.2 %collective-permute-start.15 = (bf16[2,2,2,224,256]{4,3,2,1,0:T(8,128)(2,1)S(1)}, bf16[2,2,2,224,256]{4,3,2,1,0:T(8,128)(2,1)S(1)}, u32[]{:S(2)}, u32[]{:S(2)}) collective-permute-start(bf16[2,2,2,224,256]{4,3,2,1,0:T(8,128)(2,1)S(1)} %get-tuple-element.86), channel_id=1, source_target_pairs={{0,64},{64,0},{1,65},{65,1},{2,66},{66,2},{3,67},{67,3},{4,68},{68... | collective-permute-start | bytes 2752520 | tf_op jit(solution)/shard_map/ppermute | solution.py:38
  60.6 18.8 %collective-permute-start.18 = (bf16[2,2,3,224,256]{4,3,2,1,0:T(8,128)(2,1)S(1)}, bf16[2,2,3,224,256]{4,3,2,1,0:T(8,128)(2,1)S(1)}, u32[]{:S(2)}, u32[]{:S(2)}) collective-permute-start(bf16[2,2,3,224,256]{4,3,2,1,0:T(8,128)(2,1)S(1)} %get-tuple-element.89), channel_id=1, source_target_pairs={{0,2},{64,66},{1,3},{65,67},{2,0},{66,64},{3,1},{67,65},{4,6},{68,... | collective-permute-start | bytes 4128776 | tf_op jit(solution)/shard_map/ppermute | solution.py:38
  62.6 20.1 %collective-permute-start.17 = (f32[2,224,256]{2,1,0:T(8,128)S(1)}, f32[2,224,256]{2,1,0:T(8,128)S(1)}, u32[]{:S(2)}, u32[]{:S(2)}) collective-permute-start(f32[2,224,256]{2,1,0:T(8,128)S(1)} %copy-done.1), channel_id=1, source_target_pairs={{0,65},{64,1},{1,64},{65,0},{2,67},{66,3},{3,66},{67,2},{4,69},{68... | collective-permute-start | bytes 1376264 | tf_op jit(solution)/shard_map/ppermute | solution.py:38
  77.4 8.6 %collective-permute-start.16 = (bf16[2,2,224,256]{3,2,1,0:T(8,128)(2,1)S(1)}, bf16[2,2,224,256]{3,2,1,0:T(8,128)(2,1)S(1)}, u32[]{:S(2)}, u32[]{:S(2)}) collective-permute-start(bf16[2,2,224,256]{3,2,1,0:T(8,128)(2,1)S(1)} %get-tuple-element.122), channel_id=1, source_target_pairs={{0,2},{64,66},{1,3},{65,67},{2,0},{66,64},{3,1},{67,65},{4,6},{68,... | collective-permute-start | bytes 1376264 | tf_op jit(solution)/shard_map/ppermute | solution.py:38
  78.9 11.1 %collective-permute-start.22 = (bf16[2,3,224,256]{3,2,1,0:T(8,128)(2,1)S(1)}, bf16[2,3,224,256]{3,2,1,0:T(8,128)(2,1)S(1)}, u32[]{:S(2)}, u32[]{:S(2)}) collective-permute-start(bf16[2,3,224,256]{3,2,1,0:T(8,128)(2,1)S(1)} %get-tuple-element.120), channel_id=1, source_target_pairs={{0,64},{64,0},{1,65},{65,1},{2,66},{66,2},{3,67},{67,3},{4,68},{68... | collective-permute-start | bytes 2064392 | tf_op jit(solution)/shard_map/ppermute | solution.py:38
  79.8 12.0 %collective-permute-start.19 = (bf16[2,3,224,256]{3,2,1,0:T(8,128)(2,1)S(1)}, bf16[2,3,224,256]{3,2,1,0:T(8,128)(2,1)S(1)}, u32[]{:S(2)}, u32[]{:S(2)}) collective-permute-start(bf16[2,3,224,256]{3,2,1,0:T(8,128)(2,1)S(1)} %get-tuple-element.118), channel_id=1, source_target_pairs={{0,8},{64,72},{1,9},{65,73},{2,10},{66,74},{3,11},{67,75},{4,12},{... | collective-permute-start | bytes 2064392 | tf_op jit(solution)/shard_map/ppermute | solution.py:38
  86.1 7.4 %collective-permute-start.24 = (bf16[2,224,256]{2,1,0:T(8,128)(2,1)S(1)}, bf16[2,224,256]{2,1,0:T(8,128)(2,1)S(1)}, u32[]{:S(2)}, u32[]{:S(2)}) collective-permute-start(bf16[2,224,256]{2,1,0:T(8,128)(2,1)S(1)} %fusion.35), channel_id=1, source_target_pairs={{0,8},{64,72},{1,9},{65,73},{2,10},{66,74},{3,11},{67,75},{4,12},{... | collective-permute-start | bytes 688136 | tf_op jit(solution)/shard_map/ppermute | solution.py:38
  90.0 7.4 %collective-permute-start.23 = (bf16[3,224,256]{2,1,0:T(8,128)(2,1)S(1)}, bf16[3,224,256]{2,1,0:T(8,128)(2,1)S(1)}, u32[]{:S(2)}, u32[]{:S(2)}) collective-permute-start(bf16[3,224,256]{2,1,0:T(8,128)(2,1)S(1)} %fusion.33), channel_id=1, source_target_pairs={{0,2},{64,66},{1,3},{65,67},{2,0},{66,64},{3,1},{67,65},{4,6},{68,... | collective-permute-start | bytes 1032200 | tf_op jit(solution)/shard_map/ppermute | solution.py:38
  92.0 7.4 %collective-permute-start.20 = (bf16[3,224,256]{2,1,0:T(8,128)(2,1)S(1)}, bf16[3,224,256]{2,1,0:T(8,128)(2,1)S(1)}, u32[]{:S(2)}, u32[]{:S(2)}) collective-permute-start(bf16[3,224,256]{2,1,0:T(8,128)(2,1)S(1)} %fusion.31), channel_id=1, source_target_pairs={{0,64},{64,0},{1,65},{65,1},{2,66},{66,2},{3,67},{67,3},{4,68},{68... | collective-permute-start | bytes 1032200 | tf_op jit(solution)/shard_map/ppermute | solution.py:38
  99.7 6.0 %collective-permute-start.27 = (bf16[2,224,256]{2,1,0:T(8,128)(2,1)S(1)}, bf16[2,224,256]{2,1,0:T(8,128)(2,1)S(1)}, u32[]{:S(2)}, u32[]{:S(2)}) collective-permute-start(bf16[2,224,256]{2,1,0:T(8,128)(2,1)S(1)} %get-tuple-element.124), channel_id=1, source_target_pairs={{0,30},{64,94},{1,31},{65,95},{2,28},{66,92},{3,29},{67,93},{4,26}... | collective-permute-start | bytes 688136 | tf_op jit(solution)/shard_map/ppermute | solution.py:38
  99.8 7.4 %collective-permute-start.26 = (bf16[2,224,256]{2,1,0:T(8,128)(2,1)S(1)}, bf16[2,224,256]{2,1,0:T(8,128)(2,1)S(1)}, u32[]{:S(2)}, u32[]{:S(2)}) collective-permute-start(bf16[2,224,256]{2,1,0:T(8,128)(2,1)S(1)} %get-tuple-element.125), channel_id=1, source_target_pairs={{0,24},{64,88},{1,25},{65,89},{2,26},{66,90},{3,27},{67,91},{4,28}... | collective-permute-start | bytes 688136 | tf_op jit(solution)/shard_map/ppermute | solution.py:38
  99.9 7.3 %collective-permute-start.25 = (bf16[2,224,256]{2,1,0:T(8,128)(2,1)S(1)}, bf16[2,224,256]{2,1,0:T(8,128)(2,1)S(1)}, u32[]{:S(2)}, u32[]{:S(2)}) collective-permute-start(bf16[2,224,256]{2,1,0:T(8,128)(2,1)S(1)} %get-tuple-element.123), channel_id=1, source_target_pairs={{0,6},{64,70},{1,7},{65,71},{2,4},{66,68},{3,5},{67,69},{4,2},{68,... | collective-permute-start | bytes 688136 | tf_op jit(solution)/shard_map/ppermute | solution.py:38
  107.3 5.2 %collective-permute-start.28 = (bf16[2,224,256]{2,1,0:T(8,128)(2,1)S(1)}, bf16[2,224,256]{2,1,0:T(8,128)(2,1)S(1)}, u32[]{:S(2)}, u32[]{:S(2)}) collective-permute-start(bf16[2,224,256]{2,1,0:T(8,128)(2,1)S(1)} %fusion.25), channel_id=1, source_target_pairs={{0,65},{64,1},{1,64},{65,0},{2,67},{66,3},{3,66},{67,2},{4,69},{68... | collective-permute-start | bytes 688136 | tf_op jit(solution)/shard_map/ppermute | solution.py:38
  113.0 12.4 %collective-permute-start.32 = (bf16[224,256]{1,0:T(8,128)(2,1)S(1)}, bf16[224,256]{1,0:T(8,128)(2,1)S(1)}, u32[]{:S(2)}, u32[]{:S(2)}) collective-permute-start(bf16[224,256]{1,0:T(8,128)(2,1)S(1)} %slice_bitcast_fusion.12), channel_id=1, source_target_pairs={{0,32},{64,96},{1,33},{65,97},{2,34},{66,98},{3,35},{67,99},{4,36}... | collective-permute-start | bytes 344072 | tf_op jit(solution)/shard_map/ppermute | solution.py:38
  122.7 5.9 %collective-permute-start.29 = (bf16[2,224,256]{2,1,0:T(8,128)(2,1)S(1)}, bf16[2,224,256]{2,1,0:T(8,128)(2,1)S(1)}, u32[]{:S(2)}, u32[]{:S(2)}) collective-permute-start(bf16[2,224,256]{2,1,0:T(8,128)(2,1)S(1)} %get-tuple-element.93), channel_id=1, source_target_pairs={{0,30},{64,94},{1,31},{65,95},{2,28},{66,92},{3,29},{67,93},{4,26}... | collective-permute-start | bytes 688136 | tf_op jit(solution)/shard_map/ppermute | solution.py:38
  122.7 7.8 %collective-permute-start.30 = (bf16[2,224,256]{2,1,0:T(8,128)(2,1)S(1)}, bf16[2,224,256]{2,1,0:T(8,128)(2,1)S(1)}, u32[]{:S(2)}, u32[]{:S(2)}) collective-permute-start(bf16[2,224,256]{2,1,0:T(8,128)(2,1)S(1)} %get-tuple-element.93), channel_id=1, source_target_pairs={{0,6},{64,70},{1,7},{65,71},{2,4},{66,68},{3,5},{67,69},{4,2},{68,... | collective-permute-start | bytes 688136 | tf_op jit(solution)/shard_map/ppermute | solution.py:38
  124.4 6.9 %collective-permute-start.31 = (bf16[2,224,256]{2,1,0:T(8,128)(2,1)S(1)}, bf16[2,224,256]{2,1,0:T(8,128)(2,1)S(1)}, u32[]{:S(2)}, u32[]{:S(2)}) collective-permute-start(bf16[2,224,256]{2,1,0:T(8,128)(2,1)S(1)} %get-tuple-element.93), channel_id=1, source_target_pairs={{0,24},{64,88},{1,25},{65,89},{2,26},{66,90},{3,27},{67,91},{4,28}... | collective-permute-start | bytes 688136 | tf_op jit(solution)/shard_map/ppermute | solution.py:38
  131.2 5.7 %collective-permute-start.36 = (bf16[224,512]{1,0:T(8,128)(2,1)S(1)}, bf16[224,512]{1,0:T(8,128)(2,1)S(1)}, u32[]{:S(2)}, u32[]{:S(2)}) collective-permute-start(bf16[224,512]{1,0:T(8,128)(2,1)S(1)} %maximum_select_fusion.1), channel_id=1, source_target_pairs={{0,64},{64,0},{1,65},{65,1},{2,66},{66,2},{3,67},{67,3},{4,68},{68... | collective-permute-start | bytes 688136 | tf_op jit(solution)/shard_map/ppermute | solution.py:38
  132.3 9.7 %collective-permute-start.33 = (bf16[3,224,256]{2,1,0:T(8,128)(2,1)S(1)}, bf16[3,224,256]{2,1,0:T(8,128)(2,1)S(1)}, u32[]{:S(2)}, u32[]{:S(2)}) collective-permute-start(bf16[3,224,256]{2,1,0:T(8,128)(2,1)S(1)} %get-tuple-element.98), channel_id=1, source_target_pairs={{0,64},{64,0},{1,65},{65,1},{2,66},{66,2},{3,67},{67,3},{4,68},{68... | collective-permute-start | bytes 1032200 | tf_op jit(solution)/shard_map/ppermute | solution.py:38
  134.8 7.3 %collective-permute-start.34 = (bf16[3,224,256]{2,1,0:T(8,128)(2,1)S(1)}, bf16[3,224,256]{2,1,0:T(8,128)(2,1)S(1)}, u32[]{:S(2)}, u32[]{:S(2)}) collective-permute-start(bf16[3,224,256]{2,1,0:T(8,128)(2,1)S(1)} %get-tuple-element.100), channel_id=1, source_target_pairs={{0,2},{64,66},{1,3},{65,67},{2,0},{66,64},{3,1},{67,65},{4,6},{68,... | collective-permute-start | bytes 1032200 | tf_op jit(solution)/shard_map/ppermute | solution.py:38
  135.9 6.1 %collective-permute-start.35 = (bf16[2,224,256]{2,1,0:T(8,128)(2,1)S(1)}, bf16[2,224,256]{2,1,0:T(8,128)(2,1)S(1)}, u32[]{:S(2)}, u32[]{:S(2)}) collective-permute-start(bf16[2,224,256]{2,1,0:T(8,128)(2,1)S(1)} %collective-permute-done.29), channel_id=1, source_target_pairs={{0,8},{64,72},{1,9},{65,73},{2,10},{66,74},{3,11},{67,75},{4,12},{... | collective-permute-start | bytes 688136 | tf_op jit(solution)/shard_map/ppermute | solution.py:38
  142.1 11.1 %collective-permute-start.37 = (bf16[2,3,224,256]{3,2,1,0:T(8,128)(2,1)S(1)}, bf16[2,3,224,256]{3,2,1,0:T(8,128)(2,1)S(1)}, u32[]{:S(2)}, u32[]{:S(2)}) collective-permute-start(bf16[2,3,224,256]{3,2,1,0:T(8,128)(2,1)S(1)} %pad_maximum_fusion.6), channel_id=1, source_target_pairs={{0,8},{64,72},{1,9},{65,73},{2,10},{66,74},{3,11},{67,75},{4,12},{... | collective-permute-start | bytes 2064392 | tf_op jit(solution)/shard_map/ppermute | solution.py:38
  143.3 11.1 %collective-permute-start.38 = (bf16[2,3,224,256]{3,2,1,0:T(8,128)(2,1)S(1)}, bf16[2,3,224,256]{3,2,1,0:T(8,128)(2,1)S(1)}, u32[]{:S(2)}, u32[]{:S(2)}) collective-permute-start(bf16[2,3,224,256]{3,2,1,0:T(8,128)(2,1)S(1)} %pad_maximum_fusion.7), channel_id=1, source_target_pairs={{0,64},{64,0},{1,65},{65,1},{2,66},{66,2},{3,67},{67,3},{4,68},{68... | collective-permute-start | bytes 2064392 | tf_op jit(solution)/shard_map/ppermute | solution.py:38
  143.8 8.6 %collective-permute-start.39 = (bf16[2,2,224,256]{3,2,1,0:T(8,128)(2,1)S(1)}, bf16[2,2,224,256]{3,2,1,0:T(8,128)(2,1)S(1)}, u32[]{:S(2)}, u32[]{:S(2)}) collective-permute-start(bf16[2,2,224,256]{3,2,1,0:T(8,128)(2,1)S(1)} %pad_maximum_fusion.11), channel_id=1, source_target_pairs={{0,2},{64,66},{1,3},{65,67},{2,0},{66,64},{3,1},{67,65},{4,6},{68,... | collective-permute-start | bytes 1376264 | tf_op jit(solution)/shard_map/ppermute | solution.py:38
  154.5 18.5 %collective-permute-start.40 = (bf16[2,2,3,224,256]{4,3,2,1,0:T(8,128)(2,1)S(1)}, bf16[2,2,3,224,256]{4,3,2,1,0:T(8,128)(2,1)S(1)}, u32[]{:S(2)}, u32[]{:S(2)}) collective-permute-start(bf16[2,2,3,224,256]{4,3,2,1,0:T(8,128)(2,1)S(1)} %pad_maximum_fusion.refs_0_), channel_id=1, source_target_pairs={{0,2},{64,66},{1,3},{65,67},{2,0},{66,64},{3,1},{67,65},{4,6},{68,... | collective-permute-start | bytes 4128776 | tf_op jit(solution)/shard_map/ppermute | solution.py:38
  156.2 18.5 %collective-permute-start.41 = (bf16[2,2,3,224,256]{4,3,2,1,0:T(8,128)(2,1)S(1)}, bf16[2,2,3,224,256]{4,3,2,1,0:T(8,128)(2,1)S(1)}, u32[]{:S(2)}, u32[]{:S(2)}) collective-permute-start(bf16[2,2,3,224,256]{4,3,2,1,0:T(8,128)(2,1)S(1)} %pad_maximum_fusion.1.refs_1_), channel_id=1, source_target_pairs={{0,8},{64,72},{1,9},{65,73},{2,10},{66,74},{3,11},{67,75},{4,12},{... | collective-permute-start | bytes 4128776 | tf_op jit(solution)/shard_map/ppermute | solution.py:38
  158.0 13.5 %collective-permute-start.42 = (bf16[2,2,2,224,256]{4,3,2,1,0:T(8,128)(2,1)S(1)}, bf16[2,2,2,224,256]{4,3,2,1,0:T(8,128)(2,1)S(1)}, u32[]{:S(2)}, u32[]{:S(2)}) collective-permute-start(bf16[2,2,2,224,256]{4,3,2,1,0:T(8,128)(2,1)S(1)} %pad_maximum_fusion.3.refs_2_), channel_id=1, source_target_pairs={{0,64},{64,0},{1,65},{65,1},{2,66},{66,2},{3,67},{67,3},{4,68},{68... | collective-permute-start | bytes 2752520 | tf_op jit(solution)/shard_map/ppermute | solution.py:38
  159.3 15.5 %collective-permute-start.48 = (bf16[2,2,2,224,256]{4,3,2,1,0:T(8,128)(2,1)S(1)}, bf16[2,2,2,224,256]{4,3,2,1,0:T(8,128)(2,1)S(1)}, u32[]{:S(2)}, u32[]{:S(2)}) collective-permute-start(bf16[2,2,2,224,256]{4,3,2,1,0:T(8,128)(2,1)S(1)} %pad_maximum_fusion.3.refs_2_), channel_id=1, source_target_pairs={{0,32},{64,96},{1,33},{65,97},{2,34},{66,98},{3,35},{67,99},{4,36}... | collective-permute-start | bytes 2752520 | tf_op jit(solution)/shard_map/ppermute | solution.py:38
  160.9 16.7 %collective-permute-start.46 = (bf16[2,2,3,224,256]{4,3,2,1,0:T(8,128)(2,1)S(1)}, bf16[2,2,3,224,256]{4,3,2,1,0:T(8,128)(2,1)S(1)}, u32[]{:S(2)}, u32[]{:S(2)}) collective-permute-start(bf16[2,2,3,224,256]{4,3,2,1,0:T(8,128)(2,1)S(1)} %pad_maximum_fusion.refs_0_), channel_id=1, source_target_pairs={{0,32},{64,96},{1,33},{65,97},{2,34},{66,98},{3,35},{67,99},{4,36}... | collective-permute-start | bytes 4128776 | tf_op jit(solution)/shard_map/ppermute | solution.py:38
  171.6 6.0 %collective-permute-start.47 = (bf16[2,2,3,224,256]{4,3,2,1,0:T(8,128)(2,1)S(1)}, bf16[2,2,3,224,256]{4,3,2,1,0:T(8,128)(2,1)S(1)}, u32[]{:S(2)}, u32[]{:S(2)}) collective-permute-start(bf16[2,2,3,224,256]{4,3,2,1,0:T(8,128)(2,1)S(1)} %pad_maximum_fusion.1.refs_1_), channel_id=1, source_target_pairs={{0,32},{64,96},{1,33},{65,97},{2,34},{66,98},{3,35},{67,99},{4,36}... | collective-permute-start | bytes 4128776 | tf_op jit(solution)/shard_map/ppermute | solution.py:38
  173.0 7.2 %collective-permute-start.43 = (bf16[2,2,3,224,256]{4,3,2,1,0:T(8,128)(2,1)S(1)}, bf16[2,2,3,224,256]{4,3,2,1,0:T(8,128)(2,1)S(1)}, u32[]{:S(2)}, u32[]{:S(2)}) collective-permute-start(bf16[2,2,3,224,256]{4,3,2,1,0:T(8,128)(2,1)S(1)} %collective-permute-done.40.refs_0_), channel_id=1, source_target_pairs={{0,32},{64,96},{1,33},{65,97},{2,34},{66,98},{3,35},{67,99},{4,36}... | collective-permute-start | bytes 4128776 | tf_op jit(solution)/shard_map/ppermute | solution.py:38
  174.6 5.5 %collective-permute-start.44 = (bf16[2,2,3,224,256]{4,3,2,1,0:T(8,128)(2,1)S(1)}, bf16[2,2,3,224,256]{4,3,2,1,0:T(8,128)(2,1)S(1)}, u32[]{:S(2)}, u32[]{:S(2)}) collective-permute-start(bf16[2,2,3,224,256]{4,3,2,1,0:T(8,128)(2,1)S(1)} %collective-permute-done.41.refs_1_), channel_id=1, source_target_pairs={{0,32},{64,96},{1,33},{65,97},{2,34},{66,98},{3,35},{67,99},{4,36}... | collective-permute-start | bytes 4128776 | tf_op jit(solution)/shard_map/ppermute | solution.py:38
  174.8 5.3 %collective-permute-start.45 = (bf16[2,2,2,224,256]{4,3,2,1,0:T(8,128)(2,1)S(1)}, bf16[2,2,2,224,256]{4,3,2,1,0:T(8,128)(2,1)S(1)}, u32[]{:S(2)}, u32[]{:S(2)}) collective-permute-start(bf16[2,2,2,224,256]{4,3,2,1,0:T(8,128)(2,1)S(1)} %collective-permute-done.42.refs_2_), channel_id=1, source_target_pairs={{0,32},{64,96},{1,33},{65,97},{2,34},{66,98},{3,35},{67,99},{4,36}... | collective-permute-start | bytes 2752520 | tf_op jit(solution)/shard_map/ppermute | solution.py:38
  (10 other events, 75.9 us)
